TPU v7x, 32 devices: a whole 2x2x4 slice. The times are simulated.
32 devices in a mesh: dp: 4 (over y, core), blk: 4 (over z), head: 2 (over x).
Axes of the slice: x: 2, y: 2, z: 4, core: 2. Of those that a mesh axis runs over, the one named last changes fastest.
Arguments:
- inputs: bfloat16 [2048, 4, 2048], P('blk', 'dp', 'head'), may hold values from -32 to 32
- cotangent: bfloat16 [2048, 4, 2048], P('blk', 'dp', 'head'), may hold values from -6 to 6
- lengths: int32 [4, 8], P('dp'), may hold values from 0 to 2048, as said below
- attn_gain: bfloat16 [2048], replicated, may hold values from 0.5 to 1.5
- w_query: bfloat16 [2048, 2048], P(None, 'head'), may hold values from -0.125 to 0.125
- w_key: bfloat16 [2048, 256], P(None, 'head'), may hold values from -0.125 to 0.125
- w_value: bfloat16 [2048, 256], P(None, 'head'), may hold values from -0.125 to 0.125
- w_out: bfloat16 [2048, 2048], P(None, 'head'), may hold values from -1 to 1
- mlp_gain: bfloat16 [2048], replicated, may hold values from 0.5 to 1.5
- gate_weight: bfloat16 [2048, 5632], P(None, 'head'), may hold values from -0.125 to 0.125
- up_weight: bfloat16 [2048, 5632], P(None, 'head'), may hold values from -0.125 to 0.125
- down_weight: bfloat16 [2048, 5632], P(None, 'head'), may hold values from -0.15625 to 0.15625
Outputs:
- output: bfloat16 [2048, 4, 2048], P('blk', 'dp', 'head')
- grad_input: float32 [2048, 4, 2048], P('blk', 'dp', 'head')
- grad_attn_gain: float32 [2048], P(('dp', 'blk'))
- grad_w_query: float32 [2048, 2048], P(('dp', 'blk'), 'head')
- grad_w_key: float32 [2048, 256], P(('dp', 'blk'), 'head')
- grad_w_value: float32 [2048, 256], P(('dp', 'blk'), 'head')
- grad_w_out: float32 [2048, 2048], P(('dp', 'blk'), 'head')
- grad_mlp_gain: float32 [2048], P(('dp', 'blk'))
- grad_w_gate: float32 [2048, 5632], P(('dp', 'blk'), 'head')
- grad_w_up: float32 [2048, 5632], P(('dp', 'blk'), 'head')
- grad_w_down: float32 [2048, 5632], P(('dp', 'blk'), 'head')
- stats: float32 [3], replicated
Inputs may be any that keep to these rules, and one draw needn't show every extreme that they name: Each row's 8 lengths are documents laid end to end from position 0; they sum to at most 2048, and the positions past the sum are padding. Among the rows of each index of dp, one holds a single document that starts at position 0 and ends within the last 512 positions; its other lengths are 0. In the rows of the first index of dp that document fills the whole row.
All inputs are finite; a program needn't handle non-finite values.
Results may differ from a plain program's by a relative error of at most 0.02.
Values may be sent and summed in bfloat16 or wider, within the bound.
A program may use at most 320 MiB of HBM per device.

v0:
```python
import jax
import jax.numpy as jnp
from jax import lax
from jax.sharding import PartitionSpec as P

HD = 64
DOCS = 8


EPS = 1e-05
THETA = 10000.0
NEG_FILL = -1e30


def rope_tables(positions):
    idx_freq = jnp.arange(HD // 2, dtype=jnp.float32)
    inv_freq = jnp.power(THETA, -2.0 * idx_freq / HD)
    angles = positions.astype(jnp.float32)[:, None] * inv_freq[None, :]
    return (jnp.cos(angles), jnp.sin(angles))


def rotate(tensor, cos_tab, sin_tab):
    first_h = tensor[..., : HD // 2]
    second_h = tensor[..., HD // 2 :]
    cos_b = cos_tab[:, None, None, :]
    sin_b = sin_tab[:, None, None, :]
    return jnp.concatenate(
        [first_h * cos_b - second_h * sin_b, second_h * cos_b + first_h * sin_b], axis=-1
    )


def unrotate(tensor, cos_tab, sin_tab):
    first_h = tensor[..., : HD // 2]
    second_h = tensor[..., HD // 2 :]
    cos_b = cos_tab[:, None, None, :]
    sin_b = sin_tab[:, None, None, :]
    return jnp.concatenate(
        [first_h * cos_b + second_h * sin_b, second_h * cos_b - first_h * sin_b], axis=-1
    )


def segment_ids(doc_ends, positions):
    return jnp.sum((doc_ends[None, :, :] <= positions[:, None, None]).astype(jnp.int32), axis=2)


def body(
    inputs,
    cotangent,
    lengths,
    attn_gain,
    w_query,
    w_key,
    w_value,
    w_out,
    mlp_gain,
    gate_weight,
    up_weight,
    down_weight,
):
    block_len, row_count, half_width = inputs.shape
    cycle_size = lax.axis_size("blk")
    seq_total = block_len * cycle_size
    full_width = half_width * lax.axis_size("head")
    first_pos = lax.axis_index("blk") * block_len
    head_slot = lax.axis_index("head")
    kv_width = w_key.shape[1]
    kv_local = kv_width // HD
    heads_local = w_query.shape[1] // HD
    group = heads_local // kv_local
    scale = HD ** (-0.5)
    single_float = jnp.float32
    bf16 = jnp.bfloat16
    doc_ends = jnp.cumsum(lengths, axis=1)
    query_pos = first_pos + jnp.arange(block_len, dtype=jnp.int32)
    query_seg = segment_ids(doc_ends, query_pos)
    cos_tab, sin_tab = rope_tables(query_pos)
    full_in, full_output_gradient = (
        lax.all_gather(inputs, "head", axis=2, tiled=True),
        lax.all_gather(cotangent, "head", axis=2, tiled=True),
    )
    in_f32 = full_in.astype(single_float)
    inv_one = lax.rsqrt(jnp.mean(in_f32 * in_f32, axis=-1, keepdims=True) + EPS)
    norm_one = in_f32 * inv_one
    gain_one = attn_gain.astype(single_float)
    a_one = (norm_one * gain_one).astype(bf16)
    q_lin = jnp.einsum("trd,de->tre", a_one, w_query, preferred_element_type=single_float)
    k_lin = jnp.einsum("trd,de->tre", a_one, w_key, preferred_element_type=single_float)
    v_lin = jnp.einsum("trd,de->tre", a_one, w_value, preferred_element_type=single_float)
    queries = rotate(q_lin.reshape(block_len, row_count, heads_local, HD), cos_tab, sin_tab).astype(
        bf16
    )
    queries = queries.reshape(block_len, row_count, kv_local, group, HD)
    keys = rotate(k_lin.reshape(block_len, row_count, kv_local, HD), cos_tab, sin_tab).astype(bf16)
    keys = keys.reshape(block_len, row_count, kv_width)
    values = v_lin.astype(bf16)

    def block_scores(key_blk, key_pos):
        key_four = key_blk.reshape(block_len, row_count, kv_local, HD)
        raw_score = jnp.einsum(
            "qrkgd,srkd->qrkgs", queries, key_four, preferred_element_type=single_float
        )
        key_seg = segment_ids(doc_ends, key_pos)
        same_doc = query_seg[:, :, None] == jnp.transpose(key_seg)[None, :, :]
        causal = key_pos[None, None, :] <= query_pos[:, None, None]
        return (raw_score * scale, (same_doc & causal)[:, :, None, None, :])

    stat_shape = (block_len, row_count, kv_local, group)
    start_fwd = (
        jnp.full(stat_shape, NEG_FILL, single_float),
        jnp.zeros(stat_shape, single_float),
        jnp.zeros(stat_shape + (HD,), single_float),
    )
    keys_in = lax.all_gather(keys, "blk", axis=0, tiled=True)
    values_in = lax.all_gather(values, "blk", axis=0, tiled=True)
    block_count = keys_in.shape[0] // block_len

    def visit(step_index, carry_state):
        running_max, denom_sum, accum_out = carry_state
        offset = step_index * block_len
        key_blk = lax.dynamic_slice_in_dim(keys_in, offset, block_len, 0)
        value_blk = lax.dynamic_slice_in_dim(values_in, offset, block_len, 0)
        key_pos = offset + jnp.arange(block_len, dtype=jnp.int32)
        scores, key_mask = block_scores(key_blk, key_pos)
        scores = jnp.where(key_mask, scores, NEG_FILL)
        new_max = jnp.maximum(running_max, jnp.max(scores, axis=-1))
        prob_w = jnp.where(key_mask, jnp.exp(scores - new_max[..., None]), 0.0)
        factor = jnp.exp(running_max - new_max)
        denom_sum = denom_sum * factor + jnp.sum(prob_w, axis=-1)
        value_four = value_blk.reshape(block_len, row_count, kv_local, HD)
        accum_out = accum_out * factor[..., None] + jnp.einsum(
            "qrkgs,srkd->qrkgd",
            prob_w.astype(bf16),
            value_four,
            preferred_element_type=single_float,
        )
        return (new_max, denom_sum, accum_out)

    running_max, denom_sum, accum_out = lax.fori_loop(0, block_count, visit, start_fwd)
    log_total = running_max + jnp.log(denom_sum)
    attn_o = accum_out / denom_sum[..., None]
    out_low = attn_o.reshape(block_len, row_count, heads_local * HD).astype(bf16)
    attn_part = jnp.einsum("tre,de->trd", out_low, w_out, preferred_element_type=single_float)
    attn_half = lax.psum_scatter(
        attn_part.astype(jnp.bfloat16), "head", scatter_dimension=2, tiled=True
    ).astype(jnp.float32)
    in_half = inputs.astype(single_float)
    resid_half = in_half + attn_half
    resid = lax.all_gather(resid_half.astype(jnp.bfloat16), "head", axis=2, tiled=True).astype(
        resid_half.dtype
    )
    inv_two = lax.rsqrt(jnp.mean(resid * resid, axis=-1, keepdims=True) + EPS)
    norm_two = resid * inv_two
    gain_two = mlp_gain.astype(single_float)
    second_activation = (norm_two * gain_two).astype(bf16)
    gate_value = jnp.einsum(
        "guz,zo->guo", second_activation, gate_weight, preferred_element_type=single_float
    )
    up_projected = jnp.einsum(
        "guz,zo->guo", second_activation, up_weight, preferred_element_type=single_float
    )
    sigma_gate = jax.nn.sigmoid(gate_value)
    act_gate = gate_value * sigma_gate
    hidden_state = (act_gate * up_projected).astype(bf16)
    perceptron_part = jnp.einsum(
        "uel,ql->ueq", hidden_state, down_weight, preferred_element_type=single_float
    )
    mlp_half = lax.psum_scatter(
        perceptron_part.astype(jnp.bfloat16), "head", scatter_dimension=2, tiled=True
    ).astype(jnp.float32)
    output = (resid_half + mlp_half).astype(bf16)
    valid = (query_seg < DOCS).astype(single_float)
    local_sums = jnp.stack(
        [
            jnp.sum(valid) / lax.axis_size("head"),
            jnp.sum(valid * jnp.sum(in_half * in_half, axis=-1)),
            jnp.sum(valid * jnp.sum(attn_half * attn_half, axis=-1)),
            jnp.sum(valid * jnp.sum(mlp_half * mlp_half, axis=-1)),
        ]
    )
    total_sums = lax.psum(local_sums, ("dp", "blk", "head"))
    stats = jnp.sqrt(total_sums[1:] / (total_sums[0] * full_width))
    hidden_gradient = jnp.einsum(
        "guz,zo->guo", full_output_gradient, down_weight, preferred_element_type=single_float
    )
    down_weight_gradient = jnp.einsum(
        "clj,clv->jv", full_output_gradient, hidden_state, preferred_element_type=single_float
    )
    gate_gradient = (
        hidden_gradient * up_projected * sigma_gate * (1.0 + gate_value * (1.0 - sigma_gate))
    ).astype(bf16)
    up_gradient = (hidden_gradient * act_gate).astype(bf16)
    gate_weight_gradient = jnp.einsum(
        "clj,clv->jv", second_activation, gate_gradient, preferred_element_type=single_float
    )
    up_weight_gradient = jnp.einsum(
        "clj,clv->jv", second_activation, up_gradient, preferred_element_type=single_float
    )
    second_part_gradient = jnp.einsum(
        "uel,ql->ueq", gate_gradient, gate_weight, preferred_element_type=single_float
    ) + jnp.einsum("uel,ql->ueq", up_gradient, up_weight, preferred_element_type=single_float)
    d_two = lax.psum(second_part_gradient.astype(jnp.bfloat16), "head").astype(jnp.float32)
    grad_mlp_gain = jnp.sum(d_two * norm_two, axis=(0, 1))
    d_norm_two = d_two * gain_two
    d_resid = full_output_gradient.astype(single_float) + inv_two * (
        d_norm_two - norm_two * jnp.mean(d_norm_two * norm_two, axis=-1, keepdims=True)
    )
    d_attn = d_resid.astype(bf16)
    grad_out = jnp.einsum("trd,tre->de", d_attn, out_low, preferred_element_type=single_float)
    d_out = jnp.einsum("trd,de->tre", d_attn, w_out, preferred_element_type=single_float).astype(
        bf16
    )
    d_out = d_out.reshape(block_len, row_count, kv_local, group, HD)
    row_delta = jnp.sum(d_out.astype(single_float) * attn_o, axis=-1)
    start_back = (
        jnp.zeros(stat_shape + (HD,), single_float),
        jnp.zeros((seq_total, row_count, kv_width), single_float),
        jnp.zeros((seq_total, row_count, kv_width), single_float),
    )
    fold_keys_in = lax.all_gather(keys, "blk", axis=0, tiled=True)
    fold_values_in = lax.all_gather(values, "blk", axis=0, tiled=True)
    block_count = fold_keys_in.shape[0] // block_len

    def visit(step_index, carry_state):
        d_query, d_keys, d_values = carry_state
        offset = step_index * block_len
        key_blk = lax.dynamic_slice_in_dim(fold_keys_in, offset, block_len, 0)
        value_blk = lax.dynamic_slice_in_dim(fold_values_in, offset, block_len, 0)
        key_pos = offset + jnp.arange(block_len, dtype=jnp.int32)
        scores, key_mask = block_scores(key_blk, key_pos)
        prob_w = jnp.where(key_mask, jnp.exp(scores - log_total[..., None]), 0.0)
        value_four = value_blk.reshape(block_len, row_count, kv_local, HD)
        key_four = key_blk.reshape(block_len, row_count, kv_local, HD)
        d_probs = jnp.einsum(
            "qrkgd,srkd->qrkgs", d_out, value_four, preferred_element_type=single_float
        )
        d_scores = (prob_w * (d_probs - row_delta[..., None]) * scale).astype(bf16)
        d_query = d_query + jnp.einsum(
            "qrkgs,srkd->qrkgd", d_scores, key_four, preferred_element_type=single_float
        )
        key_term = jnp.einsum(
            "qrkgs,qrkgd->srkd", d_scores, queries, preferred_element_type=single_float
        ).reshape(block_len, row_count, kv_width)
        value_term = jnp.einsum(
            "qrkgs,qrkgd->srkd", prob_w.astype(bf16), d_out, preferred_element_type=single_float
        ).reshape(block_len, row_count, kv_width)
        d_keys = lax.dynamic_update_slice_in_dim(
            d_keys, lax.dynamic_slice_in_dim(d_keys, offset, block_len, 0) + key_term, offset, 0
        )
        d_values = lax.dynamic_update_slice_in_dim(
            d_values,
            lax.dynamic_slice_in_dim(d_values, offset, block_len, 0) + value_term,
            offset,
            0,
        )
        return (d_query, d_keys, d_values)

    d_query, d_keys, d_values = lax.fori_loop(0, block_count, visit, start_back)
    own_dkeys, own_dvalues = (
        lax.psum_scatter(
            d_keys.astype(jnp.bfloat16), "blk", scatter_dimension=0, tiled=True
        ).astype(jnp.float32),
        lax.psum_scatter(
            d_values.astype(jnp.bfloat16), "blk", scatter_dimension=0, tiled=True
        ).astype(jnp.float32),
    )
    d_q_lin = unrotate(
        d_query.reshape(block_len, row_count, heads_local, HD), cos_tab, sin_tab
    ).astype(bf16)
    d_q_lin = d_q_lin.reshape(block_len, row_count, heads_local * HD)
    d_k_lin = unrotate(
        own_dkeys.reshape(block_len, row_count, kv_local, HD), cos_tab, sin_tab
    ).astype(bf16)
    d_k_lin = d_k_lin.reshape(block_len, row_count, kv_width)
    d_v_lin = own_dvalues.astype(bf16)
    grad_query = jnp.einsum("trd,tre->de", a_one, d_q_lin, preferred_element_type=single_float)
    grad_key = jnp.einsum("trd,tre->de", a_one, d_k_lin, preferred_element_type=single_float)
    grad_value = jnp.einsum("trd,tre->de", a_one, d_v_lin, preferred_element_type=single_float)
    d_one_part = jnp.einsum("tre,de->trd", d_q_lin, w_query, preferred_element_type=single_float)
    d_one_part = d_one_part + jnp.einsum(
        "tre,de->trd", d_k_lin, w_key, preferred_element_type=single_float
    )
    d_one_part = d_one_part + jnp.einsum(
        "tre,de->trd", d_v_lin, w_value, preferred_element_type=single_float
    )
    d_one = lax.psum(d_one_part.astype(jnp.bfloat16), "head").astype(jnp.float32)
    grad_attn_gain = jnp.sum(d_one * norm_one, axis=(0, 1))
    d_norm_one = d_one * gain_one
    d_input = d_resid + inv_one * (
        d_norm_one - norm_one * jnp.mean(d_norm_one * norm_one, axis=-1, keepdims=True)
    )
    d_input_half = lax.dynamic_slice_in_dim(d_input, head_slot * half_width, half_width, 2)
    sum_query, sum_key, sum_value, sum_out, sum_again, sum_gate, sum_up, sum_down, sum_mgain = (
        lax.psum_scatter(grad_query, ("dp", "blk"), scatter_dimension=0, tiled=True),
        lax.psum_scatter(grad_key, ("dp", "blk"), scatter_dimension=0, tiled=True),
        lax.psum_scatter(grad_value, ("dp", "blk"), scatter_dimension=0, tiled=True),
        lax.psum_scatter(grad_out, ("dp", "blk"), scatter_dimension=0, tiled=True),
        lax.psum_scatter(grad_attn_gain, ("dp", "blk"), scatter_dimension=0, tiled=True),
        lax.psum_scatter(gate_weight_gradient, ("dp", "blk"), scatter_dimension=0, tiled=True),
        lax.psum_scatter(up_weight_gradient, ("dp", "blk"), scatter_dimension=0, tiled=True),
        lax.psum_scatter(down_weight_gradient, ("dp", "blk"), scatter_dimension=0, tiled=True),
        lax.psum_scatter(grad_mlp_gain, ("dp", "blk"), scatter_dimension=0, tiled=True),
    )
    return (
        output,
        d_input_half,
        sum_again,
        sum_query,
        sum_key,
        sum_value,
        sum_out,
        sum_mgain,
        sum_gate,
        sum_up,
        sum_down,
        stats,
    )


def solution(mesh):
    in_specs = (
        P("blk", "dp", "head"),
        P("blk", "dp", "head"),
        P("dp", None),
        P(),
        P(None, "head"),
        P(None, "head"),
        P(None, "head"),
        P(None, "head"),
        P(),
        P(None, "head"),
        P(None, "head"),
        P(None, "head"),
    )
    out_specs = (
        P("blk", "dp", "head"),
        P("blk", "dp", "head"),
        P(("dp", "blk")),
        P(("dp", "blk"), "head"),
        P(("dp", "blk"), "head"),
        P(("dp", "blk"), "head"),
        P(("dp", "blk"), "head"),
        P(("dp", "blk")),
        P(("dp", "blk"), "head"),
        P(("dp", "blk"), "head"),
        P(("dp", "blk"), "head"),
        P(),
    )
    return jax.shard_map(body, mesh=mesh, in_specs=in_specs, out_specs=out_specs, check_vma=False)
```

profile of v0, /device:TPU:0, one launch (start us, length us, event | category | flops | bytes accessed | tf_op | source)
XLA Modules:
  0.0 1749.6 jit_solution(10123397866645457139)
XLA Ops:
  16.2 29.3 %all-gather.5.cloned.1.call-done = bf16[512,1,2048]{2,0,1:T(8,128)(2,1)} async-done(((bf16[512,1,1024]{2,0,1:T(8,128)(2,1)}), bf16[512,1,2048]{2,0,1:T(8,128)(2,1)}) %all-gather.5.cloned.1.call-update) | async-done | bytes 2097168 | tf_op jit(solution)/shard_map/all_gather | solution.py:78
  55.3 15.6 all_gather.18
  71.7 16.5 all-gather
  89.7 93.7 %while.36 = (s32[]{:T(128)}, f32[512,1,2,8]{0,3,2,1:T(8,128)S(1)}, f32[512,1,2,8]{0,3,2,1:T(8,128)S(1)}, f32[512,1,2,8,64]{0,4,3,2,1:T(8,128)}, s32[512,1]{0,1:T...) while((s32[]{:T(128)}, f32[512,1,2,8]{0,3,2,1:T(8,128)S(1)}, ...), condition=%wide.region_7.8_spmd.clone, body=%wide.region_3.7_spmd.clone.sunk | while | flops 1130689024 | bytes 125059328 | solution.py:138
  192.6 31.4 %reduce-scatter.12.cloned.1.call-done = bf16[512,1,1024]{2,0,1:T(8,128)(2,1)} async-done(((bf16[512,1,2048]{2,0,1:T(8,128)(2,1)}), bf16[512,1,1024]{2,0,1:T(8,128)(2,1)}) %reduce-scatter.12.cloned.1.call-update) | async-done | bytes 1048592 | tf_op jit(solution)/shard_map/reduce_scatter | solution.py:143
  227.6 32.2 %all-gather.7.cloned.1.call-done = bf16[512,1,2048]{2,0,1:T(8,128)(2,1)} async-done(((bf16[512,1,1024]{2,0,1:T(8,128)(2,1)}), bf16[512,1,2048]{2,0,1:T(8,128)(2,1)}) %all-gather.7.cloned.1.call-update) | async-done | bytes 2097168 | tf_op jit(solution)/shard_map/all_gather | solution.py:148
  261.9 12.8 fusion.103
  294.5 16.4 multiply_convert_fusion
  310.9 12.3 fusion.107
  333.2 62.2 %all-reduce.6.cloned.1.call-done = bf16[512,1,2048]{2,0,1:T(8,128)(2,1)} async-done(((bf16[512,1,2048]{2,0,1:T(8,128)(2,1)}), bf16[512,1,2048]{2,0,1:T(8,128)(2,1)}) %all-reduce.6.cloned.1.call-update) | async-done | bytes 2097168 | tf_op jit(solution)/shard_map/psum | solution.py:201
  413.9 151.8 %while.37 = (s32[]{:T(128)}, f32[512,1,2,8,64]{0,4,3,2,1:T(8,128)}, f32[2048,1,128]{0,2,1:T(8,128)S(1)}, f32[2048,1,128]{0,2,1:T(8,128)}, bf16[2048,1,128]{0,2,1...) while((s32[]{:T(128)}, f32[512,1,2,8,64]{0,4,3,2,1:T(8,128)}, ...), condition=%wide.region_16.17_spmd.clone, body=%wide.region_14.16_spmd.clone.sunk | while | flops 2732470784 | bytes 130007464 | solution.py:257
  592.2 19.1 %reduce-scatter.18.cloned.1.call-done = bf16[512,1,128]{0,2,1:T(8,128)(2,1)} async-done(((bf16[2048,1,128]{0,2,1:T(8,128)(2,1)}), bf16[512,1,128]{0,2,1:T(8,128)(2,1)}) %reduce-scatter.18.cloned.1.call-update) | async-done | bytes 131088 | tf_op jit(solution)/shard_map/reduce_scatter | solution.py:262
  616.9 13.2 convolution_bitcast_fusion
  653.6 12.7 fusion.101
  666.3 12.9 fusion.99
  687.5 38.6 %psum.23 = f32[4]{0:T(128)S(1)} all-reduce(f32[4]{0:T(128)S(1)} %pad_maximum_fusion.2), channel_id=1, replica_groups=mesh['dp'=4,'blk'=4,'head'=2] {'dp','blk','head'}, use_global_device_ids=true, to_apply=%region_39.40 | all-reduce | flops 4 | bytes 32 | tf_op jit(solution)/shard_map/psum | solution.py:180
  735.9 63.1 %all-reduce.2 = (f32[2048]{0:T(1024)S(1)}, f32[2048]{0:T(1024)S(1)}) all-reduce(f32[2048]{0:T(1024)S(1)} %get-tuple-element.628, f32[2048]{0:T(1024)S(1)} %copy-done.33), channel_id=7, replica_groups=mesh['dp'=4,'blk'=4,'head'=2] {'dp','blk'}, use_global_device_ids=true, to_apply=%region_22.23.clone | all-reduce | flops 4096 | bytes 32768
  807.0 135.3 %reduce-scatter.32.cloned.1.call-done = f32[128,2816]{0,1:T(8,128)} async-done(((f32[2048,2816]{0,1:T(8,128)}), f32[128,2816]{0,1:T(8,128)}) %reduce-scatter.32.cloned.1.call-update) | async-done | bytes 1441808 | tf_op jit(solution)/shard_map/reduce_scatter | solution.py:300
  945.2 57.8 %reduce-scatter.22.cloned.1.call-done = f32[128,128]{1,0:T(8,128)} async-done(((f32[2048,128]{1,0:T(8,128)}), f32[128,128]{1,0:T(8,128)}) %reduce-scatter.22.cloned.1.call-update) | async-done | bytes 65552 | tf_op jit(solution)/shard_map/reduce_scatter | solution.py:294
  1003.0 61.0 %reduce-scatter.24.cloned.1.call-done = f32[128,128]{1,0:T(8,128)} async-done(((f32[2048,128]{1,0:T(8,128)}), f32[128,128]{1,0:T(8,128)}) %reduce-scatter.24.cloned.1.call-update) | async-done | bytes 65552 | tf_op jit(solution)/shard_map/reduce_scatter | solution.py:295
  1064.0 108.2 %reduce-scatter.26.cloned.1.call-done = f32[128,1024]{1,0:T(8,128)} async-done(((f32[2048,1024]{1,0:T(8,128)}), f32[128,1024]{1,0:T(8,128)}) %reduce-scatter.26.cloned.1.call-update) | async-done | bytes 524304 | tf_op jit(solution)/shard_map/reduce_scatter | solution.py:296
  1172.3 108.9 %reduce-scatter.20.cloned.1.call-done = f32[128,1024]{1,0:T(8,128)} async-done(((f32[2048,1024]{1,0:T(8,128)}), f32[128,1024]{1,0:T(8,128)}) %reduce-scatter.20.cloned.1.call-update) | async-done | bytes 524304 | tf_op jit(solution)/shard_map/reduce_scatter | solution.py:293
  1281.1 231.2 %reduce-scatter.28.cloned.1.call-done = f32[128,2816]{1,0:T(8,128)} async-done(((f32[2048,2816]{1,0:T(8,128)}), f32[128,2816]{1,0:T(8,128)}) %reduce-scatter.28.cloned.1.call-update) | async-done | bytes 1441808 | tf_op jit(solution)/shard_map/reduce_scatter | solution.py:298
  1512.3 230.5 %reduce-scatter.30.cloned.1.call-done = f32[128,2816]{1,0:T(8,128)} async-done(((f32[2048,2816]{1,0:T(8,128)}), f32[128,2816]{1,0:T(8,128)}) %reduce-scatter.30.cloned.1.call-update) | async-done | bytes 1441808 | tf_op jit(solution)/shard_map/reduce_scatter | solution.py:299
  (331 shorter events, 411.5 us)
Async XLA Ops:
  7.2 63.7 %copy-start = (bf16[2048,128]{1,0:T(8,128)(2,1)S(1)}, bf16[2048,128]{1,0:T(8,128)(2,1)}, u32[]{:S(2)}) copy-start(bf16[2048,128]{1,0:T(8,128)(2,1)} %param.22) | copy-start | bytes 1572868
  7.2 38.2 %all-gather.5.cloned.1.call-start = ((), (), s32[]{:S(2)}) async-start(), calls=%async_computation.11 | async-start | bytes 3145728 | tf_op jit(solution)/shard_map/all_gather | solution.py:78
  7.9 216.0 %reduce-scatter.12.cloned.1.call-start = ((), (), s32[]{:S(2)}) async-start(), calls=%async_computation.12 | async-start | bytes 3145728 | tf_op jit(solution)/shard_map/reduce_scatter | solution.py:143
  8.7 62.2 %copy-start.35 = (f32[2048]{0:T(1024)}, f32[2048]{0:T(1024)S(1)}, u32[]{:S(2)}) copy-start(f32[2048]{0:T(1024)S(1)} %convert_element_type.273) | copy-start | bytes 24580
  16.1 39.0 %copy-start.24 = (f32[512,32]{0,1:T(8,128)}, f32[512,32]{0,1:T(8,128)S(1)}, u32[]{:S(2)}) copy-start(f32[512,32]{0,1:T(8,128)S(1)} %get-tuple-element.709) | copy-start | bytes 196612
  16.1 39.0 %copy-start.26 = (f32[512,32]{0,1:T(8,128)}, f32[512,32]{0,1:T(8,128)S(1)}, u32[]{:S(2)}) copy-start(f32[512,32]{0,1:T(8,128)S(1)} %get-tuple-element.710) | copy-start | bytes 196612
  186.5 37.5 %copy-start.8 = (bf16[512,1,1024]{2,0,1:T(8,128)(2,1)S(1)}, bf16[512,1,1024]{2,0,1:T(8,128)(2,1)}, u32[]{:S(2)}) copy-start(bf16[512,1,1024]{2,0,1:T(8,128)(2,1)} %param.16) | copy-start | bytes 3145732
  192.5 35.1 %copy-start.41 = (bf16[2048]{0:T(1024)(128)(2,1)S(1)}, bf16[2048]{0:T(1024)(128)(2,1)}, u32[]{:S(2)}) copy-start(bf16[2048]{0:T(1024)(128)(2,1)} %param.24) | copy-start | bytes 12292
  192.5 67.3 %all-gather.7.cloned.1.call-start = ((), (), s32[]{:S(2)}) async-start(), calls=%async_computation.13 | async-start | bytes 3145728 | tf_op jit(solution)/shard_map/all_gather | solution.py:148
  226.6 67.9 %all-gather.9.cloned.1.call-start = ((), (), s32[]{:S(2)}) async-start(), calls=%async_computation.15 | async-start | bytes 3145728 | tf_op jit(solution)/shard_map/all_gather | solution.py:79
  227.1 168.2 %all-reduce.6.cloned.1.call-start = ((), (), s32[]{:S(2)}) async-start(), calls=%async_computation.16 | async-start | bytes 4194304 | tf_op jit(solution)/shard_map/psum | solution.py:201
  227.6 172.0 %copy-start.30 = (f32[2048]{0:T(1024)}, f32[2048]{0:T(1024)S(1)}, u32[]{:S(2)}) copy-start(f32[2048]{0:T(1024)S(1)} %convert_element_type.286) | copy-start | bytes 24580
  261.9 137.7 %copy-start.37 = (f32[512]{0:T(512)}, f32[512]{0:T(512)S(1)}, u32[]{:S(2)}) copy-start(f32[512]{0:T(512)S(1)} %add_rsqrt_fusion) | copy-start | bytes 6148
  332.3 256.2 %reduce-scatter.16.cloned.1.call-start = ((), (), s32[]{:S(2)}) async-start(), calls=%async_computation.17 | async-start | bytes 655360 | tf_op jit(solution)/shard_map/reduce_scatter | solution.py:259
  566.7 44.6 %reduce-scatter.18.cloned.1.call-start = ((), (), s32[]{:S(2)}) async-start(), calls=%async_computation.18 | async-start | bytes 655360 | tf_op jit(solution)/shard_map/reduce_scatter | solution.py:262
  568.8 112.3 %reduce-scatter.14.cloned.1.call-start = ((), (), s32[]{:S(2)}) async-start(), calls=%async_computation.14 | async-start | bytes 3145728 | tf_op jit(solution)/shard_map/reduce_scatter | solution.py:167
  579.9 146.8 %all-reduce.8.cloned.1.call-start = ((), (), s32[]{:S(2)}) async-start(), calls=%async_computation.19 | async-start | bytes 4194304 | tf_op jit(solution)/shard_map/psum | solution.py:285
  616.9 325.4 %reduce-scatter.32.cloned.1.call-start = ((), (), s32[]{:S(2)}) async-start(), calls=%async_computation.26 | async-start | bytes 24510464 | tf_op jit(solution)/shard_map/reduce_scatter | solution.py:300
  630.2 372.8 %reduce-scatter.22.cloned.1.call-start = ((), (), s32[]{:S(2)}) async-start(), calls=%async_computation.21 | async-start | bytes 1114112 | tf_op jit(solution)/shard_map/reduce_scatter | solution.py:294
  633.7 430.3 %reduce-scatter.24.cloned.1.call-start = ((), (), s32[]{:S(2)}) async-start(), calls=%async_computation.22 | async-start | bytes 1114112 | tf_op jit(solution)/shard_map/reduce_scatter | solution.py:295
  635.8 536.4 %reduce-scatter.26.cloned.1.call-start = ((), (), s32[]{:S(2)}) async-start(), calls=%async_computation.23 | async-start | bytes 8912896 | tf_op jit(solution)/shard_map/reduce_scatter | solution.py:296
  644.2 637.0 %reduce-scatter.20.cloned.1.call-start = ((), (), s32[]{:S(2)}) async-start(), calls=%async_computation.20 | async-start | bytes 8912896 | tf_op jit(solution)/shard_map/reduce_scatter | solution.py:293
  651.6 860.8 %reduce-scatter.28.cloned.1.call-start = ((), (), s32[]{:S(2)}) async-start(), calls=%async_computation.24 | async-start | bytes 24510464 | tf_op jit(solution)/shard_map/reduce_scatter | solution.py:298
  666.3 1076.6 %reduce-scatter.30.cloned.1.call-start = ((), (), s32[]{:S(2)}) async-start(), calls=%async_computation.25 | async-start | bytes 24510464 | tf_op jit(solution)/shard_map/reduce_scatter | solution.py:299
  (62 other events, 497.4 us)
Sparse Core Ops, SparseCore 0:
  9.6 35.7 all-gather.4
  192.6 31.2 reduce-scatter.11
  226.7 33.1 all-gather.6
  261.3 33.1 all-gather.8
  332.4 62.9 all-reduce.5
  566.8 21.6 reduce-scatter.15
  591.3 19.9 reduce-scatter.17
  614.1 30.1 reduce-scatter.13
  646.7 63.6 all-reduce.7
  714.3 227.9 reduce-scatter.31
  946.5 56.4 reduce-scatter.21
  1007.5 56.4 reduce-scatter.23
  1068.7 103.5 reduce-scatter.25
  1176.8 104.3 reduce-scatter.19
  1285.7 226.6 reduce-scatter.27
  1516.9 225.9 reduce-scatter.29
where the time goes:
time: 1760 us; the launch traced here: 1750 us
  waiting for transfers between devices  1120 us (64%)
  matrix products  367 us (21%)
  blocking collectives  134 us (8%)
  other arithmetic  72.9 us (4%)
  local copies, waits for them, and re-layouts  39.4 us (2%)
    reduce_scatter x1, waiting for transfers between devices, body(): lax.psum_scatter(gate_weight_gradient, ('dp', 'blk'), scatter_dimension=0...  231 us
    reduce_scatter x1, waiting for transfers between devices, body(): lax.psum_scatter(up_weight_gradient, ('dp', 'blk'), scatter_dimension=0,...  231 us
    reduce_scatter x1, waiting for transfers between devices, body(): lax.psum_scatter(down_weight_gradient, ('dp', 'blk'), scatter_dimension=0...  135 us
    reduce_scatter x1, waiting for transfers between devices, body(): lax.psum_scatter(grad_query, ('dp', 'blk'), scatter_dimension=0, tiled=True)  109 us
    reduce_scatter x1, waiting for transfers between devices, body(): lax.psum_scatter(grad_out, ('dp', 'blk'), scatter_dimension=0, tiled=True)  108 us
    unnamed x1, blocking collectives  63.1 us
    psum x1, waiting for transfers between devices, body(): lax.psum(second_part_gradient.astype(jnp.bfloat16), 'head')  62.2 us
    dot_general x8, matrix products, block_scores(): jnp.einsum('qrkgd,srkd->qrkgs', queries, key_four, preferred_element_type...  61.3 us
  transfers between devices with their start and end apart: 16, of which 14 were waited for; matrix products, arithmetic and copies ran while one was open for 8% of the time, Pallas kernels for 0%

commit v1 on v0

v1 whole, which is shorter than its diff:
```python
import functools

import jax
import jax.numpy as jnp
from jax import lax
from jax.experimental import pallas as pl
from jax.experimental.pallas import tpu as pltpu
from jax.sharding import PartitionSpec as P

HD = 64
PAIR = 2 * HD
DOCS = 8
EPS = 1e-05
THETA = 10000.0
NEG = -1e30
F32 = jnp.float32
BF16 = jnp.bfloat16
FT = 256


EARLY, LATE = 0.4, 0.4
WEIGHT = [EARLY]


def params(mib):
    return pltpu.CompilerParams(vmem_limit_bytes=mib << 20)


def cost(flops, byte_count, trans=0):
    return pl.CostEstimate(
        flops=int(flops * WEIGHT[0]),
        bytes_accessed=int(byte_count * WEIGHT[0]),
        transcendentals=int(trans * WEIGHT[0]),
    )


CHAIN = []


def in_hbm(x):
    return pltpu.with_memory_space_constraint(x, pltpu.HBM)


def launch(kernel, args, *, grid, in_specs, out_specs, out_shape, mib, estimate, name, scratch=(), prefetch=0, deps=(), pin_in=True, pin_out=True):
    extra = list(CHAIN) + list(deps)
    n_in, n_out = len(args), len(out_shape)

    def wrapped(*refs):
        rest = refs[n_in + len(extra) :]
        kernel(*refs[:n_in], *rest[:n_out], *rest[n_out + 1 :])

    if pin_in:
        args = tuple(args[:prefetch]) + tuple(in_hbm(x) for x in args[prefetch:])
    if pin_out:
        out_shape = [pltpu.HBM(o.shape, o.dtype) for o in out_shape]
    extra = [in_hbm(x) for x in extra]
    *outs, token = pl.pallas_call(
        wrapped,
        grid_spec=pltpu.PrefetchScalarGridSpec(
            num_scalar_prefetch=prefetch,
            grid=grid,
            in_specs=list(in_specs) + [pl.BlockSpec(memory_space=pltpu.HBM)] * len(extra),
            out_specs=list(out_specs) + [pl.BlockSpec(memory_space=pltpu.HBM)],
            scratch_shapes=list(scratch),
        ),
        out_shape=list(out_shape) + [pltpu.HBM((8, 128), F32)],
        compiler_params=params(mib),
        cost_estimate=estimate,
        name=name,
    )(*args, *extra)
    CHAIN[:] = [token]
    return outs


def dot(a, b):
    return jnp.dot(a, b, preferred_element_type=F32)


def dot_nt(a, b):
    return lax.dot_general(a, b, (((1,), (1,)), ((), ())), preferred_element_type=F32)


def dot_tn(a, b):
    return lax.dot_general(a, b, (((0,), (0,)), ((), ())), preferred_element_type=F32)


def swap(x, axis, bit):
    n = lax.axis_size(axis)
    return lax.ppermute(x, axis, [(i, i ^ bit) for i in range(n)])


def lanes(shape):
    return lax.broadcasted_iota(jnp.int32, shape, len(shape) - 1)


def turn(x, cos, sin):
    out = []
    for c in range(x.shape[1] // PAIR):
        v = x[:, c * PAIR : (c + 1) * PAIR]
        low = lanes(v.shape) % HD < HD // 2
        other = jnp.where(low, pltpu.roll(v, PAIR - HD // 2, 1), pltpu.roll(v, HD // 2, 1))
        out.append(v * cos + other * sin)
    return out[0] if len(out) == 1 else jnp.concatenate(out, axis=1)


def project_kernel(h_ref, own, oth, gain, wq, wk, wv, cos, sin, full, a1, q, kv, ssx):
    first = h_ref[0] == 0
    x_own = own[...].astype(F32)
    x_oth = oth[...].astype(F32)
    x = jnp.concatenate(
        [jnp.where(first, x_own, x_oth), jnp.where(first, x_oth, x_own)], axis=1
    )
    width = x.shape[1]
    total = jnp.sum(x * x, axis=1, keepdims=True)
    inv = lax.rsqrt(total * (1.0 / width) + EPS)
    act = (x * inv * gain[...]).astype(BF16)
    full[...] = x.astype(BF16)
    a1[...] = act
    ssx[...] = jnp.broadcast_to(total, ssx.shape)
    q[...] = turn(dot(act, wq[...]), cos[...], sin[...]).astype(BF16) * (HD**-0.5)
    kvw = wk.shape[1]
    kv[:, :kvw] = turn(dot(act, wk[...]), cos[...], sin[...]).astype(BF16)
    kv[:, kvw:] = dot(act, wv[...]).astype(BF16)


def project(h, own, oth, gain, wq, wk, wv, cos, sin):
    n, half = own.shape
    d = 2 * half
    tt = min(n, 256)
    qw, kvw = wq.shape[1], wk.shape[1]
    row = lambda w: pl.BlockSpec((tt, w), lambda i, *_: (i, 0))
    const = lambda a: pl.BlockSpec(a.shape, lambda i, *_: (0, 0), pipeline_mode=pl.Buffered(1))
    return launch(
        project_kernel,
        (h, own, oth, gain, wq, wk, wv, cos, sin),
        prefetch=1,
        grid=(n // tt,),
        in_specs=[row(half), row(half), const(gain), const(wq), const(wk), const(wv)]
        + [row(PAIR), row(PAIR)],
        out_specs=[row(d), row(d), row(qw), row(2 * kvw), row(PAIR)],
        out_shape=[
            jax.ShapeDtypeStruct((n, d), BF16),
            jax.ShapeDtypeStruct((n, d), BF16),
            jax.ShapeDtypeStruct((n, qw), BF16),
            jax.ShapeDtypeStruct((n, 2 * kvw), BF16),
            jax.ShapeDtypeStruct((n, PAIR), F32),
        ],
        mib=32,
        pin_in=False,
        estimate=cost(2 * n * d * (qw + 2 * kvw), 2 * d * (qw + 2 * kvw) + 12 * n * d),
        name="project",
    )


def place(kv, kvh, base):
    x = kv[:, base : base + PAIR].astype(F32)
    x = jnp.where(kvh == 0, x, pltpu.roll(x, HD, 1))
    low = jnp.where(lanes(x.shape) < HD, x, 0.0)
    return low.astype(BF16), pltpu.roll(low, HD, 1).astype(BF16)


def flip_head(kv, kvh, base):
    x = kv[:, base : base + PAIR].astype(F32).T
    return jnp.where(kvh == 0, x[:HD, :], x[HD:, :])


def attend_kernel(step, last, ppk, sc, q_ref, kv_ref, start_ref, *refs):
    refs = list(refs)
    if step:
        acc_in, ml_in = refs[:2]
        refs = refs[2:]
    acc_out, ml_out = refs
    t = q_ref.shape[0]
    kvh = pl.program_id(1)
    blk = sc[0]

    def finish(pair, par, acc, m, l):
        rows = slice(pair * PAIR + par * HD, pair * PAIR + (par + 1) * HD)
        if last:
            acc = acc / l
            m = m + jnp.log(l)
        acc_out[rows, :] = acc
        ml_out[pair, par : par + 1, :] = m
        ml_out[pair, 2 + par : 3 + par, :] = l

    heads = [(pair, par) for pair in range(ppk) for par in range(2)]

    def work():
        u = lax.broadcasted_iota(jnp.int32, (t, t), 0) + (blk - step) * t
        keep = u >= start_ref[0]
        if step == 0:
            keep = keep & (u <= lanes((t, t)) + blk * t)
        bias = jnp.where(keep, 0.0, NEG)
        kv = kv_ref[...]
        kk = place(kv, kvh, 0)
        ones = jnp.where(lax.broadcasted_iota(jnp.int32, (16, t), 0) == 0, 1.0, 0.0)
        vt = jnp.concatenate([flip_head(kv, kvh, PAIR), ones], axis=0).astype(BF16)
        scores = [
            dot_nt(kk[par], q_ref[:, pair * PAIR : (pair + 1) * PAIR]) + bias
            for pair, par in heads
        ]
        for (pair, par), s in zip(heads, scores, strict=True):
            m = jnp.max(s, axis=0, keepdims=True)
            if step:
                old = ml_in[pair, par : par + 1, :]
                m = jnp.maximum(m, old)
            pv = dot(vt, jnp.exp(s - m).astype(BF16))
            acc, l = pv[:HD], pv[HD : HD + 1]
            if step:
                factor = jnp.exp(old - m)
                rows = slice(pair * PAIR + par * HD, pair * PAIR + (par + 1) * HD)
                acc = acc + acc_in[rows, :] * factor
                l = l + ml_in[pair, 2 + par : 3 + par, :] * factor
            finish(pair, par, acc, m, l)

    if step == 0:
        work()
    else:
        pl.when(blk >= step)(work)

        @pl.when(blk < step)
        def _():
            for pair, par in heads:
                rows = slice(pair * PAIR + par * HD, pair * PAIR + (par + 1) * HD)
                m = ml_in[pair, par : par + 1, :]
                finish(pair, par, acc_in[rows, :], m, ml_in[pair, 2 + par : 3 + par, :])


def attend(step, last, sc, q, kv, start, state, rows, deps=()):
    n, qw = q.shape
    t = n // rows
    pairs = qw // PAIR
    kv_heads = kv.shape[1] // 2 // HD
    ppk = pairs // kv_heads
    accspec = pl.BlockSpec((ppk * PAIR, t), lambda r, k, *_: (k, r))
    mlspec = pl.BlockSpec((ppk, 8, t), lambda r, k, *_: (k, 0, r))
    work = n * t * qw
    return launch(
        functools.partial(attend_kernel, step, last, ppk),
        (sc, in_hbm(q), in_hbm(kv), in_hbm(start), *state),
        prefetch=1,
        grid=(rows, kv_heads),
        in_specs=[
            pl.BlockSpec((t, ppk * PAIR), lambda r, k, *_: (r, k)),
            pl.BlockSpec((t, kv.shape[1]), lambda r, k, *_: (r, 0)),
            pl.BlockSpec((1, 1, t), lambda r, k, *_: (r, 0, 0)),
        ]
        + ([accspec, mlspec] if state else []),
        out_specs=[accspec, mlspec],
        out_shape=[
            jax.ShapeDtypeStruct((qw, n), F32),
            jax.ShapeDtypeStruct((pairs, 8, n), F32),
        ],
        mib=28,
        estimate=cost(24 * work, 20 * n * qw, n * t * qw // HD),
        name=f"attend{step}",
        deps=deps,
        pin_in=False,
        pin_out=False,
    )


def flip_kernel(x, out):
    out[...] = x[...].T.astype(BF16)


def flip(x, name="flip"):
    w, n = x.shape
    by_rows = w > n
    step = 512 if max(w, n) % 512 == 0 else max(w, n)
    across = pl.BlockSpec((step, n) if by_rows else (w, step), lambda i: (i, 0) if by_rows else (0, i))
    down = pl.BlockSpec((n, step) if by_rows else (step, w), lambda i: (0, i) if by_rows else (i, 0))
    return launch(
        flip_kernel,
        (x,),
        grid=(max(w, n) // step,),
        in_specs=[across],
        out_specs=[down],
        out_shape=[jax.ShapeDtypeStruct((n, w), BF16)],
        mib=32,
        estimate=cost(8 * n * w, 6 * n * w),
        name=name,
        pin_in=False,
    )[0]


def attend_back_kernel(step, first, last, ppk, sc, q_ref, do_ref, ml_ref, start_ref, kv_ref, *refs):
    refs = list(refs)
    o_ref = refs.pop(0) if first else None
    dq_in, delta_in = (None, None) if first else (refs.pop(0), refs.pop(0))
    cos, sin = (refs.pop(0), refs.pop(0)) if last else (None, None)
    dq_out, dkv_out = refs.pop(0), refs.pop(0)
    delta_out = refs.pop(0) if first else None
    dk_acc, dv_acc, dq_acc = refs
    t = q_ref.shape[0]
    kvh = pl.program_id(1)
    blk = sc[0]
    heads = [(pair, par) for pair in range(ppk) for par in range(2)]

    if first:
        for pair in range(ppk):
            both = slice(pair * PAIR, (pair + 1) * PAIR)
            prod = (do_ref[:, both].astype(F32) * o_ref[:, both].astype(F32)).T
            for par in range(2):
                delta_out[pair, par : par + 1, :] = jnp.sum(
                    prod[par * HD : (par + 1) * HD, :], axis=0, keepdims=True
                )
        dq_acc[...] = jnp.zeros_like(dq_acc)
    else:
        dq_acc[...] = dq_in[...]
    delta = delta_out if first else delta_in

    @pl.when(kvh == 0)
    def _():
        dkv_out[...] = jnp.zeros_like(dkv_out)

    def work():
        u = lax.broadcasted_iota(jnp.int32, (t, t), 0) + (blk - step) * t
        keep = u >= start_ref[0]
        if step == 0:
            keep = keep & (u <= lanes((t, t)) + blk * t)
        bias = jnp.where(keep, 0.0, NEG)
        kv = kv_ref[...]
        kk = place(kv, kvh, 0)
        vv = place(kv, kvh, PAIR)
        kt = flip_head(kv, kvh, 0).astype(BF16)
        dk_acc[...] = jnp.zeros_like(dk_acc)
        dv_acc[...] = jnp.zeros_like(dv_acc)
        for pair, par in heads:
            q = q_ref[:, pair * PAIR : (pair + 1) * PAIR]
            do = do_ref[:, pair * PAIR : (pair + 1) * PAIR]
            st = dot_nt(kk[par], q) + bias
            dp = dot_nt(vv[par], do)
            pt = jnp.exp(st - ml_ref[pair, par : par + 1, :])
            ds = (pt * (dp - delta[pair, par : par + 1, :])).astype(BF16)
            dv_acc[par] += dot(pt.astype(BF16), do)
            dk_acc[par] += dot(ds, q)
            rows = slice(pair * PAIR + par * HD, pair * PAIR + (par + 1) * HD)
            dq_acc[rows, :] += dot(kt, ds)
        low = lanes((t, PAIR)) < HD
        for acc, base in ((dk_acc, 0), (dv_acc, PAIR)):
            both = acc[0] + pltpu.roll(acc[1], HD, 1)
            here = jnp.where(kvh == 0, both, pltpu.roll(both, HD, 1))
            mine = low == (kvh == 0)
            old = dkv_out[:, base : base + PAIR].astype(F32)
            dkv_out[:, base : base + PAIR] = jnp.where(mine, here, old).astype(BF16)

    if step == 0:
        work()
    else:
        pl.when(blk >= step)(work)

    if last:
        for pair in range(ppk):
            rows = slice(pair * PAIR, (pair + 1) * PAIR)
            dq = (dq_acc[rows, :] * (HD**-0.5)).T
            dq_out[:, rows] = turn(dq, cos[...], -sin[...]).astype(BF16)
    else:
        dq_out[...] = dq_acc[...]


def attend_back(step, first, last, sc, q, do, o, ml, start, cos, sin, kv, state, rows, deps=()):
    n, qw = q.shape
    t = n // rows
    pairs = qw // PAIR
    kvw = kv.shape[1]
    kv_heads = kvw // 2 // HD
    ppk = pairs // kv_heads
    width = ppk * PAIR
    pairspec = pl.BlockSpec((t, width), lambda r, k, *_: (r, k))
    accspec = pl.BlockSpec((width, t), lambda r, k, *_: (k, r))
    mlspec = pl.BlockSpec((ppk, 8, t), lambda r, k, *_: (k, 0, r))
    rowspec = lambda w: pl.BlockSpec((t, w), lambda r, k, *_: (r, 0))
    work = n * t * qw
    return launch(
        functools.partial(attend_back_kernel, step, first, last, ppk),
        (sc, q, do, ml, start, kv)
        + ((o,) if first else tuple(state))
        + ((cos, sin) if last else ()),
        prefetch=1,
        grid=(rows, kv_heads),
        in_specs=[pairspec, pairspec, mlspec]
        + [pl.BlockSpec((1, 1, t), lambda r, k, *_: (r, 0, 0))]
        + [rowspec(kvw)]
        + ([pairspec] if first else [accspec, mlspec])
        + ([rowspec(PAIR)] * 2 if last else []),
        out_specs=[pairspec if last else accspec, rowspec(kvw)] + ([mlspec] if first else []),
        scratch=[
            pltpu.VMEM((2, t, PAIR), F32),
            pltpu.VMEM((2, t, PAIR), F32),
            pltpu.VMEM((width, t), F32),
        ],
        out_shape=[
            jax.ShapeDtypeStruct((n, qw), BF16) if last else jax.ShapeDtypeStruct((qw, n), F32),
            jax.ShapeDtypeStruct((n, kvw), BF16),
        ]
        + ([jax.ShapeDtypeStruct((pairs, 8, n), F32)] if first else []),
        mib=40,
        estimate=cost(54 * work, 20 * n * qw, work // HD),
        name=f"attend_back{step}",
        deps=deps,
    )


def gather_dkv_kernel(count, *refs):
    parts = refs[:count]
    cos, sin, out = refs[count:]
    total = parts[0][...].astype(F32)
    for x in parts[1:]:
        total = total + x[...].astype(F32)
    half = total.shape[1] // 2
    out[:, :half] = turn(total[:, :half], cos[...], -sin[...]).astype(BF16)
    out[:, half:] = total[:, half:].astype(BF16)


def gather_dkv(parts, cos, sin, deps=()):
    whole = lambda x: pl.BlockSpec(x.shape, lambda i: (0, 0))
    return launch(
        functools.partial(gather_dkv_kernel, len(parts)),
        (*parts, cos, sin),
        grid=(1,),
        in_specs=[whole(x) for x in (*parts, cos, sin)],
        out_specs=[whole(parts[0])],
        out_shape=[jax.ShapeDtypeStruct(parts[0].shape, BF16)],
        mib=32,
        estimate=cost(10 * parts[0].size, 4 * len(parts) * parts[0].size),
        name="gather_dkv",
        deps=deps,
    )[0]


def merge_kernel(o_own, o_oth, w_own, w_oth, full, gain, h1, a2, a2_t, r2, ssa, held, sums):
    i = pl.program_id(0)
    attn = dot_nt(o_own[...], w_own[...]) + dot_nt(o_oth[...], w_oth[...])
    x = full[...].astype(F32) + attn
    h1[0] = x
    held[i] = x

    @pl.when(i == 0)
    def _():
        sums[...] = jnp.zeros_like(sums)
        ssa[...] = jnp.zeros_like(ssa)

    sums[...] += jnp.sum(x * x, axis=1, keepdims=True)
    ssa[...] += jnp.sum(attn * attn, axis=1, keepdims=True)

    @pl.when(i == pl.num_programs(0) - 1)
    def _():
        count, _, dt = held.shape
        inv = lax.rsqrt(sums[...] * (1.0 / (count * dt)) + EPS)
        r2[...] = inv
        for j in range(count):
            at = slice(j * dt, (j + 1) * dt)
            act = (held[j] * inv[:, :1] * gain[:, at]).astype(BF16)
            a2[:, at] = act
            a2_t[at, :] = act.T


def merge(o_own, o_oth, w_own, w_oth, full, gain, deps=()):
    n, d = full.shape
    dt = 512
    e = o_own.shape[1]
    const = lambda a: pl.BlockSpec(a.shape, lambda i: (0, 0), pipeline_mode=pl.Buffered(1))
    return launch(
        merge_kernel,
        (o_own, o_oth, w_own, w_oth, full, gain),
        grid=(d // dt,),
        in_specs=[
            const(o_own),
            const(o_oth),
            pl.BlockSpec((dt, e), lambda i: (i, 0)),
            pl.BlockSpec((dt, e), lambda i: (i, 0)),
            pl.BlockSpec((n, dt), lambda i: (0, i)),
            const(gain),
        ],
        out_specs=[
            pl.BlockSpec((1, n, dt), lambda i: (i, 0, 0)),
            pl.BlockSpec((n, d), lambda i: (0, 0)),
            pl.BlockSpec((d, n), lambda i: (0, 0)),
            pl.BlockSpec((n, PAIR), lambda i: (0, 0)),
            pl.BlockSpec((n, PAIR), lambda i: (0, 0)),
        ],
        out_shape=[
            jax.ShapeDtypeStruct((d // dt, n, dt), F32),
            jax.ShapeDtypeStruct((n, d), BF16),
            jax.ShapeDtypeStruct((d, n), BF16),
            jax.ShapeDtypeStruct((n, PAIR), F32),
            jax.ShapeDtypeStruct((n, PAIR), F32),
        ],
        scratch=[pltpu.VMEM((d // dt, n, dt), F32), pltpu.VMEM((n, PAIR), F32)],
        mib=48,
        estimate=cost(3 * n * d * d, 2 * d * d + 12 * n * d),
        name="merge",
        deps=deps,
    )


def units_kernel(a2, g, wg, wu, wd, out):
    gate = dot(a2[...], wg[...])
    up = dot(a2[...], wu[...])
    dh = dot(g[...], wd[...])
    sig = jax.nn.sigmoid(gate)
    act = gate * sig
    out[0] = (act * up).astype(BF16)
    out[1] = (dh * up * sig * (1.0 + gate * (1.0 - sig))).astype(BF16)
    out[2] = (dh * act).astype(BF16)


def units(a2, g, wg, wu, wd, first, count):
    n, d = a2.shape
    const = pl.BlockSpec((n, d), lambda i: (0, 0), pipeline_mode=pl.Buffered(1))
    wspec = pl.BlockSpec((d, FT), lambda i: (0, first + i))
    return launch(
        units_kernel,
        (a2, g, wg, wu, wd),
        grid=(count,),
        in_specs=[const, const, wspec, wspec, wspec],
        out_specs=[pl.BlockSpec((3, n, FT), lambda i: (0, 0, i))],
        out_shape=[jax.ShapeDtypeStruct((3, n, count * FT), BF16)],
        mib=58,
        estimate=cost(10 * n * d * FT * count, 6 * d * FT * count, n * FT * count),
        name=f"units{first}",
    )[0]


def back_kernel(plan, split, *refs):
    acts = refs[: len(plan)]
    weights = refs[len(plan) : -1]
    out = refs[-1]
    total = None
    for act, (w, at) in zip(acts, plan, strict=True):
        term = dot_nt(act[0], weights[w][:, at : at + act.shape[2]])
        total = term if total is None else total + term
    if split:
        out[0] = total.astype(BF16)
    else:
        out[...] = total.astype(BF16)


def back(groups, split, name):
    acts, specs, plan = [], [], []
    for w, (members, _) in enumerate(groups):
        at = 0
        for x, i in members:
            acts.append(x)
            specs.append(
                pl.BlockSpec(
                    (1,) + x.shape[1:], lambda j, i=i: (i, 0, 0), pipeline_mode=pl.Buffered(1)
                )
            )
            plan.append((w, at))
            at += x.shape[2]
    weights = [w for _, w in groups]
    n = acts[0].shape[1]
    d = weights[0].shape[0]
    dt = 256
    per = d // 2 // dt
    if split:
        ospec = pl.BlockSpec((1, n, dt), lambda i: (i // per, 0, i % per))
        oshape = (2, n, d // 2)
    else:
        ospec = pl.BlockSpec((n, dt), lambda i: (0, i))
        oshape = (n, d)
    ktotal = sum(w.shape[1] for w in weights)
    return launch(
        functools.partial(back_kernel, tuple(plan), split),
        (*acts, *weights),
        grid=(d // dt,),
        in_specs=specs + [pl.BlockSpec((dt, w.shape[1]), lambda i: (i, 0)) for w in weights],
        out_specs=[ospec],
        out_shape=[jax.ShapeDtypeStruct(oshape, BF16)],
        mib=58,
        estimate=cost(4 * n * d * ktotal, 2 * d * ktotal + 2 * n * (d + ktotal)),
        name=name,
    )[0]


def stream_kernel(da_own, da_oth, h1, r2, gain, g, w_out, dh1, dattn_t, dout, gsum):
    da = da_own[...].astype(F32) + da_oth[...].astype(F32)
    inv = r2[:, :1]
    norm = jnp.concatenate([h1[j] for j in range(h1.shape[0])], axis=1) * inv
    grad = da * norm

    @pl.when(pl.program_id(0) == 0)
    def _():
        gsum[...] = jnp.zeros_like(gsum)

    gsum[...] += jnp.sum(grad, axis=0, keepdims=True)
    e2 = da * gain[...]
    mean = jnp.sum(e2 * norm, axis=1, keepdims=True) * (1.0 / da.shape[1])
    dh = g[...].astype(F32) + inv * (e2 - norm * mean)
    dh1[...] = dh
    low = dh.astype(BF16)
    dattn_t[...] = low.T
    dout[...] = dot(low, w_out[...]).astype(BF16)


def stream(da_own, da_oth, h1, r2, gain, g, w_out, deps=()):
    parts, n, dt = h1.shape
    d = parts * dt
    tt = min(n, 128)
    ew = w_out.shape[1]
    row = lambda w: pl.BlockSpec((tt, w), lambda i: (i, 0))
    const = lambda a: pl.BlockSpec(a.shape, lambda i: (0, 0), pipeline_mode=pl.Buffered(1))
    return launch(
        stream_kernel,
        (da_own, da_oth, h1, r2, gain, g, w_out),
        grid=(n // tt,),
        in_specs=[
            row(d),
            row(d),
            pl.BlockSpec((parts, tt, dt), lambda i: (0, i, 0)),
            row(PAIR),
            const(gain),
            row(d),
            const(w_out),
        ],
        out_specs=[
            row(d),
            pl.BlockSpec((d, tt), lambda i: (0, i)),
            row(ew),
            pl.BlockSpec((1, d), lambda i: (0, 0)),
        ],
        out_shape=[
            jax.ShapeDtypeStruct((n, d), F32),
            jax.ShapeDtypeStruct((d, n), BF16),
            jax.ShapeDtypeStruct((n, ew), BF16),
            jax.ShapeDtypeStruct((1, d), F32),
        ],
        mib=56,
        estimate=cost(2 * n * d * ew, 2 * d * ew + 20 * n * d),
        name="stream",
        deps=deps,
    )


def entry_kernel(dq, dkv, wq, wk, wv, full, ssx, gain, part, gsum, rsum):
    kvw = wk.shape[1]
    da = dot_nt(dq[...], wq[...])
    da = da + dot_nt(dkv[:, :kvw], wk[...]) + dot_nt(dkv[:, kvw:], wv[...])
    width = pl.num_programs(0) * da.shape[1]
    inv = lax.rsqrt(ssx[:, :1] * (1.0 / width) + EPS)
    grad = da * (full[...].astype(F32) * inv)
    gsum[...] = jnp.sum(grad, axis=0, keepdims=True)

    @pl.when(pl.program_id(0) == 0)
    def _():
        rsum[...] = jnp.zeros_like(rsum)

    rsum[...] += jnp.sum(grad * gain[...], axis=1, keepdims=True)
    part[0] = da.astype(BF16)


def entry(dq, dkv, wq, wk, wv, full, ssx, gain):
    n, d = full.shape
    dt = 256
    per = d // 2 // dt
    const = lambda a: pl.BlockSpec(a.shape, lambda i: (0, 0), pipeline_mode=pl.Buffered(1))
    wspec = lambda w: pl.BlockSpec((dt, w.shape[1]), lambda i: (i, 0))
    return launch(
        entry_kernel,
        (dq, dkv, wq, wk, wv, full, ssx, gain),
        grid=(d // dt,),
        in_specs=[const(dq), const(dkv), wspec(wq), wspec(wk), wspec(wv)]
        + [
            pl.BlockSpec((n, dt), lambda i: (0, i)),
            const(ssx),
            pl.BlockSpec((1, dt), lambda i: (0, i)),
        ],
        out_specs=[
            pl.BlockSpec((1, n, dt), lambda i: (i // per, 0, i % per)),
            pl.BlockSpec((1, dt), lambda i: (0, i)),
            pl.BlockSpec((n, PAIR), lambda i: (0, 0)),
        ],
        out_shape=[
            jax.ShapeDtypeStruct((2, n, d // 2), BF16),
            jax.ShapeDtypeStruct((1, d), F32),
            jax.ShapeDtypeStruct((n, PAIR), F32),
        ],
        mib=56,
        estimate=cost(2 * n * d * (wq.shape[1] + 2 * wk.shape[1]), 20 * n * d),
        name="entry",
    )


def outer_kernel(shares, count, parts, adds, sc, *refs):
    k = 0
    lefts, rights = [], []
    for share in shares:
        lefts.append((refs[k : k + count], refs[k + count : k + 2 * count]))
        k += 2 * count
        rights.append([(refs[k + 2 * i], refs[k + 2 * i + 1]) for i in range(share)])
        k += 2 * share
    got = refs[k] if adds else None
    outs = refs[k + adds :]

    def work(out):
        m = 0
        for (left_own, left_oth), group in zip(lefts, rights, strict=True):
            rows = left_own[0].shape[0]
            for own, oth in group:
                at = slice(m * FT, (m + 1) * FT)
                for i in range(count):
                    part = slice(i * rows, (i + 1) * rows)
                    total = dot(left_own[i][...], own[0]) + dot(left_oth[i][...], oth[0])
                    if adds:
                        total = total + got[part, at].astype(F32)
                    out[part, at] = total.astype(BF16)
                m += 1

    if len(parts) == 1:
        work(outs[0])
        return
    step = pl.program_id(0)
    start = 0
    for out, size in zip(outs, parts, strict=True):
        pl.when((step >= start) & (step < start + size))(functools.partial(work, out))
        start += size


def outer(sc, groups, rows, first, parts, name, got=None, deps=()):
    n = groups[0][0].shape[1]
    count = sc.shape[0]
    number = sum(parts)
    shares = tuple(len(g[2]) for g in groups)
    ins, specs = [], []
    for own, oth, rights in groups:
        ins += [own] * count + [oth] * count
        for i in range(count):
            specs.append(pl.BlockSpec((rows, n), lambda j, s, i=i: (s[i], 0)))
        specs += specs[-count:]
        for r_own, r_oth, at in rights:
            ins += [r_own, r_oth]
            specs += [pl.BlockSpec((1, n, FT), lambda i, s, at=at: (at, 0, first + i))] * 2
    members = sum(shares)
    height = count * rows
    ospecs, start = [], 0
    for size in parts:
        ospecs.append(
            pl.BlockSpec(
                (height, members * FT),
                lambda i, s, start=start, size=size: (0, jnp.clip(i - start, 0, size - 1)),
            )
        )
        start += size
    if got is not None:
        ins.append(got)
        specs.append(ospecs[0])
    c = number * FT
    return launch(
        functools.partial(outer_kernel, shares, count, tuple(parts), int(got is not None)),
        (sc, *ins),
        prefetch=1,
        grid=(number,),
        in_specs=specs,
        out_specs=ospecs,
        out_shape=[jax.ShapeDtypeStruct((height, members * size * FT), BF16) for size in parts],
        mib=48,
        estimate=cost(8 * n * height * c * members, members * c * (4 * n + 2 * height)),
        name=name,
        deps=deps,
    )


def finish_kernel(count, *refs):
    parts = refs[:count]
    outs = refs[count:]
    at = 0
    for part in parts:
        for tile in range(part.shape[2] // (3 * FT)):
            for m in range(3):
                columns = slice((3 * tile + m) * FT, (3 * tile + m + 1) * FT)
                total = part[0, :, columns].astype(F32)
                for b in range(1, part.shape[0]):
                    total = total + part[b, :, columns].astype(F32)
                outs[m][:, at : at + FT] = total
            at += FT


def finish(parts, nblk):
    parts = [x.reshape(nblk, x.shape[0] // nblk, x.shape[1]) for x in parts]
    rows = parts[0].shape[1]
    width = sum(x.shape[2] for x in parts) // 3
    whole = lambda shape: pl.BlockSpec(shape, lambda i: (0,) * len(shape))
    return launch(
        functools.partial(finish_kernel, len(parts)),
        tuple(parts),
        grid=(1,),
        in_specs=[whole(x.shape) for x in parts],
        out_specs=[whole((rows, width))] * 3,
        out_shape=[jax.ShapeDtypeStruct((rows, width), F32)] * 3,
        mib=48,
        estimate=cost(0, 8 * nblk * rows * width),
        name="finish",
    )


def body(
    inputs,
    cotangent,
    lengths,
    attn_gain,
    w_query,
    w_key,
    w_value,
    w_out,
    mlp_gain,
    gate_weight,
    up_weight,
    down_weight,
):
    t, rows, half = inputs.shape
    n = t * rows
    heads = lax.axis_size("head")
    nblk = lax.axis_size("blk")
    ndp = lax.axis_size("dp")
    d = half * heads
    h = lax.axis_index("head").astype(jnp.int32)
    blk = lax.axis_index("blk").astype(jnp.int32)
    dp = lax.axis_index("dp").astype(jnp.int32)
    sc_h = h.reshape(1)
    sc_blk = blk.reshape(1)

    def flat(x):
        return jnp.transpose(x, (1, 0, 2)).reshape(n, x.shape[2])

    def unflat(x):
        return jnp.transpose(x.reshape(rows, t, x.shape[1]), (1, 0, 2))

    x_own = flat(inputs)
    g_own = flat(cotangent)
    gain_one = attn_gain.astype(F32).reshape(1, d)
    gain_two = mlp_gain.astype(F32).reshape(1, d)

    pos = blk * t + jnp.arange(t, dtype=jnp.int32)
    ends = jnp.cumsum(lengths, axis=1)
    passed = ends[:, None, :] <= pos[None, :, None]
    start = jnp.max(jnp.where(passed, ends[:, None, :], 0), axis=2)
    valid = (jnp.sum(passed.astype(jnp.int32), axis=2) < DOCS).astype(F32).reshape(n)
    start_rows = start.reshape(rows, 1, t)
    freq = jnp.power(THETA, -2.0 * jnp.arange(HD // 2, dtype=F32) / HD)
    angles = pos.astype(F32)[:, None] * freq[None, :]
    cos_h, sin_h = jnp.cos(angles), jnp.sin(angles)
    cos = jnp.tile(jnp.concatenate([cos_h, cos_h, cos_h, cos_h], axis=1), (rows, 1))
    sin = jnp.tile(jnp.concatenate([-sin_h, sin_h, -sin_h, sin_h], axis=1), (rows, 1))

    CHAIN.clear()
    WEIGHT[0] = EARLY

    def tie(x, *also):
        return lax.optimization_barrier((x, *also))[0]

    def by_head(x):
        return jnp.where(h == 0, x[:, :half], x[:, half:])

    def gate(x):
        x, CHAIN[0] = lax.optimization_barrier((x, CHAIN[0]))
        return x

    def mate(x):
        return swap(x, "dp", 1)

    x_oth = swap(x_own, "head", 1)
    share = w_out.shape[0] // ndp
    piece = lax.dynamic_slice_in_dim(w_out, dp * share, share, 0)
    x_oth, piece, g_own, cos, sin, start_rows = lax.optimization_barrier(
        (x_oth, piece, g_own, cos, sin, start_rows)
    )
    piece = swap(piece, "head", 1)
    full, a_one, queries, kv, ssx = project(
        sc_h, x_own, x_oth, gain_one, w_query, w_key, w_value, cos, sin
    )

    kvs, state = [kv], ()
    for s in range(nblk):
        if s + 1 < nblk:
            steps = [(i, i + 1) for i in range(s, nblk - 1)]
            kvs.append(lax.ppermute(kvs[s], "blk", steps))
        state = attend(s, s == nblk - 1, sc_blk, queries, kvs[s], start_rows, state, rows)
        if s + 1 < nblk - 1:
            kvs[s + 1] = gate(kvs[s + 1])
        if s == 0:
            a_one_t = flip(a_one, "flip_a")
            piece = gate(piece)
            w_out_oth = lax.all_gather(piece, "dp", axis=0, tiled=True)
            g_own, piece = lax.optimization_barrier((g_own, piece))
            g_oth = swap(g_own, "head", 1)
    acc, ml = state
    o_own = flip(acc)
    o_oth = swap(o_own, "head", 1)
    g_full = jnp.concatenate(
        [jnp.where(h == 0, g_own, g_oth), jnp.where(h == 0, g_oth, g_own)], axis=1
    )
    g_t = flip(g_full, "flip_g")
    o_mate, g_mate = mate(o_own), mate(g_t)
    h_one, a_two, a_two_t, inv_two, ssa = merge(
        o_own, o_oth, w_out, w_out_oth, full, gain_two
    )
    a_two_mate = mate(a_two_t)

    low_bit = dp & 1
    block_rows = d // ndp
    sc_send = (dp ^ 2).reshape(1)
    sc_keep = dp.reshape(1)
    sc_both = jnp.stack([2 * i + low_bit for i in range(ndp // 2)])
    y_groups = [[0, 2], [1, 3]]

    def both_halves(groups, parts, name, deps=()):
        return [
            lax.psum_scatter(
                x, "dp", scatter_dimension=0, axis_index_groups=y_groups, tiled=True
            )
            for x in outer(sc_both, groups, block_rows, 0, parts, name, deps=deps)
        ]

    def over_blk(x):
        return lax.all_to_all(x, "blk", split_axis=0, concat_axis=0, tiled=True)

    tiles = gate_weight.shape[1] // FT
    head_tiles = tiles // 4 + 1
    rest = tiles - head_tiles
    third = (rest + 2) // 3

    def unit_part(first, count):
        x = units(a_two, g_full, gate_weight, up_weight, down_weight, first, count)
        x_mate = mate(x)
        return x, [
            (g_t, g_mate, [(x, x_mate, 0)]),
            (a_two_t, a_two_mate, [(x, x_mate, 1), (x, x_mate, 2)]),
        ]

    part_a, groups_a = unit_part(0, head_tiles)
    (sum0,) = both_halves(groups_a, (head_tiles,), "mlp0")
    part_b, groups_b = unit_part(head_tiles, rest)

    da_own = back(
        [
            ([(part_a, 1), (part_b, 1)], gate_weight),
            ([(part_a, 2), (part_b, 2)], up_weight),
        ],
        False,
        "da_two",
    )
    da_oth = swap(da_own, "head", 1)
    sum1, sum2, sum3 = both_halves(groups_b, (third, third, rest - 2 * third), "mlp1")
    all0 = over_blk(gate(sum0))
    dh_one, d_attn_t, d_out, gain_two_sum = stream(
        da_own, da_oth, h_one, inv_two, gain_two, g_full, w_out
    )
    WEIGHT[0] = LATE
    d_attn_mate, a_one_mate = mate(d_attn_t), mate(gate(a_one_t))
    out_groups = [(d_attn_t, d_attn_mate, [(o_own[None], o_mate[None], 0)])]
    out_parts = (o_own.shape[1] // FT,)
    (first_out,) = outer(
        sc_send, out_groups, block_rows, 0, out_parts, "out_send", deps=(a_one_mate, all0)
    )
    got_out = swap(first_out, "dp", 2)
    all1 = over_blk(gate(sum1))
    branch = back([([(part_a, 0), (part_b, 0)], down_weight)], True, "branch")
    to_other = gate(lax.dynamic_index_in_dim(branch, 1 - h, 0, keepdims=False))
    branch_oth = swap(to_other, "head", 1)

    state, parts = (), []
    for s in reversed(range(nblk)):
        out = attend_back(
            s, s == nblk - 1, s == 0, sc_blk, queries, d_out, o_own, ml, start_rows, cos, sin,
            kvs[s], state, rows, deps=(),
        )
        state = (out[0], out[2] if s == nblk - 1 else state[1])
        part = out[1]
        parts.append(
            lax.ppermute(part, "blk", [(i, i - s) for i in range(s, nblk)]) if s else part
        )
        if s == 1:
            (keep_out,) = outer(
                sc_keep, out_groups, block_rows, 0, out_parts, "out_keep", got_out, deps=(all1,)
            )
            all2 = over_blk(gate(sum2))
            sum_out = lax.psum_scatter(keep_out, "blk", scatter_dimension=0, tiled=True)
    d_q = state[0]
    d_kv_own = gather_dkv(parts, cos, sin, deps=(branch_oth,))
    h_late, d_kv_own = lax.optimization_barrier((h_one, d_kv_own))
    h_half = jnp.concatenate(
        [
            jnp.where(h == 0, h_late[i], h_late[i + h_late.shape[0] // 2])
            for i in range(h_late.shape[0] // 2)
        ],
        axis=1,
    )
    mlp_half = lax.dynamic_index_in_dim(branch, h, 0, keepdims=False).astype(F32) + (
        branch_oth.astype(F32)
    )
    output = unflat((h_half + mlp_half).astype(BF16))
    d_qkv = jnp.concatenate([d_q, d_kv_own], axis=1)
    d_qkv_mate = mate(d_qkv)
    d_part, gain_one_sum, row_sum = entry(
        d_q, d_kv_own, w_query, w_key, w_value, full, ssx, gain_one
    )
    qkv_groups = [(a_one_t, a_one_mate, [(d_qkv[None], d_qkv_mate[None], 0)])]
    (sum_qkv,) = both_halves(qkv_groups, (d_qkv.shape[1] // FT,), "qkv", deps=(sum3,))
    sum3, all2 = lax.optimization_barrier((sum3, all2))
    all3 = over_blk(sum3)
    d_send = lax.dynamic_index_in_dim(d_part, 1 - h, 0, keepdims=False)
    d_send, row_sum, gain_one_sum, CHAIN[0] = lax.optimization_barrier(
        (d_send, row_sum, gain_one_sum, CHAIN[0])
    )
    d_other = swap(d_send, "head", 1)
    row_total = row_sum + swap(row_sum, "head", 1)
    sum_qkv = lax.psum_scatter(sum_qkv, "blk", scatter_dimension=0, tiled=True)
    grad_down, grad_gate, grad_up = finish([all0, all1, all2, all3], nblk)
    sum_out, sum_qkv = sum_out.astype(F32), sum_qkv.astype(F32)
    qw, kvw = w_query.shape[1], w_key.shape[1]

    inv_one = lax.rsqrt(ssx[:, :1] * (1.0 / d) + EPS)
    d_one = lax.dynamic_index_in_dim(d_part, h, 0, keepdims=False).astype(F32) + d_other.astype(F32)
    norm_half = x_own.astype(F32) * inv_one
    grad_input = by_head(tie(dh_one, d_other)) + inv_one * (
        d_one * by_head(gain_one) - norm_half * (row_total[:, :1] * (1.0 / d))
    )

    per_head = 1.0 / heads
    tail = jnp.stack(
        [
            jnp.sum(valid) * per_head,
            jnp.sum(valid * ssx[:, 0]) * per_head,
            jnp.sum(valid * ssa[:, 0]) * per_head,
            jnp.sum(valid[:, None] * mlp_half * mlp_half),
        ]
    )
    small = jnp.concatenate(
        [gain_one_sum[0], gain_two_sum[0] * per_head, tail, jnp.zeros((PAIR - 4,), F32)]
    ).reshape(-1, PAIR)
    for axis in ("head", "dp", "blk"):
        for i in range(lax.axis_size(axis).bit_length() - 1):
            small = small + swap(small, axis, 1 << i)
    small = small.reshape(-1)
    at = (dp * nblk + blk) * (d // (ndp * nblk))
    size = d // (ndp * nblk)
    grad_attn_gain = lax.dynamic_slice_in_dim(small, at, size, 0)
    grad_mlp_gain = lax.dynamic_slice_in_dim(small, d + at, size, 0)
    sums4 = small[2 * d : 2 * d + 4]
    stats = jnp.sqrt(sums4[1:] / (sums4[0] * d))

    return (
        output,
        unflat(grad_input),
        grad_attn_gain,
        sum_qkv[:, :qw],
        sum_qkv[:, qw : qw + kvw],
        sum_qkv[:, qw + kvw :],
        sum_out,
        grad_mlp_gain,
        grad_gate,
        grad_up,
        grad_down,
        stats,
    )


def solution(mesh):
    tokens = P("blk", "dp", "head")
    split = P(None, "head")
    in_specs = (tokens, tokens, P("dp", None), P()) + (split,) * 4 + (P(),) + (split,) * 3
    vec, mat = P(("dp", "blk")), P(("dp", "blk"), "head")
    out_specs = (tokens, tokens, vec, mat, mat, mat, mat, vec, mat, mat, mat, P())
    return jax.shard_map(body, mesh=mesh, in_specs=in_specs, out_specs=out_specs, check_vma=False)
```

time: 1760 us -> 591 us (0.34)
  waiting for transfers between devices: 1120 us -> 256 us
  matrix products: 367 us -> 0 us
  Pallas kernels: 0 us -> 207 us
  blocking collectives: 134 us -> 0 us
  starting transfers between devices: 1.82 us -> 58.5 us
  other arithmetic: 72.9 us -> 19.3 us
    reduce_scatter x11 -> x7, waiting for transfers between devices: 985 us -> 49 us  [the longest x5 49 us: both_halves(): lax.psum_scatter(x, 'dp', scatter_dimension=0, axis_index_groups=y_groups...]
    dot_general x49 -> x0, matrix products: 367 us -> none  [the longest x8 61.3 us: block_scores(): jnp.einsum('qrkgd,srkd->qrkgs', queries, key_four, preferred_element_type...]
    pallas_call x0 -> x26, Pallas kernels: none -> 207 us  [launch(): pl.pallas_call(wrapped, grid_spec=pltpu.PrefetchScalarGridSpec(num_scalar...]
    ppermute x0 -> x28, waiting for transfers between devices: none -> 164 us  [the longest x22 162 us: swap(): return lax.ppermute(x, axis, [(i, i ^ bit) for i in range(n)])]
    all_gather x3 -> x1, waiting for transfers between devices: 70 us -> 0.01 us  [body(): w_out_oth = lax.all_gather(piece, 'dp', axis=0, tiled=True)]
    unnamed x1 -> x0, blocking collectives: 63.1 us -> none
    psum x2 -> x0, waiting for transfers between devices: 62.2 us -> none  [the longest x1 62.2 us: body(): lax.psum(second_part_gradient.astype(jnp.bfloat16), 'head')]
    all_to_all x0 -> x4, waiting for transfers between devices: none -> 41.1 us  [over_blk(): return lax.all_to_all(x, 'blk', split_axis=0, concat_axis=0, tiled=True)]
  transfers between devices with their start and end apart: 16 -> 40, of which waited for: 14 -> 19; matrix products, arithmetic and copies ran while one was open for 8% -> 6% of each run, Pallas kernels for 0% -> 28%
where the time goes in v1:
time: 591 us; the launch traced here: 581 us
  waiting for transfers between devices  256 us (43%)
  Pallas kernels  207 us (35%)
  starting transfers between devices  58.5 us (10%)
  local copies, waits for them, and re-layouts  23.5 us (4%)
  other arithmetic  19.3 us (3%)
  between operations  17.4 us (3%)
    pallas_call x26, Pallas kernels, launch(): pl.pallas_call(wrapped, grid_spec=pltpu.PrefetchScalarGridSpec(num_scalar...  207 us
    ppermute x22, waiting for transfers between devices, swap(): return lax.ppermute(x, axis, [(i, i ^ bit) for i in range(n)])  162 us
    reduce_scatter x5, waiting for transfers between devices, both_halves(): lax.psum_scatter(x, 'dp', scatter_dimension=0, axis_index_groups=y_groups...  49 us
    all_to_all x4, waiting for transfers between devices, over_blk(): return lax.all_to_all(x, 'blk', split_axis=0, concat_axis=0, tiled=True)  41.1 us
    all_to_all x4, starting transfers between devices, over_blk(): return lax.all_to_all(x, 'blk', split_axis=0, concat_axis=0, tiled=True)  25.9 us
    ppermute x22, starting transfers between devices, swap(): return lax.ppermute(x, axis, [(i, i ^ bit) for i in range(n)])  22.3 us
  transfers between devices with their start and end apart: 40, of which 19 were waited for; matrix products, arithmetic and copies ran while one was open for 6% of the time, Pallas kernels for 28%

profile of v1, /device:TPU:0, one launch (start us, length us, event | category | flops | bytes accessed | tf_op | source)
XLA Modules:
  0.0 581.2 jit_solution(7839064822234464658)
XLA Ops:
  15.7 18.0 %collective-permute-done.refs_2_ = bf16[512,1024]{1,0:T(8,128)(2,1)} collective-permute-done((bf16[512,1024]{1,0:T(8,128)(2,1)}, bf16[512,1024]{1,0:T(8,128)(2,1)}, u32[]{:S(2)}, u32[]{:S(2)}) %collective-permute-start) | collective-permute-done | bytes 1048608 | tf_op jit(solution)/shard_map/ppermute | solution.py:89
  48.8 7.6 %attend0.1 = (f32[1024,512]{1,0:T(8,128)S(1)}, f32[8,8,512]{2,1,0:T(8,128)S(1)}, f32[8,128]{1,0:T(8,128)}) custom-call(s32[1]{0:T(128)} %bitcast.refs_0_, bf16[512,1024]{1,0:T(8,128)(2,1)} %get-tuple-element.124.refs_1_, bf16[512,256]{1,0:T(8,128)(2,1)} %get-tuple-element.125.refs_2_.refs_5_, s32[1,1,512]{2,1,0:T(1,128)} %bitcast.79, ...), custom_call_target="tpu_custom_call" | custom-call | flops 2576980480 | bytes 4194304 | tf_op jit(solution)/shard_map/attend0/pallas_call | solution.py:57
  69.7 16.3 %collective-permute-done.6 = bf16[512,1024]{1,0:T(8,128)(2,1)} collective-permute-done((bf16[512,1024]{1,0:T(8,128)(2,1)}, bf16[512,1024]{1,0:T(8,128)(2,1)}, u32[]{:S(2)}, u32[]{:S(2)}) %collective-permute-start.6) | collective-permute-done | bytes 1048608 | tf_op jit(solution)/shard_map/ppermute | solution.py:89
  90.1 15.7 %collective-permute-done.5.refs_1_ = bf16[512,1024]{1,0:T(8,128)(2,1)} collective-permute-done((bf16[512,1024]{1,0:T(8,128)(2,1)}, bf16[512,1024]{1,0:T(8,128)(2,1)}, u32[]{:S(2)}, u32[]{:S(2)}) %collective-permute-start.5) | collective-permute-done | bytes 1048608 | tf_op jit(solution)/shard_map/ppermute | solution.py:89
  105.8 13.1 %merge.1 = (f32[4,512,512]{2,1,0:T(8,128)}, bf16[512,2048]{1,0:T(8,128)(2,1)}, bf16[2048,512]{1,0:T(8,128)(2,1)}, f32[512,128]{1,0:T(8,128)}, f32[512,128]{1,0:T(8,128)}, /*index=5*/f32[8,128]{1,0:T(8,128)}) custom-call(bf16[512,1024]{1,0:T(8,128)(2,1)} %get-tuple-element.147.refs_0_.refs_6_, bf16[512,1024]{1,0:T(8,128)(2,1)} %collective-permute-done.5.refs_1_, ...), custom_call_target="tpu_custom_call" | custom-call | flops 2576980480 | bytes 8388608 | tf_op jit(solution)/shard_map/merge/pallas_call | solution.py:57
  119.0 10.6 %units0.1 = (bf16[3,512,768]{2,1,0:T(8,128)(2,1)}, f32[8,128]{1,0:T(8,128)}) custom-call(bf16[512,2048]{1,0:T(8,128)(2,1)} %get-tuple-element.155.refs_0_, bf16[512,2048]{1,0:T(8,128)(2,1)} %copy-done, bf16[2048,2816]{1,0:T(8,128)(2,1)} %refs_4_.8, bf16[2048,2816]{1,0:T(8,128)(2,1)} %refs_5_.3, bf16[2048,2816]{1,0:T(8,128)(2,1)} %refs_2_.8, ...), custom_call_target="tpu_custom_call" | custom-call | flops 3221225472 | bytes 3774873 | tf_op jit(solution)/shard_map/units0/pallas_call | solution.py:57
  130.2 9.6 %collective-permute-done.7.refs_3_.refs_4_ = bf16[2048,512]{1,0:T(8,128)(2,1)} collective-permute-done((bf16[2048,512]{1,0:T(8,128)(2,1)S(1)}, bf16[2048,512]{1,0:T(8,128)(2,1)}, u32[]{:S(2)}, u32[]{:S(2)}) %collective-permute-start.7) | collective-permute-done | bytes 2097184 | tf_op jit(solution)/shard_map/ppermute | solution.py:89
  140.4 10.2 %mlp0.1 = (bf16[1024,2304]{1,0:T(8,128)(2,1)}, f32[8,128]{1,0:T(8,128)}) custom-call(s32[2]{0:T(128)S(1)} %pad_add_fusion.refs_0_, bf16[2048,512]{1,0:T(8,128)(2,1)} %get-tuple-element.158.refs_1_.refs_2_, bf16[2048,512]{1,0:T(8,128)(2,1)} %get-tuple-element.158.refs_1_.refs_2_, bf16[2048,512]{1,0:T(8,128)(2,1)} %collective-permute-done.7.refs_3_.refs_4_, ...), custom_call_target="tpu_custom_call" | custom-call | flops 3865470464 | bytes 3774873 | tf_op jit(solution)/shard_map/mlp0/pallas_call | solution.py:57
  150.9 21.1 %units3.1 = (bf16[3,512,2048]{2,1,0:T(8,128)(2,1)}, f32[8,128]{1,0:T(8,128)}) custom-call(bf16[512,2048]{1,0:T(8,128)(2,1)} %get-tuple-element.155.refs_0_, bf16[512,2048]{1,0:T(8,128)(2,1)} %copy-done, bf16[2048,2816]{1,0:T(8,128)(2,1)} %refs_4_.8, bf16[2048,2816]{1,0:T(8,128)(2,1)} %refs_5_.3, bf16[2048,2816]{1,0:T(8,128)(2,1)} %refs_2_.8, ...), custom_call_target="tpu_custom_call" | custom-call | flops 8589934592 | bytes 10066329 | tf_op jit(solution)/shard_map/units3/pallas_call | solution.py:57
  171.9 18.9 %da_two.1 = (bf16[512,2048]{1,0:T(8,128)(2,1)}, f32[8,128]{1,0:T(8,128)}) custom-call(bf16[3,512,768]{2,1,0:T(8,128)(2,1)} %get-tuple-element.157.refs_5_.refs_11_.refs_13_.refs_0_.refs_2_, bf16[3,512,2048]{2,1,0:T(8,128)(2,1)} %get-tuple-element.162.refs_1_.refs_3_.refs_5_.refs_11_.refs_13_, ...), custom_call_target="tpu_custom_call" | custom-call | flops 9448928256 | bytes 12373196 | tf_op jit(solution)/shard_map/da_two/pallas_call | solution.py:57
  190.9 21.0 %mlp1.1 = (bf16[1024,2304]{1,0:T(8,128)(2,1)}, bf16[1024,2304]{1,0:T(8,128)(2,1)}, bf16[1024,1536]{1,0:T(8,128)(2,1)}, f32[8,128]{1,0:T(8,128)}) custom-call(s32[2]{0:T(128)S(1)} %pad_add_fusion.refs_0_, bf16[2048,512]{1,0:T(8,128)(2,1)} %get-tuple-element.158.refs_1_.refs_2_, bf16[2048,512]{1,0:T(8,128)(2,1)} %get-tuple-element.158.refs_1_.refs_2_, ...), custom_call_target="tpu_custom_call" | custom-call | flops 10307921920 | bytes 10066329 | tf_op jit(solution)/shard_map/mlp1/pallas_call | solution.py:57
  222.8 38.0 %collective-permute-done.10.refs_1_ = bf16[512,2048]{1,0:T(8,128)(2,1)} collective-permute-done((bf16[512,2048]{1,0:T(8,128)(2,1)}, bf16[512,2048]{1,0:T(8,128)(2,1)}, u32[]{:S(2)}, u32[]{:S(2)}) %collective-permute-start.10) | collective-permute-done | bytes 2097184 | tf_op jit(solution)/shard_map/ppermute | solution.py:89
  260.8 10.3 %stream.1 = (f32[512,2048]{1,0:T(8,128)}, bf16[2048,512]{1,0:T(8,128)(2,1)}, bf16[512,1024]{1,0:T(8,128)(2,1)}, f32[1,2048]{1,0:T(1,128)}, f32[8,128]{1,0:T(8,128)}) custom-call(bf16[512,2048]{1,0:T(8,128)(2,1)} %get-tuple-element.164.refs_0_, bf16[512,2048]{1,0:T(8,128)(2,1)} %collective-permute-done.10.refs_1_, f32[4,512,512]{2,1,0:T(8,128)} %get-tuple-element.203.refs_2_, ...), custom_call_target="tpu_custom_call" | custom-call | flops 858993472 | bytes 10066329 | tf_op jit(solution)/shard_map/stream/pallas_call | solution.py:57
  271.7 8.4 %collective-permute-done.13 = bf16[512,1024]{1,0:T(8,128)(2,1)} collective-permute-done((bf16[512,1024]{1,0:T(8,128)(2,1)}, bf16[512,1024]{1,0:T(8,128)(2,1)}, u32[]{:S(2)}, u32[]{:S(2)}) %collective-permute-start.13) | collective-permute-done | bytes 1048608 | tf_op jit(solution)/shard_map/ppermute | solution.py:89
  286.2 9.9 %all-to-all-start.1 = ((bf16[4,128,2304]{2,1,0:T(8,128)(2,1)}), bf16[4,128,2304]{2,1,0:T(8,128)(2,1)S(1)}, u32[]{:S(2)}, u32[]{:S(2)}) async-start(bf16[4,128,2304]{2,1,0:T(8,128)(2,1)} %bitcast.69), calls=%async_computation.4 | async-start | bytes 4718592 | tf_op jit(solution)/shard_map/all_to_all | solution.py:917
  297.8 12.5 %branch.1 = (bf16[2,512,1024]{2,1,0:T(8,128)(2,1)}, f32[8,128]{1,0:T(8,128)}) custom-call(bf16[3,512,768]{2,1,0:T(8,128)(2,1)} %get-tuple-element.157.refs_5_.refs_11_.refs_13_.refs_0_.refs_2_, bf16[3,512,2048]{2,1,0:T(8,128)(2,1)} %get-tuple-element.162.refs_1_.refs_3_.refs_5_.refs_11_.refs_13_, bf16[2048,2816]{1,0:T(8,128)(2,1)} %refs_2_.8, ...), custom_call_target="tpu_custom_call" | custom-call | flops 4724464128 | bytes 6606028 | tf_op jit(solution)/shard_map/branch/pallas_call | solution.py:57
  327.9 16.7 %collective-permute-done.18.refs_5_ = bf16[512,1024]{1,0:T(8,128)(2,1)} collective-permute-done((bf16[512,1024]{1,0:T(8,128)(2,1)}, bf16[512,1024]{1,0:T(8,128)(2,1)}, u32[]{:S(2)}, u32[]{:S(2)}) %collective-permute-start.18) | collective-permute-done | bytes 1048608 | tf_op jit(solution)/shard_map/ppermute | solution.py:89
  363.0 15.8 %attend_back0.1 = (bf16[512,1024]{1,0:T(8,128)(2,1)}, bf16[512,256]{1,0:T(8,128)(2,1)}, f32[8,128]{1,0:T(8,128)}) custom-call(s32[1]{0:T(128)} %bitcast.refs_0_, bf16[512,1024]{1,0:T(8,128)(2,1)} %get-tuple-element.124.refs_1_, bf16[512,1024]{1,0:T(8,128)(2,1)} %get-tuple-element.170.refs_2_, f32[8,8,512]{2,1,0:T(8,128)} %copy-done.10, ...), custom_call_target="tpu_custom_call" | custom-call | flops 5798205952 | bytes 4194304 | tf_op jit(solution)/shard_map/attend_back0/pallas_call | solution.py:57
  384.5 10.8 %entry.1 = (bf16[2,512,1024]{2,1,0:T(8,128)(2,1)}, f32[1,2048]{1,0:T(1,128)}, f32[512,128]{1,0:T(8,128)}, f32[8,128]{1,0:T(8,128)}) custom-call(bf16[512,1024]{1,0:T(8,128)(2,1)} %get-tuple-element.205.refs_0_, bf16[512,256]{1,0:T(8,128)(2,1)} %get-tuple-element.206.refs_1_, bf16[2048,1024]{1,0:T(8,128)(2,1)} %refs_2_.9, bf16[2048,128]{1,0:T(8,128)(2,1)} %refs_3_.5, ...), custom_call_target="tpu_custom_call" | custom-call | flops 1073741824 | bytes 8388608 | tf_op jit(solution)/shard_map/entry/pallas_call | solution.py:57
  395.3 13.3 %reduce-scatter.14.cloned.1.call-done.refs_8_ = bf16[512,1536]{1,0:T(8,128)(2,1)} async-done(((bf16[1024,1536]{1,0:T(8,128)(2,1)}), bf16[512,1536]{1,0:T(8,128)(2,1)}) %reduce-scatter.14.cloned.1.call-update) | async-done | bytes 1572880 | tf_op jit(solution)/shard_map/reduce_scatter | solution.py:910
  408.6 7.7 %qkv.1 = (bf16[1024,1280]{1,0:T(8,128)(2,1)}, f32[8,128]{1,0:T(8,128)}) custom-call(s32[2]{0:T(128)S(1)} %pad_add_fusion.refs_0_, bf16[2048,512]{1,0:T(8,128)(2,1)} %get-tuple-element.177.refs_1_.refs_2_, bf16[2048,512]{1,0:T(8,128)(2,1)} %get-tuple-element.177.refs_1_.refs_2_, bf16[2048,512]{1,0:T(8,128)(2,1)} %collective-permute-done.14.refs_6_.refs_3_.refs_4_, ...), custom_call_target="tpu_custom_call" | custom-call | flops 2147483648 | bytes 2097152 | tf_op jit(solution)/shard_map/qkv/pallas_call | solution.py:57
  426.7 27.4 %reduce-scatter.16.cloned.1.call-done = bf16[512,1280]{1,0:T(8,128)(2,1)} async-done(((bf16[1024,1280]{1,0:T(8,128)(2,1)}), bf16[512,1280]{1,0:T(8,128)(2,1)}) %reduce-scatter.16.cloned.1.call-update) | async-done | bytes 1310736 | tf_op jit(solution)/shard_map/reduce_scatter | solution.py:910
  456.4 35.2 %all-to-all-done.2 = bf16[4,128,2304]{2,1,0:T(8,128)(2,1)S(1)} async-done(((bf16[4,128,2304]{2,1,0:T(8,128)(2,1)}), bf16[4,128,2304]{2,1,0:T(8,128)(2,1)S(1)}, u32[]{:S(2)}, u32[]{:S(2)}) %all-to-all-start.2) | async-done | bytes 2359328 | tf_op jit(solution)/shard_map/all_to_all | solution.py:917
  514.6 27.2 %collective-permute-done.26 = f32[33,128]{1,0:T(8,128)S(1)} collective-permute-done((f32[33,128]{1,0:T(8,128)S(1)}, f32[33,128]{1,0:T(8,128)S(1)}, u32[]{:S(2)}, u32[]{:S(2)}) %collective-permute-start.26) | collective-permute-done | bytes 16928 | tf_op jit(solution)/shard_map/ppermute | solution.py:89
  (187 shorter events, 168.4 us)
Async XLA Ops:
  7.2 98.6 %all-gather.2.cloned.1.call-start = ((), (), s32[]{:S(2)}) async-start(), calls=%async_computation.11 | async-start | bytes 5242880 | tf_op jit(solution)/shard_map/all_gather | solution.py:885
  7.2 26.5 %collective-permute-start = (bf16[512,1024]{1,0:T(8,128)(2,1)}, bf16[512,1024]{1,0:T(8,128)(2,1)}, u32[]{:S(2)}, u32[]{:S(2)}) collective-permute-start(bf16[512,1024]{1,0:T(8,128)(2,1)} %bitcast.59), channel_id=1, source_target_pairs={{0,1},{1,0},{2,3},{3,2},{4,5},{5,4},{6,7},{7,6},{8,9},{9,8},{10,11... | collective-permute-start | bytes 3145736 | tf_op jit(solution)/shard_map/ppermute | solution.py:89
  33.7 25.0 %collective-permute-start.3 = (bf16[512,1024]{1,0:T(8,128)(2,1)}, bf16[512,1024]{1,0:T(8,128)(2,1)}, u32[]{:S(2)}, u32[]{:S(2)}) collective-permute-start(bf16[512,1024]{1,0:T(8,128)(2,1)} %constant_dynamic-slice_fusion), channel_id=1, source_target_pairs={{0,1},{1,0},{2,3},{3,2},{4,5},{5,4},{6,7},{7,6},{8,9},{9,8},{10,11... | collective-permute-start | bytes 3145736 | tf_op jit(solution)/shard_map/ppermute | solution.py:89
  58.8 157.1 %reduce-scatter.8.cloned.1.call-start = ((), (), s32[]{:S(2)}) async-start(), calls=%async_computation.12 | async-start | bytes 7077888 | tf_op jit(solution)/shard_map/reduce_scatter | solution.py:910
  59.5 26.5 %collective-permute-start.6 = (bf16[512,1024]{1,0:T(8,128)(2,1)}, bf16[512,1024]{1,0:T(8,128)(2,1)}, u32[]{:S(2)}, u32[]{:S(2)}) collective-permute-start(bf16[512,1024]{1,0:T(8,128)(2,1)} %bitcast.71), channel_id=1, source_target_pairs={{0,1},{1,0},{2,3},{3,2},{4,5},{5,4},{6,7},{7,6},{8,9},{9,8},{10,11... | collective-permute-start | bytes 3145736 | tf_op jit(solution)/shard_map/ppermute | solution.py:89
  68.1 37.7 %collective-permute-start.5 = (bf16[512,1024]{1,0:T(8,128)(2,1)}, bf16[512,1024]{1,0:T(8,128)(2,1)}, u32[]{:S(2)}, u32[]{:S(2)}) collective-permute-start(bf16[512,1024]{1,0:T(8,128)(2,1)} %get-tuple-element.147.refs_0_.refs_6_), channel_id=1, source_target_pairs={{0,1},{1,0},{2,3},{3,2},{4,5},{5,4},{6,7},{7,6},{8,9},{9,8},{10,11... | collective-permute-start | bytes 3145736 | tf_op jit(solution)/shard_map/ppermute | solution.py:89
  150.6 135.6 %reduce-scatter.10.cloned.1.call-start = ((), (), s32[]{:S(2)}) async-start(), calls=%async_computation.13 | async-start | bytes 7077888 | tf_op jit(solution)/shard_map/reduce_scatter | solution.py:910
  211.9 151.1 %reduce-scatter.12.cloned.1.call-start = ((), (), s32[]{:S(2)}) async-start(), calls=%async_computation.14 | async-start | bytes 7077888 | tf_op jit(solution)/shard_map/reduce_scatter | solution.py:910
  212.5 48.3 %collective-permute-start.10 = (bf16[512,2048]{1,0:T(8,128)(2,1)}, bf16[512,2048]{1,0:T(8,128)(2,1)}, u32[]{:S(2)}, u32[]{:S(2)}) collective-permute-start(bf16[512,2048]{1,0:T(8,128)(2,1)} %get-tuple-element.164.refs_0_), channel_id=1, source_target_pairs={{0,1},{1,0},{2,3},{3,2},{4,5},{5,4},{6,7},{7,6},{8,9},{9,8},{10,11... | collective-permute-start | bytes 6291464 | tf_op jit(solution)/shard_map/ppermute | solution.py:89
  215.9 64.2 %all-to-all-start = ((bf16[4,128,2304]{2,1,0:T(8,128)(2,1)}), bf16[4,128,2304]{2,1,0:T(8,128)(2,1)S(1)}, u32[]{:S(2)}, u32[]{:S(2)}) async-start(bf16[4,128,2304]{2,1,0:T(8,128)(2,1)} %bitcast.70), calls=%async_computation.2 | async-start | bytes 4718592 | tf_op jit(solution)/shard_map/all_to_all | solution.py:917
  222.8 185.8 %reduce-scatter.14.cloned.1.call-start = ((), (), s32[]{:S(2)}) async-start(), calls=%async_computation.15 | async-start | bytes 4718592 | tf_op jit(solution)/shard_map/reduce_scatter | solution.py:910
  286.2 64.2 %all-to-all-start.1 = ((bf16[4,128,2304]{2,1,0:T(8,128)(2,1)}), bf16[4,128,2304]{2,1,0:T(8,128)(2,1)S(1)}, u32[]{:S(2)}, u32[]{:S(2)}) async-start(bf16[4,128,2304]{2,1,0:T(8,128)(2,1)} %bitcast.69), calls=%async_computation.4 | async-start | bytes 4718592 | tf_op jit(solution)/shard_map/all_to_all | solution.py:917
  296.2 157.9 %reduce-scatter.16.cloned.1.call-start = ((), (), s32[]{:S(2)}) async-start(), calls=%async_computation.16 | async-start | bytes 3932160 | tf_op jit(solution)/shard_map/reduce_scatter | solution.py:910
  296.2 48.4 %collective-permute-start.18 = (bf16[512,1024]{1,0:T(8,128)(2,1)}, bf16[512,1024]{1,0:T(8,128)(2,1)}, u32[]{:S(2)}, u32[]{:S(2)}) collective-permute-start(bf16[512,1024]{1,0:T(8,128)(2,1)} %get-tuple-element.194), channel_id=1, source_target_pairs={{0,16},{8,24},{16,0},{24,8},{1,17},{9,25},{17,1},{25,9},{2,18},{10... | collective-permute-start | bytes 3145736 | tf_op jit(solution)/shard_map/ppermute | solution.py:89
  312.6 68.5 %collective-permute-start.19 = (bf16[512,1024]{1,0:T(8,128)(2,1)}, bf16[512,1024]{1,0:T(8,128)(2,1)}, u32[]{:S(2)}, u32[]{:S(2)}) collective-permute-start(bf16[512,1024]{1,0:T(8,128)(2,1)} %dynamic-slice_bitcast_fusion.1), channel_id=1, source_target_pairs={{0,1},{1,0},{2,3},{3,2},{4,5},{5,4},{6,7},{7,6},{8,9},{9,8},{10,11... | collective-permute-start | bytes 3145736 | tf_op jit(solution)/shard_map/ppermute | solution.py:89
  324.1 54.7 %collective-permute-start.17 = (bf16[512,256]{1,0:T(8,128)(2,1)}, bf16[512,256]{1,0:T(8,128)(2,1)}, u32[]{:S(2)}, u32[]{:S(2)}) collective-permute-start(bf16[512,256]{1,0:T(8,128)(2,1)} %get-tuple-element.191), channel_id=1, source_target_pairs={{2,0},{4,2},{6,4},{3,1},{5,3},{7,5},{10,8},{12,10},{14,12},{11,9},... | collective-permute-start | bytes 786440 | tf_op jit(solution)/shard_map/ppermute | solution.py:972
  325.3 53.4 %collective-permute-start.16 = (bf16[512,256]{1,0:T(8,128)(2,1)}, bf16[512,256]{1,0:T(8,128)(2,1)}, u32[]{:S(2)}, u32[]{:S(2)}) collective-permute-start(bf16[512,256]{1,0:T(8,128)(2,1)} %get-tuple-element.188), channel_id=1, source_target_pairs={{4,0},{6,2},{5,1},{7,3},{12,8},{14,10},{13,9},{15,11},{20,16},{22,... | collective-permute-start | bytes 786440 | tf_op jit(solution)/shard_map/ppermute | solution.py:972
  326.6 54.5 %collective-permute-start.15 = (bf16[512,256]{1,0:T(8,128)(2,1)}, bf16[512,256]{1,0:T(8,128)(2,1)}, u32[]{:S(2)}, u32[]{:S(2)}) collective-permute-start(bf16[512,256]{1,0:T(8,128)(2,1)} %get-tuple-element.184), channel_id=1, source_target_pairs={{6,0},{7,1},{14,8},{15,9},{22,16},{23,17},{30,24},{31,25}} | collective-permute-start | bytes 786440 | tf_op jit(solution)/shard_map/ppermute | solution.py:972
  416.3 75.3 %all-to-all-start.2 = ((bf16[4,128,2304]{2,1,0:T(8,128)(2,1)}), bf16[4,128,2304]{2,1,0:T(8,128)(2,1)S(1)}, u32[]{:S(2)}, u32[]{:S(2)}) async-start(bf16[4,128,2304]{2,1,0:T(8,128)(2,1)} %bitcast.68), calls=%async_computation.9 | async-start | bytes 4718592 | tf_op jit(solution)/shard_map/all_to_all | solution.py:917
  420.9 135.3 %reduce-scatter.20.cloned.1.call-start = ((), (), s32[]{:S(2)}) async-start(), calls=%async_computation.18 | async-start | bytes 1310720 | tf_op jit(solution)/shard_map/reduce_scatter | solution.py:979
  421.7 149.3 %reduce-scatter.18.cloned.1.call-start = ((), (), s32[]{:S(2)}) async-start(), calls=%async_computation.17 | async-start | bytes 1638400 | tf_op jit(solution)/shard_map/reduce_scatter | solution.py:1009
  491.6 73.3 %all-to-all-start.3 = ((bf16[4,128,1536]{2,1,0:T(8,128)(2,1)}), bf16[4,128,1536]{2,1,0:T(8,128)(2,1)}, u32[]{:S(2)}, u32[]{:S(2)}) async-start(bf16[4,128,1536]{2,1,0:T(8,128)(2,1)} %bitcast.66), calls=%async_computation.10 | async-start | bytes 3145728 | tf_op jit(solution)/shard_map/all_to_all | solution.py:917
  507.2 50.9 %collective-permute-start.21 = (bf16[512,1024]{1,0:T(8,128)(2,1)}, bf16[512,1024]{1,0:T(8,128)(2,1)}, u32[]{:S(2)}, u32[]{:S(2)}) collective-permute-start(bf16[512,1024]{1,0:T(8,128)(2,1)} %dynamic-slice_bitcast_fusion), channel_id=1, source_target_pairs={{0,1},{1,0},{2,3},{3,2},{4,5},{5,4},{6,7},{7,6},{8,9},{9,8},{10,11... | collective-permute-start | bytes 3145736 | tf_op jit(solution)/shard_map/ppermute | solution.py:89
  512.4 29.4 %collective-permute-start.26 = (f32[33,128]{1,0:T(8,128)S(1)}, f32[33,128]{1,0:T(8,128)S(1)}, u32[]{:S(2)}, u32[]{:S(2)}) collective-permute-start(f32[33,128]{1,0:T(8,128)S(1)} %add.109), channel_id=1, source_target_pairs={{0,2},{2,0},{4,6},{6,4},{1,3},{3,1},{5,7},{7,5},{8,10},{10,8},{12,... | collective-permute-start | bytes 50696 | tf_op jit(solution)/shard_map/ppermute | solution.py:89
  (44 other events, 612.1 us)
Sparse Core Ops, SparseCore 0:
  58.9 35.2 all-gather.1
  150.7 65.1 reduce-scatter.7
  218.3 59.9 reduce-scatter.9
  280.5 82.4 reduce-scatter.11
  365.2 43.3 reduce-scatter.13
  416.5 37.5 reduce-scatter.15
  457.0 34.8 reduce-scatter.19
  494.2 49.2 reduce-scatter.17

commit v2 on v1

--- a/solution.py
+++ b/solution.py
@@ -22,8 +22,12 @@
 WEIGHT = [EARLY]
 
 
-def params(mib):
-    return pltpu.CompilerParams(vmem_limit_bytes=mib << 20)
+def params(mib, collective=None):
+    if collective is None:
+        return pltpu.CompilerParams(vmem_limit_bytes=mib << 20)
+    return pltpu.CompilerParams(
+        vmem_limit_bytes=mib << 20, collective_id=collective, has_side_effects=True
+    )
 
 
 def cost(flops, byte_count, trans=0):
@@ -41,7 +45,7 @@
     return pltpu.with_memory_space_constraint(x, pltpu.HBM)
 
 
-def launch(kernel, args, *, grid, in_specs, out_specs, out_shape, mib, estimate, name, scratch=(), prefetch=0, deps=(), pin_in=True, pin_out=True):
+def launch(kernel, args, *, grid, in_specs, out_specs, out_shape, mib, estimate, name, scratch=(), prefetch=0, deps=(), pin_in=True, pin_out=True, collective=None):
     extra = list(CHAIN) + list(deps)
     n_in, n_out = len(args), len(out_shape)
 
@@ -64,7 +68,7 @@
             scratch_shapes=list(scratch),
         ),
         out_shape=list(out_shape) + [pltpu.HBM((8, 128), F32)],
-        compiler_params=params(mib),
+        compiler_params=params(mib, collective),
         cost_estimate=estimate,
         name=name,
     )(*args, *extra)
@@ -506,7 +510,7 @@
     out[2] = (dh * act).astype(BF16)
 
 
-def units(a2, g, wg, wu, wd, first, count):
+def units(a2, g, wg, wu, wd, first, count, deps=()):
     n, d = a2.shape
     const = pl.BlockSpec((n, d), lambda i: (0, 0), pipeline_mode=pl.Buffered(1))
     wspec = pl.BlockSpec((d, FT), lambda i: (0, first + i))
@@ -520,63 +524,145 @@
         mib=58,
         estimate=cost(10 * n * d * FT * count, 6 * d * FT * count, n * FT * count),
         name=f"units{first}",
+        deps=deps,
     )[0]
 
 
-def back_kernel(plan, split, *refs):
-    acts = refs[: len(plan)]
-    weights = refs[len(plan) : -1]
-    out = refs[-1]
-    total = None
-    for act, (w, at) in zip(acts, plan, strict=True):
-        term = dot_nt(act[0], weights[w][:, at : at + act.shape[2]])
-        total = term if total is None else total + term
-    if split:
-        out[0] = total.astype(BF16)
-    else:
-        out[...] = total.astype(BF16)
-
-
-def back(groups, split, name):
-    acts, specs, plan = [], [], []
-    for w, (members, _) in enumerate(groups):
-        at = 0
-        for x, i in members:
-            acts.append(x)
-            specs.append(
-                pl.BlockSpec(
-                    (1,) + x.shape[1:], lambda j, i=i: (i, 0, 0), pipeline_mode=pl.Buffered(1)
-                )
+def exchange_kernel(count, tiles, nblk, *refs):
+    acts = refs[: 3 * count]
+    wg, wu, wd, early, total, branch, shares = refs[3 * count : 3 * count + 7]
+    mine, theirs, send_sem, recv_sem, z_send, z_recv, own_sem = refs[3 * count + 7 :]
+    i = pl.program_id(0)
+    other = 1 - lax.axis_index("head")
+    blk = lax.axis_index("blk")
+    rows = early.shape[0] // nblk
+
+    def copy(j):
+        return pltpu.make_async_remote_copy(
+            src_ref=mine.at[j],
+            dst_ref=theirs.at[j],
+            send_sem=send_sem.at[j],
+            recv_sem=recv_sem.at[j],
+            device_id={"head": other},
+            device_id_type=pl.DeviceIdType.MESH,
+        )
+
+    def block(b):
+        return early.at[pl.ds(pl.multiple_of(b * rows, rows), rows), :]
+
+    def share(k):
+        to = lax.rem(blk + k, nblk)
+        return pltpu.make_async_remote_copy(
+            src_ref=block(to),
+            dst_ref=shares.at[blk],
+            send_sem=z_send.at[k],
+            recv_sem=z_recv.at[k],
+            device_id={"blk": to},
+            device_id_type=pl.DeviceIdType.MESH,
+        )
+
+    def keep():
+        return pltpu.make_async_copy(block(blk), shares.at[blk], own_sem)
+
+    def product(m, weight):
+        out, at = None, 0
+        for act in acts[m * count : (m + 1) * count]:
+            term = dot_nt(act[0], weight[:, at : at + act.shape[2]])
+            out = term if out is None else out + term
+            at += act.shape[2]
+        return out
+
+    @pl.when(i == 0)
+    def _():
+        barrier = pltpu.get_barrier_semaphore()
+        pl.semaphore_signal(
+            barrier, inc=1, device_id={"head": other}, device_id_type=pl.DeviceIdType.MESH
+        )
+        for k in range(1, nblk):
+            pl.semaphore_signal(
+                barrier,
+                inc=1,
+                device_id={"blk": lax.rem(blk + k, nblk)},
+                device_id_type=pl.DeviceIdType.MESH,
             )
-            plan.append((w, at))
-            at += x.shape[2]
-    weights = [w for _, w in groups]
-    n = acts[0].shape[1]
-    d = weights[0].shape[0]
+        pl.semaphore_wait(barrier, nblk)
+        for k in range(1, nblk):
+            share(k).start()
+        keep().start()
+
+    @pl.when(i < tiles)
+    def _():
+        mine[i] = (product(1, wg) + product(2, wu)).astype(BF16)
+        copy(i).start()
+
+    @pl.when(i >= tiles)
+    def _():
+        branch[0] = product(0, wd).astype(BF16)
+
+    @pl.when(i == 2 * tiles - 1)
+    def _():
+        width = mine.shape[2]
+        for j in range(tiles):
+            copy(j).wait()
+            total[:, j * width : (j + 1) * width] = mine[j].astype(F32) + theirs[j].astype(F32)
+        for k in range(1, nblk):
+            share(k).wait()
+        keep().wait()
+
+
+def exchange(stacks, wg, wu, wd, early, nblk, name):
+    n = stacks[0].shape[1]
+    d, ff = wg.shape
     dt = 256
-    per = d // 2 // dt
-    if split:
-        ospec = pl.BlockSpec((1, n, dt), lambda i: (i // per, 0, i % per))
-        oshape = (2, n, d // 2)
-    else:
-        ospec = pl.BlockSpec((n, dt), lambda i: (0, i))
-        oshape = (n, d)
-    ktotal = sum(w.shape[1] for w in weights)
+    tiles = d // dt
+    per = tiles // 2
+    acts = [x for _ in range(3) for x in stacks]
+    specs = [
+        pl.BlockSpec((1,) + x.shape[1:], lambda i, m=m: (m, 0, 0), pipeline_mode=pl.Buffered(1))
+        for m in range(3)
+        for x in stacks
+    ]
+    first = pl.BlockSpec((dt, ff), lambda i: (jnp.minimum(i, tiles - 1), 0))
+    second = pl.BlockSpec((dt, ff), lambda i: (jnp.maximum(i - tiles, 0), 0))
+    place_hbm = pl.BlockSpec(memory_space=pltpu.HBM)
+
+    def branch_at(i):
+        j = jnp.maximum(i - tiles, 0)
+        return (j // per, 0, j % per)
+
     return launch(
-        functools.partial(back_kernel, tuple(plan), split),
-        (*acts, *weights),
-        grid=(d // dt,),
-        in_specs=specs + [pl.BlockSpec((dt, w.shape[1]), lambda i: (i, 0)) for w in weights],
-        out_specs=[ospec],
-        out_shape=[jax.ShapeDtypeStruct(oshape, BF16)],
+        functools.partial(exchange_kernel, len(stacks), tiles, nblk),
+        (*acts, wg, wu, wd, early),
+        grid=(2 * tiles,),
+        in_specs=specs + [first, first, second, place_hbm],
+        out_specs=[
+            pl.BlockSpec((n, d), lambda i: (0, 0)),
+            pl.BlockSpec((1, n, dt), branch_at),
+            place_hbm,
+        ],
+        out_shape=[
+            jax.ShapeDtypeStruct((n, d), F32),
+            jax.ShapeDtypeStruct((2, n, d // 2), BF16),
+            jax.ShapeDtypeStruct((nblk, early.shape[0] // nblk, early.shape[1]), BF16),
+        ],
+        scratch=[
+            pltpu.VMEM((tiles, n, dt), BF16),
+            pltpu.VMEM((tiles, n, dt), BF16),
+            pltpu.SemaphoreType.DMA((tiles,)),
+            pltpu.SemaphoreType.DMA((tiles,)),
+            pltpu.SemaphoreType.DMA((nblk,)),
+            pltpu.SemaphoreType.DMA((nblk,)),
+            pltpu.SemaphoreType.DMA,
+        ],
         mib=58,
-        estimate=cost(4 * n * d * ktotal, 2 * d * ktotal + 2 * n * (d + ktotal)),
+        estimate=cost(6 * n * d * ff, 6 * d * ff),
         name=name,
-    )[0]
-
-
-def stream_kernel(da_own, da_oth, h1, r2, gain, g, w_out, dh1, dattn_t, dout, gsum):
-    da = da_own[...].astype(F32) + da_oth[...].astype(F32)
+        collective=1,
+    )
+
+
+def stream_kernel(da_sum, h1, r2, gain, g, w_out, dh1, dattn_t, dout, gsum):
+    da = da_sum[...]
     inv = r2[:, :1]
     norm = jnp.concatenate([h1[j] for j in range(h1.shape[0])], axis=1) * inv
     grad = da * norm
@@ -595,7 +681,7 @@
     dout[...] = dot(low, w_out[...]).astype(BF16)
 
 
-def stream(da_own, da_oth, h1, r2, gain, g, w_out, deps=()):
+def stream(da, h1, r2, gain, g, w_out, deps=()):
     parts, n, dt = h1.shape
     d = parts * dt
     tt = min(n, 128)
@@ -604,10 +690,9 @@
     const = lambda a: pl.BlockSpec(a.shape, lambda i: (0, 0), pipeline_mode=pl.Buffered(1))
     return launch(
         stream_kernel,
-        (da_own, da_oth, h1, r2, gain, g, w_out),
+        (da, h1, r2, gain, g, w_out),
         grid=(n // tt,),
         in_specs=[
-            row(d),
             row(d),
             pl.BlockSpec((parts, tt, dt), lambda i: (0, i, 0)),
             row(PAIR),
@@ -683,7 +768,7 @@
     )
 
 
-def outer_kernel(shares, count, parts, adds, sc, *refs):
+def outer_kernel(shares, count, parts, adds, spread, sc, *refs):
     k = 0
     lefts, rights = [], []
     for share in shares:
@@ -705,7 +790,13 @@
                     total = dot(left_own[i][...], own[0]) + dot(left_oth[i][...], oth[0])
                     if adds:
                         total = total + got[part, at].astype(F32)
-                    out[part, at] = total.astype(BF16)
+                    if spread == 1:
+                        out[part, at] = total.astype(BF16)
+                    else:
+                        size = rows // spread
+                        for b in range(spread):
+                            to = slice((b * count + i) * size, (b * count + i + 1) * size)
+                            out[to, at] = total[b * size : (b + 1) * size, :].astype(BF16)
                 m += 1
 
     if len(parts) == 1:
@@ -718,7 +809,7 @@
         start += size
 
 
-def outer(sc, groups, rows, first, parts, name, got=None, deps=()):
+def outer(sc, groups, rows, first, parts, name, got=None, deps=(), spread=1):
     n = groups[0][0].shape[1]
     count = sc.shape[0]
     number = sum(parts)
@@ -748,7 +839,7 @@
         specs.append(ospecs[0])
     c = number * FT
     return launch(
-        functools.partial(outer_kernel, shares, count, tuple(parts), int(got is not None)),
+        functools.partial(outer_kernel, shares, count, tuple(parts), int(got is not None), spread),
         (sc, *ins),
         prefetch=1,
         grid=(number,),
@@ -777,8 +868,8 @@
             at += FT
 
 
-def finish(parts, nblk):
-    parts = [x.reshape(nblk, x.shape[0] // nblk, x.shape[1]) for x in parts]
+def finish(parts):
+    parts = [x.reshape(count, x.shape[0] // count, x.shape[1]) for x, count in parts]
     rows = parts[0].shape[1]
     width = sum(x.shape[2] for x in parts) // 3
     whole = lambda shape: pl.BlockSpec(shape, lambda i: (0,) * len(shape))
@@ -790,7 +881,7 @@
         out_specs=[whole((rows, width))] * 3,
         out_shape=[jax.ShapeDtypeStruct((rows, width), F32)] * 3,
         mib=48,
-        estimate=cost(0, 8 * nblk * rows * width),
+        estimate=cost(0, 8 * parts[0].shape[0] * rows * width),
         name="finish",
     )
 
@@ -917,46 +1008,40 @@
         return lax.all_to_all(x, "blk", split_axis=0, concat_axis=0, tiled=True)
 
     tiles = gate_weight.shape[1] // FT
-    head_tiles = tiles // 4 + 1
-    rest = tiles - head_tiles
-    third = (rest + 2) // 3
-
-    def unit_part(first, count):
-        x = units(a_two, g_full, gate_weight, up_weight, down_weight, first, count)
+    size_a = max(1, tiles // 5)
+    size_b = (tiles - size_a + 1) // 3
+    size_c = tiles - size_a - size_b
+
+    def unit_part(first, count, deps=()):
+        x = units(a_two, g_full, gate_weight, up_weight, down_weight, first, count, deps)
         x_mate = mate(x)
         return x, [
             (g_t, g_mate, [(x, x_mate, 0)]),
             (a_two_t, a_two_mate, [(x, x_mate, 1), (x, x_mate, 2)]),
         ]
 
-    part_a, groups_a = unit_part(0, head_tiles)
-    (sum0,) = both_halves(groups_a, (head_tiles,), "mlp0")
-    part_b, groups_b = unit_part(head_tiles, rest)
-
-    da_own = back(
-        [
-            ([(part_a, 1), (part_b, 1)], gate_weight),
-            ([(part_a, 2), (part_b, 2)], up_weight),
-        ],
-        False,
-        "da_two",
-    )
-    da_oth = swap(da_own, "head", 1)
-    sum1, sum2, sum3 = both_halves(groups_b, (third, third, rest - 2 * third), "mlp1")
-    all0 = over_blk(gate(sum0))
+    part_a, groups_a = unit_part(0, size_a)
+    (sum0,) = both_halves(groups_a, (size_a,), "mlp0")
+    part_b, groups_b = unit_part(size_a, size_b)
+    part_c, groups_c = unit_part(size_a + size_b, size_c)
+    (sum1,) = both_halves(groups_b, (size_b,), "mlp1")
+
+    da, branch, all0 = exchange(
+        [part_a, part_b, part_c], gate_weight, up_weight, down_weight, sum0, nblk, "exchange"
+    )
+    WEIGHT[0] = LATE
+    sum2, sum3 = both_halves(groups_c, (size_c - size_c // 2, size_c // 2), "mlp2")
+    all1 = over_blk(gate(sum1))
     dh_one, d_attn_t, d_out, gain_two_sum = stream(
-        da_own, da_oth, h_one, inv_two, gain_two, g_full, w_out
-    )
-    WEIGHT[0] = LATE
+        da, h_one, inv_two, gain_two, g_full, w_out
+    )
     d_attn_mate, a_one_mate = mate(d_attn_t), mate(gate(a_one_t))
     out_groups = [(d_attn_t, d_attn_mate, [(o_own[None], o_mate[None], 0)])]
     out_parts = (o_own.shape[1] // FT,)
     (first_out,) = outer(
-        sc_send, out_groups, block_rows, 0, out_parts, "out_send", deps=(a_one_mate, all0)
+        sc_send, out_groups, block_rows, 0, out_parts, "out_send", deps=(a_one_mate,)
     )
     got_out = swap(first_out, "dp", 2)
-    all1 = over_blk(gate(sum1))
-    branch = back([([(part_a, 0), (part_b, 0)], down_weight)], True, "branch")
     to_other = gate(lax.dynamic_index_in_dim(branch, 1 - h, 0, keepdims=False))
     branch_oth = swap(to_other, "head", 1)
 
@@ -971,14 +1056,14 @@
         parts.append(
             lax.ppermute(part, "blk", [(i, i - s) for i in range(s, nblk)]) if s else part
         )
-        if s == 1:
+        if s == min(1, nblk - 1):
             (keep_out,) = outer(
-                sc_keep, out_groups, block_rows, 0, out_parts, "out_keep", got_out, deps=(all1,)
+                sc_keep, out_groups, block_rows, 0, out_parts, "out_keep", got_out,
+                deps=(all1,) + tuple(parts[:2]) * (nblk > 2),
             )
-            all2 = over_blk(gate(sum2))
-            sum_out = lax.psum_scatter(keep_out, "blk", scatter_dimension=0, tiled=True)
     d_q = state[0]
     d_kv_own = gather_dkv(parts, cos, sin, deps=(branch_oth,))
+    all2 = over_blk(gate(sum2))
     h_late, d_kv_own = lax.optimization_barrier((h_one, d_kv_own))
     h_half = jnp.concatenate(
         [
@@ -997,27 +1082,19 @@
         d_q, d_kv_own, w_query, w_key, w_value, full, ssx, gain_one
     )
     qkv_groups = [(a_one_t, a_one_mate, [(d_qkv[None], d_qkv_mate[None], 0)])]
-    (sum_qkv,) = both_halves(qkv_groups, (d_qkv.shape[1] // FT,), "qkv", deps=(sum3,))
-    sum3, all2 = lax.optimization_barrier((sum3, all2))
-    all3 = over_blk(sum3)
+    qkv_parts = (d_qkv.shape[1] // FT,)
+    (first_qkv,) = outer(sc_send, qkv_groups, block_rows, 0, qkv_parts, "qkv_send")
+    got_qkv = swap(first_qkv, "dp", 2)
+    sum3 = lax.psum_scatter(gate(sum3), "blk", scatter_dimension=0, tiled=True)
     d_send = lax.dynamic_index_in_dim(d_part, 1 - h, 0, keepdims=False)
     d_send, row_sum, gain_one_sum, CHAIN[0] = lax.optimization_barrier(
         (d_send, row_sum, gain_one_sum, CHAIN[0])
     )
     d_other = swap(d_send, "head", 1)
     row_total = row_sum + swap(row_sum, "head", 1)
-    sum_qkv = lax.psum_scatter(sum_qkv, "blk", scatter_dimension=0, tiled=True)
-    grad_down, grad_gate, grad_up = finish([all0, all1, all2, all3], nblk)
-    sum_out, sum_qkv = sum_out.astype(F32), sum_qkv.astype(F32)
-    qw, kvw = w_query.shape[1], w_key.shape[1]
-
-    inv_one = lax.rsqrt(ssx[:, :1] * (1.0 / d) + EPS)
-    d_one = lax.dynamic_index_in_dim(d_part, h, 0, keepdims=False).astype(F32) + d_other.astype(F32)
-    norm_half = x_own.astype(F32) * inv_one
-    grad_input = by_head(tie(dh_one, d_other)) + inv_one * (
-        d_one * by_head(gain_one) - norm_half * (row_total[:, :1] * (1.0 / d))
-    )
-
+    (keep_qkv,) = outer(
+        sc_keep, qkv_groups, block_rows, 0, qkv_parts, "qkv_keep", got_qkv, deps=(all2,)
+    )
     per_head = 1.0 / heads
     tail = jnp.stack(
         [
@@ -1030,16 +1107,39 @@
     small = jnp.concatenate(
         [gain_one_sum[0], gain_two_sum[0] * per_head, tail, jnp.zeros((PAIR - 4,), F32)]
     ).reshape(-1, PAIR)
-    for axis in ("head", "dp", "blk"):
+    for axis in ("head", "dp"):
         for i in range(lax.axis_size(axis).bit_length() - 1):
             small = small + swap(small, axis, 1 << i)
     small = small.reshape(-1)
-    at = (dp * nblk + blk) * (d // (ndp * nblk))
-    size = d // (ndp * nblk)
-    grad_attn_gain = lax.dynamic_slice_in_dim(small, at, size, 0)
-    grad_mlp_gain = lax.dynamic_slice_in_dim(small, d + at, size, 0)
-    sums4 = small[2 * d : 2 * d + 4]
-    stats = jnp.sqrt(sums4[1:] / (sums4[0] * d))
+    mine = [
+        lax.dynamic_slice_in_dim(small, at + dp * block_rows, block_rows, 0)[:, None]
+        for at in (0, d)
+    ]
+    sums4 = jnp.broadcast_to(small[None, 2 * d : 2 * d + 4], (block_rows, 4))
+    exact = jnp.concatenate(mine + [sums4], axis=1)
+    coarse = exact.astype(BF16)
+    fine = (exact - coarse.astype(F32)).astype(BF16)
+    extra = jnp.concatenate(
+        [coarse, fine, jnp.zeros((block_rows, PAIR - 12), BF16)], axis=1
+    )
+    all_qkv = over_blk(jnp.concatenate([keep_qkv, extra, keep_out], axis=1))
+    grad_down, grad_gate, grad_up = finish([(all0.reshape(-1, all0.shape[2]), nblk), (all1, nblk), (all2, nblk), (sum3, 1)])
+    own_rows = lambda x: jnp.sum(x.reshape(nblk, -1, x.shape[1]).astype(F32), axis=0)
+    sum_qkv = own_rows(all_qkv)
+    sum_out = sum_qkv[:, sum_qkv.shape[1] - o_own.shape[1] :]
+    qw, kvw = w_query.shape[1], w_key.shape[1]
+
+    inv_one = lax.rsqrt(ssx[:, :1] * (1.0 / d) + EPS)
+    d_one = lax.dynamic_index_in_dim(d_part, h, 0, keepdims=False).astype(F32) + d_other.astype(F32)
+    norm_half = x_own.astype(F32) * inv_one
+    grad_input = by_head(tie(dh_one, d_other)) + inv_one * (
+        d_one * by_head(gain_one) - norm_half * (row_total[:, :1] * (1.0 / d))
+    )
+
+    width = qw + 2 * kvw
+    small = sum_qkv[:, width : width + 6] + sum_qkv[:, width + 6 : width + 12]
+    grad_attn_gain, grad_mlp_gain = small[:, 0], small[:, 1]
+    stats = jnp.sqrt(small[0, 3:6] / (small[0, 2] * d))
 
     return (
         output,
@@ -1047,7 +1147,7 @@
         grad_attn_gain,
         sum_qkv[:, :qw],
         sum_qkv[:, qw : qw + kvw],
-        sum_qkv[:, qw + kvw :],
+        sum_qkv[:, qw + kvw : width],
         sum_out,
         grad_mlp_gain,
         grad_gate,

time: 591 us -> 553 us (0.936)
  waiting for transfers between devices: 256 us -> 179 us
  Pallas kernels: 207 us -> 250 us
  local copies, waits for them, and re-layouts: 23.5 us -> 31.5 us
  starting transfers between devices: 58.5 us -> 50.7 us
    ppermute x22 -> x21, waiting for transfers between devices: 162 us -> 105 us  [swap(): return lax.ppermute(x, axis, [(i, i ^ bit) for i in range(n)])]
    reduce_scatter x5 -> x4, waiting for transfers between devices: 49 us -> 0.02 us  [both_halves(): lax.psum_scatter(x, 'dp', scatter_dimension=0, axis_index_groups=y_groups...]
    pallas_call x26 -> x28, Pallas kernels: 207 us -> 250 us  [launch(): pl.pallas_call(wrapped, grid_spec=pltpu.PrefetchScalarGridSpec(num_scalar...]
    ppermute x3, waiting for transfers between devices: 2.31 us -> 43.9 us  [body(): lax.ppermute(part, 'blk', [(i, i - s) for i in range(s, nblk)])]
    all_to_all x4 -> x3, starting transfers between devices: 25.9 us -> 11.6 us  [over_blk(): return lax.all_to_all(x, 'blk', split_axis=0, concat_axis=0, tiled=True)]
    reduce_scatter x5 -> x4, starting transfers between devices: 0.3 us -> 12 us  [both_halves(): lax.psum_scatter(x, 'dp', scatter_dimension=0, axis_index_groups=y_groups...]
    all_to_all x4 -> x3, waiting for transfers between devices: 41.1 us -> 30.1 us  [over_blk(): return lax.all_to_all(x, 'blk', split_axis=0, concat_axis=0, tiled=True)]
    ppermute x22 -> x21, starting transfers between devices: 22.3 us -> 16.9 us  [swap(): return lax.ppermute(x, axis, [(i, i ^ bit) for i in range(n)])]
  transfers between devices with their start and end apart: 40 -> 36, of which waited for: 19 -> 13; matrix products, arithmetic and copies ran while one was open for 6% -> 6% of each run, Pallas kernels for 28% -> 44%
where the time goes in v2:
time: 553 us; the launch traced here: 547 us
  Pallas kernels  250 us (45%)
  waiting for transfers between devices  179 us (32%)
  starting transfers between devices  50.7 us (9%)
  local copies, waits for them, and re-layouts  31.5 us (6%)
  other arithmetic  17.9 us (3%)
  between operations  17.5 us (3%)
    pallas_call x28, Pallas kernels, launch(): pl.pallas_call(wrapped, grid_spec=pltpu.PrefetchScalarGridSpec(num_scalar...  250 us
    ppermute x21, waiting for transfers between devices, swap(): return lax.ppermute(x, axis, [(i, i ^ bit) for i in range(n)])  105 us
    ppermute x3, waiting for transfers between devices, body(): lax.ppermute(part, 'blk', [(i, i - s) for i in range(s, nblk)])  43.9 us
    all_to_all x3, waiting for transfers between devices, over_blk(): return lax.all_to_all(x, 'blk', split_axis=0, concat_axis=0, tiled=True)  30.1 us
    ppermute x21, starting transfers between devices, swap(): return lax.ppermute(x, axis, [(i, i ^ bit) for i in range(n)])  16.9 us
    unnamed x72, local copies, waits for them, and re-layouts  15.1 us
    reduce_scatter x4, starting transfers between devices, both_halves(): lax.psum_scatter(x, 'dp', scatter_dimension=0, axis_index_groups=y_groups...  12 us
    all_to_all x3, starting transfers between devices, over_blk(): return lax.all_to_all(x, 'blk', split_axis=0, concat_axis=0, tiled=True)  11.6 us
  transfers between devices with their start and end apart: 36, of which 13 were waited for; matrix products, arithmetic and copies ran while one was open for 6% of the time, Pallas kernels for 44%

profile of v2, /device:TPU:0, one launch (start us, length us, event | category | flops | bytes accessed | tf_op | source)
XLA Modules:
  0.0 547.2 jit_solution(8504526360149630157)
XLA Ops:
  15.7 18.0 %collective-permute-done.refs_2_ = bf16[512,1024]{1,0:T(8,128)(2,1)} collective-permute-done((bf16[512,1024]{1,0:T(8,128)(2,1)}, bf16[512,1024]{1,0:T(8,128)(2,1)}, u32[]{:S(2)}, u32[]{:S(2)}) %collective-permute-start) | collective-permute-done | bytes 1048608 | tf_op jit(solution)/shard_map/ppermute | solution.py:93
  37.7 6.9 %project.1 = (bf16[512,2048]{1,0:T(8,128)(2,1)}, bf16[512,2048]{1,0:T(8,128)(2,1)}, bf16[512,1024]{1,0:T(8,128)(2,1)}, bf16[512,256]{1,0:T(8,128)(2,1)}, f32[512,128]{1,0:T(8,128)}, /*index=5*/f32[8,128]{1,0:T(8,128)}) custom-call(s32[1]{0:T(128)} %bitcast.1.refs_0_, bf16[512,1024]{1,0:T(8,128)(2,1)S(1)} %bitcast.62, ...), custom_call_target="tpu_custom_call" | custom-call | flops 1073741824 | bytes 7130316 | tf_op jit(solution)/shard_map/project/pallas_call | solution.py:61
  48.8 7.6 %attend0.1 = (f32[1024,512]{1,0:T(8,128)S(1)}, f32[8,8,512]{2,1,0:T(8,128)S(1)}, f32[8,128]{1,0:T(8,128)}) custom-call(s32[1]{0:T(128)} %bitcast.refs_0_, bf16[512,1024]{1,0:T(8,128)(2,1)} %get-tuple-element.127.refs_1_, bf16[512,256]{1,0:T(8,128)(2,1)} %get-tuple-element.128.refs_2_.refs_5_, s32[1,1,512]{2,1,0:T(1,128)} %bitcast.85, ...), custom_call_target="tpu_custom_call" | custom-call | flops 2576980480 | bytes 4194304 | tf_op jit(solution)/shard_map/attend0/pallas_call | solution.py:61
  69.5 16.4 %collective-permute-done.6 = bf16[512,1024]{1,0:T(8,128)(2,1)} collective-permute-done((bf16[512,1024]{1,0:T(8,128)(2,1)S(1)}, bf16[512,1024]{1,0:T(8,128)(2,1)}, u32[]{:S(2)}, u32[]{:S(2)}) %collective-permute-start.6) | collective-permute-done | bytes 1048608 | tf_op jit(solution)/shard_map/ppermute | solution.py:93
  90.0 15.7 %collective-permute-done.5.refs_1_ = bf16[512,1024]{1,0:T(8,128)(2,1)} collective-permute-done((bf16[512,1024]{1,0:T(8,128)(2,1)}, bf16[512,1024]{1,0:T(8,128)(2,1)}, u32[]{:S(2)}, u32[]{:S(2)}) %collective-permute-start.5) | collective-permute-done | bytes 1048608 | tf_op jit(solution)/shard_map/ppermute | solution.py:93
  105.7 13.1 %merge.1 = (f32[4,512,512]{2,1,0:T(8,128)}, bf16[512,2048]{1,0:T(8,128)(2,1)}, bf16[2048,512]{1,0:T(8,128)(2,1)}, f32[512,128]{1,0:T(8,128)}, f32[512,128]{1,0:T(8,128)}, /*index=5*/f32[8,128]{1,0:T(8,128)}) custom-call(bf16[512,1024]{1,0:T(8,128)(2,1)} %get-tuple-element.150.refs_0_.refs_6_, bf16[512,1024]{1,0:T(8,128)(2,1)} %collective-permute-done.5.refs_1_, ...), custom_call_target="tpu_custom_call" | custom-call | flops 2576980480 | bytes 8388608 | tf_op jit(solution)/shard_map/merge/pallas_call | solution.py:61
  118.9 8.2 %units0.1 = (bf16[3,512,512]{2,1,0:T(8,128)(2,1)}, f32[8,128]{1,0:T(8,128)}) custom-call(bf16[512,2048]{1,0:T(8,128)(2,1)} %get-tuple-element.158.refs_0_, bf16[512,2048]{1,0:T(8,128)(2,1)} %copy-done, bf16[2048,2816]{1,0:T(8,128)(2,1)} %refs_9_.1, bf16[2048,2816]{1,0:T(8,128)(2,1)} %refs_10_.1, bf16[2048,2816]{1,0:T(8,128)(2,1)} %refs_11_.1, ...), custom_call_target="tpu_custom_call" | custom-call | flops 2147483648 | bytes 2516582 | tf_op jit(solution)/shard_map/units0/pallas_call | solution.py:61
  132.2 8.3 %mlp0.1 = (bf16[1024,1536]{1,0:T(8,128)(2,1)}, f32[8,128]{1,0:T(8,128)}) custom-call(s32[2]{0:T(128)S(1)} %pad_add_fusion.refs_0_, bf16[2048,512]{1,0:T(8,128)(2,1)} %get-tuple-element.161.refs_1_.refs_2_, bf16[2048,512]{1,0:T(8,128)(2,1)} %get-tuple-element.161.refs_1_.refs_2_, bf16[2048,512]{1,0:T(8,128)(2,1)} %collective-permute-done.7.refs_3_.refs_4_, ...), custom_call_target="tpu_custom_call" | custom-call | flops 2576980480 | bytes 2516582 | tf_op jit(solution)/shard_map/mlp0/pallas_call | solution.py:61
  140.5 11.8 %reduce-scatter.8.cloned.1.call-start = ((), (), s32[]{:S(2)}) async-start(), calls=%async_computation.10 | async-start | bytes 7077888 | tf_op jit(solution)/shard_map/reduce_scatter | solution.py:1001
  152.4 10.5 %units2.1 = (bf16[3,512,768]{2,1,0:T(8,128)(2,1)}, f32[8,128]{1,0:T(8,128)}) custom-call(bf16[512,2048]{1,0:T(8,128)(2,1)} %get-tuple-element.158.refs_0_, bf16[512,2048]{1,0:T(8,128)(2,1)} %copy-done, bf16[2048,2816]{1,0:T(8,128)(2,1)} %refs_9_.1, bf16[2048,2816]{1,0:T(8,128)(2,1)} %refs_10_.1, bf16[2048,2816]{1,0:T(8,128)(2,1)} %refs_11_.1, ...), custom_call_target="tpu_custom_call" | custom-call | flops 3221225472 | bytes 3774873 | tf_op jit(solution)/shard_map/units2/pallas_call | solution.py:61
  163.2 16.5 %units5.1 = (bf16[3,512,1536]{2,1,0:T(8,128)(2,1)}, f32[8,128]{1,0:T(8,128)}) custom-call(bf16[512,2048]{1,0:T(8,128)(2,1)} %get-tuple-element.158.refs_0_, bf16[512,2048]{1,0:T(8,128)(2,1)} %copy-done, bf16[2048,2816]{1,0:T(8,128)(2,1)} %refs_9_.1, bf16[2048,2816]{1,0:T(8,128)(2,1)} %refs_10_.1, bf16[2048,2816]{1,0:T(8,128)(2,1)} %refs_11_.1, ...), custom_call_target="tpu_custom_call" | custom-call | flops 6442450944 | bytes 7549747 | tf_op jit(solution)/shard_map/units5/pallas_call | solution.py:61
  181.2 10.2 %mlp1.1 = (bf16[1024,2304]{1,0:T(8,128)(2,1)}, f32[8,128]{1,0:T(8,128)}) custom-call(s32[2]{0:T(128)S(1)} %pad_add_fusion.refs_0_, bf16[2048,512]{1,0:T(8,128)(2,1)} %get-tuple-element.161.refs_1_.refs_2_, bf16[2048,512]{1,0:T(8,128)(2,1)} %get-tuple-element.161.refs_1_.refs_2_, bf16[2048,512]{1,0:T(8,128)(2,1)} %collective-permute-done.7.refs_3_.refs_4_, ...), custom_call_target="tpu_custom_call" | custom-call | flops 3865470464 | bytes 3774873 | tf_op jit(solution)/shard_map/mlp1/pallas_call | solution.py:61
  191.6 63.8 %exchange.1 = (f32[512,2048]{1,0:T(8,128)}, bf16[2,512,1024]{2,1,0:T(8,128)(2,1)}, bf16[4,128,1536]{2,1,0:T(8,128)(2,1)}, f32[8,128]{1,0:T(8,128)}) custom-call(bf16[3,512,512]{2,1,0:T(8,128)(2,1)} %get-tuple-element.160.refs_5_.refs_11_.refs_13_.refs_0_.refs_3_.refs_6_, ...), custom_call_target="tpu_custom_call" | custom-call | flops 7086695936 | bytes 13841203 | tf_op jit(solution)/shard_map/exchange/pallas_call | solution.py:61
  255.4 16.5 %mlp2.1 = (bf16[1024,2304]{1,0:T(8,128)(2,1)}, bf16[1024,2304]{1,0:T(8,128)(2,1)}, f32[8,128]{1,0:T(8,128)}) custom-call(s32[2]{0:T(128)S(1)} %pad_add_fusion.refs_0_, bf16[2048,512]{1,0:T(8,128)(2,1)} %get-tuple-element.161.refs_1_.refs_2_, bf16[2048,512]{1,0:T(8,128)(2,1)} %get-tuple-element.161.refs_1_.refs_2_, ...), custom_call_target="tpu_custom_call" | custom-call | flops 7730940928 | bytes 7549747 | tf_op jit(solution)/shard_map/mlp2/pallas_call | solution.py:61
  272.6 10.4 %stream.1 = (f32[512,2048]{1,0:T(8,128)}, bf16[2048,512]{1,0:T(8,128)(2,1)}, bf16[512,1024]{1,0:T(8,128)(2,1)}, f32[1,2048]{1,0:T(1,128)}, f32[8,128]{1,0:T(8,128)}) custom-call(f32[512,2048]{1,0:T(8,128)} %get-tuple-element.171.refs_0_, f32[4,512,512]{2,1,0:T(8,128)} %get-tuple-element.204.refs_1_, f32[512,128]{1,0:T(8,128)} %get-tuple-element.172.refs_2_, ...), custom_call_target="tpu_custom_call" | custom-call | flops 858993472 | bytes 10066329 | tf_op jit(solution)/shard_map/stream/pallas_call | solution.py:61
  315.6 20.2 %collective-permute-done.15.refs_8_.refs_0_ = bf16[512,256]{1,0:T(8,128)(2,1)S(1)} collective-permute-done((bf16[512,256]{1,0:T(8,128)(2,1)}, bf16[512,256]{1,0:T(8,128)(2,1)S(1)}, u32[]{:S(2)}, u32[]{:S(2)}) %collective-permute-start.15) | collective-permute-done | bytes 262176 | tf_op jit(solution)/shard_map/ppermute | solution.py:1057
  335.8 23.6 %collective-permute-done.16.refs_9_.refs_1_ = bf16[512,256]{1,0:T(8,128)(2,1)S(1)} collective-permute-done((bf16[512,256]{1,0:T(8,128)(2,1)}, bf16[512,256]{1,0:T(8,128)(2,1)S(1)}, u32[]{:S(2)}, u32[]{:S(2)}) %collective-permute-start.16) | collective-permute-done | bytes 262176 | tf_op jit(solution)/shard_map/ppermute | solution.py:1057
  366.6 15.8 %attend_back0.1 = (bf16[512,1024]{1,0:T(8,128)(2,1)}, bf16[512,256]{1,0:T(8,128)(2,1)}, f32[8,128]{1,0:T(8,128)}) custom-call(s32[1]{0:T(128)} %bitcast.refs_0_, bf16[512,1024]{1,0:T(8,128)(2,1)} %get-tuple-element.127.refs_1_, bf16[512,1024]{1,0:T(8,128)(2,1)} %get-tuple-element.177.refs_2_, f32[8,8,512]{2,1,0:T(8,128)} %copy-done.11, ...), custom_call_target="tpu_custom_call" | custom-call | flops 5798205952 | bytes 4194304 | tf_op jit(solution)/shard_map/attend_back0/pallas_call | solution.py:61
  401.0 10.5 %entry.1 = (bf16[2,512,1024]{2,1,0:T(8,128)(2,1)}, f32[1,2048]{1,0:T(1,128)}, f32[512,128]{1,0:T(8,128)}, f32[8,128]{1,0:T(8,128)}) custom-call(bf16[512,1024]{1,0:T(8,128)(2,1)} %get-tuple-element.206.refs_0_, bf16[512,256]{1,0:T(8,128)(2,1)} %get-tuple-element.207.refs_1_, bf16[2048,1024]{1,0:T(8,128)(2,1)} %refs_2_.9, bf16[2048,128]{1,0:T(8,128)(2,1)} %refs_3_.7, ...), custom_call_target="tpu_custom_call" | custom-call | flops 1073741824 | bytes 8388608 | tf_op jit(solution)/shard_map/entry/pallas_call | solution.py:61
  426.2 23.0 %collective-permute-done.26 = f32[33,128]{1,0:T(8,128)S(1)} collective-permute-done((f32[33,128]{1,0:T(8,128)S(1)}, f32[33,128]{1,0:T(8,128)S(1)}, u32[]{:S(2)}, u32[]{:S(2)}) %collective-permute-start.26) | collective-permute-done | bytes 16928 | tf_op jit(solution)/shard_map/ppermute | solution.py:93
  450.5 17.2 %all-to-all-done.1.refs_2_ = bf16[4,128,2304]{2,1,0:T(8,128)(2,1)S(1)} async-done(((bf16[4,128,2304]{2,1,0:T(8,128)(2,1)}), bf16[4,128,2304]{2,1,0:T(8,128)(2,1)S(1)}, u32[]{:S(2)}, u32[]{:S(2)}) %all-to-all-start.1) | async-done | bytes 2359328 | tf_op jit(solution)/shard_map/all_to_all | solution.py:1008
  469.2 6.2 %qkv_keep.1 = (bf16[512,1280]{1,0:T(8,128)(2,1)}, f32[8,128]{1,0:T(8,128)}) custom-call(s32[1]{0:T(128)} %bitcast.15.refs_0_, bf16[2048,512]{1,0:T(8,128)(2,1)} %get-tuple-element.184.refs_1_, bf16[2048,512]{1,0:T(8,128)(2,1)} %collective-permute-done.14.refs_6_.refs_2_, bf16[1,512,1280]{2,1,0:T(8,128)(2,1)} %bitcast.23.refs_3_, ...), custom_call_target="tpu_custom_call" | custom-call | flops 1073741824 | bytes 1572864 | tf_op jit(solution)/shard_map/qkv_keep/pallas_call | solution.py:61
  486.4 22.9 %collective-permute-done.22 = f32[512,128]{1,0:T(8,128)S(1)} collective-permute-done((f32[512,128]{1,0:T(8,128)}, f32[512,128]{1,0:T(8,128)S(1)}, u32[]{:S(2)}, u32[]{:S(2)}) %collective-permute-start.22) | collective-permute-done | bytes 262176 | tf_op jit(solution)/shard_map/ppermute | solution.py:93
  522.5 12.9 %all-to-all-done.2 = bf16[4,128,2432]{2,1,0:T(8,128)(2,1)S(1)} async-done(((bf16[4,128,2432]{2,1,0:T(8,128)(2,1)}), bf16[4,128,2432]{2,1,0:T(8,128)(2,1)S(1)}, u32[]{:S(2)}, u32[]{:S(2)}) %all-to-all-start.2) | async-done | bytes 2490400 | tf_op jit(solution)/shard_map/all_to_all | solution.py:1008
  (201 shorter events, 143.4 us)
Async XLA Ops:
  7.2 98.5 %all-gather.2.cloned.1.call-start = ((), (), s32[]{:S(2)}) async-start(), calls=%async_computation.8 | async-start | bytes 5242880 | tf_op jit(solution)/shard_map/all_gather | solution.py:976
  7.2 26.5 %collective-permute-start = (bf16[512,1024]{1,0:T(8,128)(2,1)}, bf16[512,1024]{1,0:T(8,128)(2,1)}, u32[]{:S(2)}, u32[]{:S(2)}) collective-permute-start(bf16[512,1024]{1,0:T(8,128)(2,1)} %bitcast.61), channel_id=1, source_target_pairs={{0,1},{1,0},{2,3},{3,2},{4,5},{5,4},{6,7},{7,6},{8,9},{9,8},{10,11... | collective-permute-start | bytes 3145736 | tf_op jit(solution)/shard_map/ppermute | solution.py:93
  33.7 25.1 %collective-permute-start.3 = (bf16[512,1024]{1,0:T(8,128)(2,1)}, bf16[512,1024]{1,0:T(8,128)(2,1)}, u32[]{:S(2)}, u32[]{:S(2)}) collective-permute-start(bf16[512,1024]{1,0:T(8,128)(2,1)} %constant_dynamic-slice_fusion), channel_id=1, source_target_pairs={{0,1},{1,0},{2,3},{3,2},{4,5},{5,4},{6,7},{7,6},{8,9},{9,8},{10,11... | collective-permute-start | bytes 3145736 | tf_op jit(solution)/shard_map/ppermute | solution.py:93
  58.8 132.8 %reduce-scatter.6.cloned.1.call-start = ((), (), s32[]{:S(2)}) async-start(), calls=%async_computation.9 | async-start | bytes 4718592 | tf_op jit(solution)/shard_map/reduce_scatter | solution.py:1001
  59.6 26.3 %collective-permute-start.6 = (bf16[512,1024]{1,0:T(8,128)(2,1)S(1)}, bf16[512,1024]{1,0:T(8,128)(2,1)}, u32[]{:S(2)}, u32[]{:S(2)}) collective-permute-start(bf16[512,1024]{1,0:T(8,128)(2,1)S(1)} %bitcast.72), channel_id=1, source_target_pairs={{0,1},{1,0},{2,3},{3,2},{4,5},{5,4},{6,7},{7,6},{8,9},{9,8},{10,11... | collective-permute-start | bytes 3145736 | tf_op jit(solution)/shard_map/ppermute | solution.py:93
  67.9 37.8 %collective-permute-start.5 = (bf16[512,1024]{1,0:T(8,128)(2,1)}, bf16[512,1024]{1,0:T(8,128)(2,1)}, u32[]{:S(2)}, u32[]{:S(2)}) collective-permute-start(bf16[512,1024]{1,0:T(8,128)(2,1)} %get-tuple-element.150.refs_0_.refs_6_), channel_id=1, source_target_pairs={{0,1},{1,0},{2,3},{3,2},{4,5},{5,4},{6,7},{7,6},{8,9},{9,8},{10,11... | collective-permute-start | bytes 3145736 | tf_op jit(solution)/shard_map/ppermute | solution.py:93
  90.0 37.6 %collective-permute-start.7 = (bf16[2048,512]{1,0:T(8,128)(2,1)}, bf16[2048,512]{1,0:T(8,128)(2,1)}, u32[]{:S(2)}, u32[]{:S(2)}) collective-permute-start(bf16[2048,512]{1,0:T(8,128)(2,1)} %get-tuple-element.161.refs_1_.refs_2_), channel_id=1, source_target_pairs={{0,8},{8,0},{16,24},{24,16},{1,9},{9,1},{17,25},{25,17},{2,10},{10... | collective-permute-start | bytes 6291464 | tf_op jit(solution)/shard_map/ppermute | solution.py:93
  140.5 132.0 %reduce-scatter.8.cloned.1.call-start = ((), (), s32[]{:S(2)}) async-start(), calls=%async_computation.10 | async-start | bytes 7077888 | tf_op jit(solution)/shard_map/reduce_scatter | solution.py:1001
  191.4 194.4 %reduce-scatter.10.cloned.1.call-start = ((), (), s32[]{:S(2)}) async-start(), calls=%async_computation.11 | async-start | bytes 7077888 | tf_op jit(solution)/shard_map/reduce_scatter | solution.py:1001
  191.4 64.0 %collective-permute-start.11 = (bf16[3,512,1536]{2,1,0:T(8,128)(2,1)}, bf16[3,512,1536]{2,1,0:T(8,128)(2,1)}, u32[]{:S(2)}, u32[]{:S(2)}) collective-permute-start(bf16[3,512,1536]{2,1,0:T(8,128)(2,1)} %get-tuple-element.167.refs_2_.refs_5_.refs_8_.refs_11_.refs_13_), channel_id=1, source_target_pairs={{0,8},{8,0},{16,24},{24,16},{1,9},{9,1},{17,25},{25,17},{2,10},{10... | collective-permute-start | bytes 14155784 | tf_op jit(solution)/shard_map/ppermute | solution.py:93
  272.0 148.1 %reduce-scatter.12.cloned.1.call-start = ((), (), s32[]{:S(2)}) async-start(), calls=%async_computation.12 | async-start | bytes 7077888 | tf_op jit(solution)/shard_map/reduce_scatter | solution.py:1001
  283.6 76.6 %all-to-all-start = ((bf16[4,128,2304]{2,1,0:T(8,128)(2,1)}), bf16[4,128,2304]{2,1,0:T(8,128)(2,1)S(1)}, u32[]{:S(2)}, u32[]{:S(2)}) async-start(bf16[4,128,2304]{2,1,0:T(8,128)(2,1)} %bitcast.71), calls=%async_computation.2 | async-start | bytes 4718592 | tf_op jit(solution)/shard_map/all_to_all | solution.py:1008
  296.8 85.6 %collective-permute-start.19 = (bf16[512,1024]{1,0:T(8,128)(2,1)}, bf16[512,1024]{1,0:T(8,128)(2,1)S(1)}, u32[]{:S(2)}, u32[]{:S(2)}) collective-permute-start(bf16[512,1024]{1,0:T(8,128)(2,1)} %dynamic-slice_bitcast_fusion.1), channel_id=1, source_target_pairs={{0,1},{1,0},{2,3},{3,2},{4,5},{5,4},{6,7},{7,6},{8,9},{9,8},{10,11... | collective-permute-start | bytes 3145736 | tf_op jit(solution)/shard_map/ppermute | solution.py:93
  302.4 33.4 %collective-permute-start.15 = (bf16[512,256]{1,0:T(8,128)(2,1)}, bf16[512,256]{1,0:T(8,128)(2,1)S(1)}, u32[]{:S(2)}, u32[]{:S(2)}) collective-permute-start(bf16[512,256]{1,0:T(8,128)(2,1)} %get-tuple-element.187), channel_id=1, source_target_pairs={{6,0},{7,1},{14,8},{15,9},{22,16},{23,17},{30,24},{31,25}} | collective-permute-start | bytes 786440 | tf_op jit(solution)/shard_map/ppermute | solution.py:1057
  304.1 56.1 %collective-permute-start.18 = (bf16[512,1024]{1,0:T(8,128)(2,1)S(1)}, bf16[512,1024]{1,0:T(8,128)(2,1)}, u32[]{:S(2)}, u32[]{:S(2)}) collective-permute-start(bf16[512,1024]{1,0:T(8,128)(2,1)S(1)} %copy-done.32), channel_id=1, source_target_pairs={{0,16},{8,24},{16,0},{24,8},{1,17},{9,25},{17,1},{25,9},{2,18},{10... | collective-permute-start | bytes 3145736 | tf_op jit(solution)/shard_map/ppermute | solution.py:93
  309.1 50.4 %collective-permute-start.16 = (bf16[512,256]{1,0:T(8,128)(2,1)}, bf16[512,256]{1,0:T(8,128)(2,1)S(1)}, u32[]{:S(2)}, u32[]{:S(2)}) collective-permute-start(bf16[512,256]{1,0:T(8,128)(2,1)} %get-tuple-element.191), channel_id=1, source_target_pairs={{4,0},{6,2},{5,1},{7,3},{12,8},{14,10},{13,9},{15,11},{20,16},{22,... | collective-permute-start | bytes 786440 | tf_op jit(solution)/shard_map/ppermute | solution.py:1057
  314.1 68.3 %collective-permute-start.17 = (bf16[512,256]{1,0:T(8,128)(2,1)}, bf16[512,256]{1,0:T(8,128)(2,1)}, u32[]{:S(2)}, u32[]{:S(2)}) collective-permute-start(bf16[512,256]{1,0:T(8,128)(2,1)} %get-tuple-element.194), channel_id=1, source_target_pairs={{2,0},{4,2},{6,4},{3,1},{5,3},{7,5},{10,8},{12,10},{14,12},{11,9},... | collective-permute-start | bytes 786440 | tf_op jit(solution)/shard_map/ppermute | solution.py:1057
  385.8 81.9 %all-to-all-start.1 = ((bf16[4,128,2304]{2,1,0:T(8,128)(2,1)}), bf16[4,128,2304]{2,1,0:T(8,128)(2,1)S(1)}, u32[]{:S(2)}, u32[]{:S(2)}) async-start(bf16[4,128,2304]{2,1,0:T(8,128)(2,1)} %bitcast.70), calls=%async_computation.5 | async-start | bytes 4718592 | tf_op jit(solution)/shard_map/all_to_all | solution.py:1008
  389.5 127.7 %reduce-scatter.14.cloned.1.call-start = ((), (), s32[]{:S(2)}) async-start(), calls=%async_computation.13 | async-start | bytes 2949120 | tf_op jit(solution)/shard_map/reduce_scatter | solution.py:1088
  417.4 33.1 %collective-permute-start.23 = (bf16[512,1280]{1,0:T(8,128)(2,1)}, bf16[512,1280]{1,0:T(8,128)(2,1)}, u32[]{:S(2)}, u32[]{:S(2)}) collective-permute-start(bf16[512,1280]{1,0:T(8,128)(2,1)} %get-tuple-element.222), channel_id=1, source_target_pairs={{0,16},{8,24},{16,0},{24,8},{1,17},{9,25},{17,1},{25,9},{2,18},{10... | collective-permute-start | bytes 3932168 | tf_op jit(solution)/shard_map/ppermute | solution.py:93
  425.8 23.4 %collective-permute-start.26 = (f32[33,128]{1,0:T(8,128)S(1)}, f32[33,128]{1,0:T(8,128)S(1)}, u32[]{:S(2)}, u32[]{:S(2)}) collective-permute-start(f32[33,128]{1,0:T(8,128)S(1)} %fusion.23), channel_id=1, source_target_pairs={{0,16},{8,24},{16,0},{24,8},{1,17},{9,25},{17,1},{25,9},{2,18},{10... | collective-permute-start | bytes 50696 | tf_op jit(solution)/shard_map/ppermute | solution.py:93
  480.3 55.1 %all-to-all-start.2 = ((bf16[4,128,2432]{2,1,0:T(8,128)(2,1)}), bf16[4,128,2432]{2,1,0:T(8,128)(2,1)S(1)}, u32[]{:S(2)}, u32[]{:S(2)}) async-start(bf16[4,128,2432]{2,1,0:T(8,128)(2,1)} %bitcast.40), calls=%async_computation.6 | async-start | bytes 4980736 | tf_op jit(solution)/shard_map/all_to_all | solution.py:1008
  484.3 26.2 %collective-permute-start.21 = (bf16[512,1024]{1,0:T(8,128)(2,1)}, bf16[512,1024]{1,0:T(8,128)(2,1)S(1)}, u32[]{:S(2)}, u32[]{:S(2)}) collective-permute-start(bf16[512,1024]{1,0:T(8,128)(2,1)} %dynamic-slice_bitcast_fusion), channel_id=1, source_target_pairs={{0,1},{1,0},{2,3},{3,2},{4,5},{5,4},{6,7},{7,6},{8,9},{9,8},{10,11... | collective-permute-start | bytes 3145736 | tf_op jit(solution)/shard_map/ppermute | solution.py:93
  486.2 23.1 %collective-permute-start.22 = (f32[512,128]{1,0:T(8,128)}, f32[512,128]{1,0:T(8,128)S(1)}, u32[]{:S(2)}, u32[]{:S(2)}) collective-permute-start(f32[512,128]{1,0:T(8,128)} %get-tuple-element.221), channel_id=1, source_target_pairs={{0,1},{1,0},{2,3},{3,2},{4,5},{5,4},{6,7},{7,6},{8,9},{9,8},{10,11... | collective-permute-start | bytes 786440 | tf_op jit(solution)/shard_map/ppermute | solution.py:93
  (47 other events, 427.6 us)
Sparse Core Ops, SparseCore 0:
  58.9 35.5 all-gather.1
  140.7 48.2 reduce-scatter.5
  191.5 64.8 reduce-scatter.7
  272.1 80.5 reduce-scatter.9
  354.9 59.3 reduce-scatter.11
  424.7 56.9 reduce-scatter.13

commit v3 on v2

--- a/solution.py
+++ b/solution.py
@@ -1059,23 +1059,11 @@
         if s == min(1, nblk - 1):
             (keep_out,) = outer(
                 sc_keep, out_groups, block_rows, 0, out_parts, "out_keep", got_out,
-                deps=(all1,) + tuple(parts[:2]) * (nblk > 2),
+                deps=(all1,) + tuple(parts[: nblk - 1]),
             )
+            all2 = over_blk(gate(sum2))
     d_q = state[0]
-    d_kv_own = gather_dkv(parts, cos, sin, deps=(branch_oth,))
-    all2 = over_blk(gate(sum2))
-    h_late, d_kv_own = lax.optimization_barrier((h_one, d_kv_own))
-    h_half = jnp.concatenate(
-        [
-            jnp.where(h == 0, h_late[i], h_late[i + h_late.shape[0] // 2])
-            for i in range(h_late.shape[0] // 2)
-        ],
-        axis=1,
-    )
-    mlp_half = lax.dynamic_index_in_dim(branch, h, 0, keepdims=False).astype(F32) + (
-        branch_oth.astype(F32)
-    )
-    output = unflat((h_half + mlp_half).astype(BF16))
+    d_kv_own = gather_dkv(parts, cos, sin)
     d_qkv = jnp.concatenate([d_q, d_kv_own], axis=1)
     d_qkv_mate = mate(d_qkv)
     d_part, gain_one_sum, row_sum = entry(
@@ -1090,10 +1078,22 @@
     d_send, row_sum, gain_one_sum, CHAIN[0] = lax.optimization_barrier(
         (d_send, row_sum, gain_one_sum, CHAIN[0])
     )
+    h_late, branch_late = gate(h_one), gate(branch)
+    h_half = jnp.concatenate(
+        [
+            jnp.where(h == 0, h_late[i], h_late[i + h_late.shape[0] // 2])
+            for i in range(h_late.shape[0] // 2)
+        ],
+        axis=1,
+    )
+    mlp_half = lax.dynamic_index_in_dim(branch_late, h, 0, keepdims=False).astype(F32) + (
+        branch_oth.astype(F32)
+    )
+    output = unflat((h_half + mlp_half).astype(BF16))
     d_other = swap(d_send, "head", 1)
     row_total = row_sum + swap(row_sum, "head", 1)
     (keep_qkv,) = outer(
-        sc_keep, qkv_groups, block_rows, 0, qkv_parts, "qkv_keep", got_qkv, deps=(all2,)
+        sc_keep, qkv_groups, block_rows, 0, qkv_parts, "qkv_keep", got_qkv, deps=(all2, branch_oth)
     )
     per_head = 1.0 / heads
     tail = jnp.stack(

time: 553 us -> 546 us (0.987)
  starting transfers between devices: 50.7 us -> 39.3 us
    reduce_scatter x4, starting transfers between devices: 12 us -> 0.57 us  [both_halves(): lax.psum_scatter(x, 'dp', scatter_dimension=0, axis_index_groups=y_groups...]
    all_to_all x3, waiting for transfers between devices: 30.1 us -> 19.4 us  [over_blk(): return lax.all_to_all(x, 'blk', split_axis=0, concat_axis=0, tiled=True)]
    reduce_scatter x4, waiting for transfers between devices: 0.02 us -> 8.25 us  [both_halves(): lax.psum_scatter(x, 'dp', scatter_dimension=0, axis_index_groups=y_groups...]
    unnamed x72 -> x68, local copies, waits for them, and re-layouts: 15.1 us -> 15 us
  transfers between devices with their start and end apart: 36 -> 36, of which waited for: 13 -> 14; matrix products, arithmetic and copies ran while one was open for 6% -> 7% of each run, Pallas kernels for 44% -> 44%
where the time goes in v3:
time: 546 us; the launch traced here: 537 us
  Pallas kernels  246 us (45%)
  waiting for transfers between devices  183 us (34%)
  starting transfers between devices  39.3 us (7%)
  local copies, waits for them, and re-layouts  33.6 us (6%)
  other arithmetic  17.7 us (3%)
  between operations  17.6 us (3%)
    pallas_call x28, Pallas kernels, launch(): pl.pallas_call(wrapped, grid_spec=pltpu.PrefetchScalarGridSpec(num_scalar...  246 us
    ppermute x21, waiting for transfers between devices, swap(): return lax.ppermute(x, axis, [(i, i ^ bit) for i in range(n)])  108 us
    ppermute x3, waiting for transfers between devices, body(): lax.ppermute(part, 'blk', [(i, i - s) for i in range(s, nblk)])  47 us
    all_to_all x3, waiting for transfers between devices, over_blk(): return lax.all_to_all(x, 'blk', split_axis=0, concat_axis=0, tiled=True)  19.4 us
    all_to_all x3, starting transfers between devices, over_blk(): return lax.all_to_all(x, 'blk', split_axis=0, concat_axis=0, tiled=True)  15.4 us
    unnamed x68, local copies, waits for them, and re-layouts  15 us
    ppermute x21, starting transfers between devices, swap(): return lax.ppermute(x, axis, [(i, i ^ bit) for i in range(n)])  13.5 us
  transfers between devices with their start and end apart: 36, of which 14 were waited for; matrix products, arithmetic and copies ran while one was open for 7% of the time, Pallas kernels for 44%

profile of v3, /device:TPU:0, one launch (start us, length us, event | category | flops | bytes accessed | tf_op | source)
XLA Modules:
  0.0 536.8 jit_solution(8758724791558073391)
XLA Ops:
  15.7 18.0 %collective-permute-done.refs_2_ = bf16[512,1024]{1,0:T(8,128)(2,1)} collective-permute-done((bf16[512,1024]{1,0:T(8,128)(2,1)}, bf16[512,1024]{1,0:T(8,128)(2,1)}, u32[]{:S(2)}, u32[]{:S(2)}) %collective-permute-start) | collective-permute-done | bytes 1048608 | tf_op jit(solution)/shard_map/ppermute | solution.py:93
  37.7 6.9 %project.1 = (bf16[512,2048]{1,0:T(8,128)(2,1)}, bf16[512,2048]{1,0:T(8,128)(2,1)}, bf16[512,1024]{1,0:T(8,128)(2,1)}, bf16[512,256]{1,0:T(8,128)(2,1)}, f32[512,128]{1,0:T(8,128)}, /*index=5*/f32[8,128]{1,0:T(8,128)}) custom-call(s32[1]{0:T(128)} %bitcast.1.refs_0_, bf16[512,1024]{1,0:T(8,128)(2,1)S(1)} %bitcast.62, ...), custom_call_target="tpu_custom_call" | custom-call | flops 1073741824 | bytes 7130316 | tf_op jit(solution)/shard_map/project/pallas_call | solution.py:61
  48.8 7.6 %attend0.1 = (f32[1024,512]{1,0:T(8,128)S(1)}, f32[8,8,512]{2,1,0:T(8,128)S(1)}, f32[8,128]{1,0:T(8,128)}) custom-call(s32[1]{0:T(128)} %bitcast.refs_0_, bf16[512,1024]{1,0:T(8,128)(2,1)} %get-tuple-element.129.refs_1_, bf16[512,256]{1,0:T(8,128)(2,1)} %get-tuple-element.130.refs_2_.refs_5_, s32[1,1,512]{2,1,0:T(1,128)} %bitcast.85, ...), custom_call_target="tpu_custom_call" | custom-call | flops 2576980480 | bytes 4194304 | tf_op jit(solution)/shard_map/attend0/pallas_call | solution.py:61
  69.4 16.4 %collective-permute-done.6 = bf16[512,1024]{1,0:T(8,128)(2,1)} collective-permute-done((bf16[512,1024]{1,0:T(8,128)(2,1)S(1)}, bf16[512,1024]{1,0:T(8,128)(2,1)}, u32[]{:S(2)}, u32[]{:S(2)}) %collective-permute-start.6) | collective-permute-done | bytes 1048608 | tf_op jit(solution)/shard_map/ppermute | solution.py:93
  90.1 15.6 %collective-permute-done.5.refs_1_ = bf16[512,1024]{1,0:T(8,128)(2,1)} collective-permute-done((bf16[512,1024]{1,0:T(8,128)(2,1)}, bf16[512,1024]{1,0:T(8,128)(2,1)}, u32[]{:S(2)}, u32[]{:S(2)}) %collective-permute-start.5) | collective-permute-done | bytes 1048608 | tf_op jit(solution)/shard_map/ppermute | solution.py:93
  105.7 13.1 %merge.1 = (f32[4,512,512]{2,1,0:T(8,128)}, bf16[512,2048]{1,0:T(8,128)(2,1)}, bf16[2048,512]{1,0:T(8,128)(2,1)}, f32[512,128]{1,0:T(8,128)}, f32[512,128]{1,0:T(8,128)}, /*index=5*/f32[8,128]{1,0:T(8,128)}) custom-call(bf16[512,1024]{1,0:T(8,128)(2,1)} %get-tuple-element.152.refs_0_.refs_6_, bf16[512,1024]{1,0:T(8,128)(2,1)} %collective-permute-done.5.refs_1_, ...), custom_call_target="tpu_custom_call" | custom-call | flops 2576980480 | bytes 8388608 | tf_op jit(solution)/shard_map/merge/pallas_call | solution.py:61
  118.8 8.2 %units0.1 = (bf16[3,512,512]{2,1,0:T(8,128)(2,1)}, f32[8,128]{1,0:T(8,128)}) custom-call(bf16[512,2048]{1,0:T(8,128)(2,1)} %get-tuple-element.160.refs_0_, bf16[512,2048]{1,0:T(8,128)(2,1)} %copy-done, bf16[2048,2816]{1,0:T(8,128)(2,1)} %refs_9_.1, bf16[2048,2816]{1,0:T(8,128)(2,1)} %refs_10_.1, bf16[2048,2816]{1,0:T(8,128)(2,1)} %refs_11_.1, ...), custom_call_target="tpu_custom_call" | custom-call | flops 2147483648 | bytes 2516582 | tf_op jit(solution)/shard_map/units0/pallas_call | solution.py:61
  132.2 8.3 %mlp0.1 = (bf16[1024,1536]{1,0:T(8,128)(2,1)}, f32[8,128]{1,0:T(8,128)}) custom-call(s32[2]{0:T(128)S(1)} %pad_add_fusion.refs_0_, bf16[2048,512]{1,0:T(8,128)(2,1)} %get-tuple-element.163.refs_1_.refs_2_, bf16[2048,512]{1,0:T(8,128)(2,1)} %get-tuple-element.163.refs_1_.refs_2_, bf16[2048,512]{1,0:T(8,128)(2,1)} %collective-permute-done.7.refs_3_.refs_4_, ...), custom_call_target="tpu_custom_call" | custom-call | flops 2576980480 | bytes 2516582 | tf_op jit(solution)/shard_map/mlp0/pallas_call | solution.py:61
  141.0 10.5 %units2.1 = (bf16[3,512,768]{2,1,0:T(8,128)(2,1)}, f32[8,128]{1,0:T(8,128)}) custom-call(bf16[512,2048]{1,0:T(8,128)(2,1)} %get-tuple-element.160.refs_0_, bf16[512,2048]{1,0:T(8,128)(2,1)} %copy-done, bf16[2048,2816]{1,0:T(8,128)(2,1)} %refs_9_.1, bf16[2048,2816]{1,0:T(8,128)(2,1)} %refs_10_.1, bf16[2048,2816]{1,0:T(8,128)(2,1)} %refs_11_.1, ...), custom_call_target="tpu_custom_call" | custom-call | flops 3221225472 | bytes 3774873 | tf_op jit(solution)/shard_map/units2/pallas_call | solution.py:61
  151.8 16.8 %units5.1 = (bf16[3,512,1536]{2,1,0:T(8,128)(2,1)}, f32[8,128]{1,0:T(8,128)}) custom-call(bf16[512,2048]{1,0:T(8,128)(2,1)} %get-tuple-element.160.refs_0_, bf16[512,2048]{1,0:T(8,128)(2,1)} %copy-done, bf16[2048,2816]{1,0:T(8,128)(2,1)} %refs_9_.1, bf16[2048,2816]{1,0:T(8,128)(2,1)} %refs_10_.1, bf16[2048,2816]{1,0:T(8,128)(2,1)} %refs_11_.1, ...), custom_call_target="tpu_custom_call" | custom-call | flops 6442450944 | bytes 7549747 | tf_op jit(solution)/shard_map/units5/pallas_call | solution.py:61
  170.1 10.3 %mlp1.1 = (bf16[1024,2304]{1,0:T(8,128)(2,1)}, f32[8,128]{1,0:T(8,128)}) custom-call(s32[2]{0:T(128)S(1)} %pad_add_fusion.refs_0_, bf16[2048,512]{1,0:T(8,128)(2,1)} %get-tuple-element.163.refs_1_.refs_2_, bf16[2048,512]{1,0:T(8,128)(2,1)} %get-tuple-element.163.refs_1_.refs_2_, bf16[2048,512]{1,0:T(8,128)(2,1)} %collective-permute-done.7.refs_3_.refs_4_, ...), custom_call_target="tpu_custom_call" | custom-call | flops 3865470464 | bytes 3774873 | tf_op jit(solution)/shard_map/mlp1/pallas_call | solution.py:61
  180.7 8.2 %reduce-scatter.6.cloned.1.call-done.refs_12_ = bf16[512,1536]{1,0:T(8,128)(2,1)} async-done(((bf16[1024,1536]{1,0:T(8,128)(2,1)}), bf16[512,1536]{1,0:T(8,128)(2,1)}) %reduce-scatter.6.cloned.1.call-update) | async-done | bytes 1572880 | tf_op jit(solution)/shard_map/reduce_scatter | solution.py:1001
  189.0 59.3 %exchange.1 = (f32[512,2048]{1,0:T(8,128)}, bf16[2,512,1024]{2,1,0:T(8,128)(2,1)}, bf16[4,128,1536]{2,1,0:T(8,128)(2,1)}, f32[8,128]{1,0:T(8,128)}) custom-call(bf16[3,512,512]{2,1,0:T(8,128)(2,1)} %get-tuple-element.162.refs_5_.refs_11_.refs_13_.refs_0_.refs_3_.refs_6_, ...), custom_call_target="tpu_custom_call" | custom-call | flops 7086695936 | bytes 13841203 | tf_op jit(solution)/shard_map/exchange/pallas_call | solution.py:61
  248.3 16.6 %mlp2.1 = (bf16[1024,2304]{1,0:T(8,128)(2,1)}, bf16[1024,2304]{1,0:T(8,128)(2,1)}, f32[8,128]{1,0:T(8,128)}) custom-call(s32[2]{0:T(128)S(1)} %pad_add_fusion.refs_0_, bf16[2048,512]{1,0:T(8,128)(2,1)} %get-tuple-element.163.refs_1_.refs_2_, bf16[2048,512]{1,0:T(8,128)(2,1)} %get-tuple-element.163.refs_1_.refs_2_, ...), custom_call_target="tpu_custom_call" | custom-call | flops 7730940928 | bytes 7549747 | tf_op jit(solution)/shard_map/mlp2/pallas_call | solution.py:61
  265.6 10.6 %stream.1 = (f32[512,2048]{1,0:T(8,128)}, bf16[2048,512]{1,0:T(8,128)(2,1)}, bf16[512,1024]{1,0:T(8,128)(2,1)}, f32[1,2048]{1,0:T(1,128)}, f32[8,128]{1,0:T(8,128)}) custom-call(f32[512,2048]{1,0:T(8,128)} %get-tuple-element.173.refs_0_, f32[4,512,512]{2,1,0:T(8,128)} %get-tuple-element.218.refs_1_, f32[512,128]{1,0:T(8,128)} %get-tuple-element.174.refs_2_, ...), custom_call_target="tpu_custom_call" | custom-call | flops 858993472 | bytes 10066329 | tf_op jit(solution)/shard_map/stream/pallas_call | solution.py:61
  305.7 24.2 %collective-permute-done.16.refs_8_.refs_0_ = bf16[512,256]{1,0:T(8,128)(2,1)S(1)} collective-permute-done((bf16[512,256]{1,0:T(8,128)(2,1)}, bf16[512,256]{1,0:T(8,128)(2,1)S(1)}, u32[]{:S(2)}, u32[]{:S(2)}) %collective-permute-start.16) | collective-permute-done | bytes 262176 | tf_op jit(solution)/shard_map/ppermute | solution.py:1057
  329.9 22.8 %collective-permute-done.17.refs_9_.refs_1_ = bf16[512,256]{1,0:T(8,128)(2,1)S(1)} collective-permute-done((bf16[512,256]{1,0:T(8,128)(2,1)}, bf16[512,256]{1,0:T(8,128)(2,1)S(1)}, u32[]{:S(2)}, u32[]{:S(2)}) %collective-permute-start.17) | collective-permute-done | bytes 262176 | tf_op jit(solution)/shard_map/ppermute | solution.py:1057
  361.1 5.9 %all-to-all-start.1 = ((bf16[4,128,2304]{2,1,0:T(8,128)(2,1)}), bf16[4,128,2304]{2,1,0:T(8,128)(2,1)S(1)}, u32[]{:S(2)}, u32[]{:S(2)}) async-start(bf16[4,128,2304]{2,1,0:T(8,128)(2,1)} %bitcast.70), calls=%async_computation.5 | async-start | bytes 4718592 | tf_op jit(solution)/shard_map/all_to_all | solution.py:1008
  366.9 15.8 %attend_back0.1 = (bf16[512,1024]{1,0:T(8,128)(2,1)}, bf16[512,256]{1,0:T(8,128)(2,1)}, f32[8,128]{1,0:T(8,128)}) custom-call(s32[1]{0:T(128)} %bitcast.refs_0_, bf16[512,1024]{1,0:T(8,128)(2,1)} %get-tuple-element.129.refs_1_, bf16[512,1024]{1,0:T(8,128)(2,1)} %get-tuple-element.179.refs_2_, f32[8,8,512]{2,1,0:T(8,128)} %copy-done.11, ...), custom_call_target="tpu_custom_call" | custom-call | flops 5798205952 | bytes 4194304 | tf_op jit(solution)/shard_map/attend_back0/pallas_call | solution.py:61
  392.3 10.5 %entry.1 = (bf16[2,512,1024]{2,1,0:T(8,128)(2,1)}, f32[1,2048]{1,0:T(1,128)}, f32[512,128]{1,0:T(8,128)}, f32[8,128]{1,0:T(8,128)}) custom-call(bf16[512,1024]{1,0:T(8,128)(2,1)} %get-tuple-element.204.refs_0_, bf16[512,256]{1,0:T(8,128)(2,1)} %get-tuple-element.207.refs_1_, bf16[2048,1024]{1,0:T(8,128)(2,1)} %refs_2_.9, bf16[2048,128]{1,0:T(8,128)(2,1)} %refs_3_.7, ...), custom_call_target="tpu_custom_call" | custom-call | flops 1073741824 | bytes 8388608 | tf_op jit(solution)/shard_map/entry/pallas_call | solution.py:61
  426.3 16.2 %collective-permute-done.26 = f32[33,128]{1,0:T(8,128)S(1)} collective-permute-done((f32[33,128]{1,0:T(8,128)S(1)}, f32[33,128]{1,0:T(8,128)S(1)}, u32[]{:S(2)}, u32[]{:S(2)}) %collective-permute-start.26) | collective-permute-done | bytes 16928 | tf_op jit(solution)/shard_map/ppermute | solution.py:93
  445.3 6.1 %qkv_keep.1 = (bf16[512,1280]{1,0:T(8,128)(2,1)}, f32[8,128]{1,0:T(8,128)}) custom-call(s32[1]{0:T(128)} %bitcast.15.refs_0_, bf16[2048,512]{1,0:T(8,128)(2,1)} %get-tuple-element.186.refs_1_, bf16[2048,512]{1,0:T(8,128)(2,1)} %collective-permute-done.14.refs_6_.refs_2_, bf16[1,512,1280]{2,1,0:T(8,128)(2,1)} %bitcast.19.refs_3_, ...), custom_call_target="tpu_custom_call" | custom-call | flops 1073741824 | bytes 1572864 | tf_op jit(solution)/shard_map/qkv_keep/pallas_call | solution.py:61
  464.0 28.2 %collective-permute-done.22 = f32[512,128]{1,0:T(8,128)S(1)} collective-permute-done((f32[512,128]{1,0:T(8,128)}, f32[512,128]{1,0:T(8,128)S(1)}, u32[]{:S(2)}, u32[]{:S(2)}) %collective-permute-start.22) | collective-permute-done | bytes 262176 | tf_op jit(solution)/shard_map/ppermute | solution.py:93
  505.4 19.4 %all-to-all-done.2 = bf16[4,128,2432]{2,1,0:T(8,128)(2,1)S(1)} async-done(((bf16[4,128,2432]{2,1,0:T(8,128)(2,1)}), bf16[4,128,2432]{2,1,0:T(8,128)(2,1)S(1)}, u32[]{:S(2)}, u32[]{:S(2)}) %all-to-all-start.2) | async-done | bytes 2490400 | tf_op jit(solution)/shard_map/all_to_all | solution.py:1008
  (197 shorter events, 143.7 us)
Async XLA Ops:
  7.2 98.5 %all-gather.2.cloned.1.call-start = ((), (), s32[]{:S(2)}) async-start(), calls=%async_computation.8 | async-start | bytes 5242880 | tf_op jit(solution)/shard_map/all_gather | solution.py:976
  7.2 26.5 %collective-permute-start = (bf16[512,1024]{1,0:T(8,128)(2,1)}, bf16[512,1024]{1,0:T(8,128)(2,1)}, u32[]{:S(2)}, u32[]{:S(2)}) collective-permute-start(bf16[512,1024]{1,0:T(8,128)(2,1)} %bitcast.61), channel_id=1, source_target_pairs={{0,1},{1,0},{2,3},{3,2},{4,5},{5,4},{6,7},{7,6},{8,9},{9,8},{10,11... | collective-permute-start | bytes 3145736 | tf_op jit(solution)/shard_map/ppermute | solution.py:93
  33.7 25.1 %collective-permute-start.3 = (bf16[512,1024]{1,0:T(8,128)(2,1)}, bf16[512,1024]{1,0:T(8,128)(2,1)}, u32[]{:S(2)}, u32[]{:S(2)}) collective-permute-start(bf16[512,1024]{1,0:T(8,128)(2,1)} %constant_dynamic-slice_fusion), channel_id=1, source_target_pairs={{0,1},{1,0},{2,3},{3,2},{4,5},{5,4},{6,7},{7,6},{8,9},{9,8},{10,11... | collective-permute-start | bytes 3145736 | tf_op jit(solution)/shard_map/ppermute | solution.py:93
  58.8 130.2 %reduce-scatter.6.cloned.1.call-start = ((), (), s32[]{:S(2)}) async-start(), calls=%async_computation.9 | async-start | bytes 4718592 | tf_op jit(solution)/shard_map/reduce_scatter | solution.py:1001
  59.5 26.3 %collective-permute-start.6 = (bf16[512,1024]{1,0:T(8,128)(2,1)S(1)}, bf16[512,1024]{1,0:T(8,128)(2,1)}, u32[]{:S(2)}, u32[]{:S(2)}) collective-permute-start(bf16[512,1024]{1,0:T(8,128)(2,1)S(1)} %bitcast.72), channel_id=1, source_target_pairs={{0,1},{1,0},{2,3},{3,2},{4,5},{5,4},{6,7},{7,6},{8,9},{9,8},{10,11... | collective-permute-start | bytes 3145736 | tf_op jit(solution)/shard_map/ppermute | solution.py:93
  67.8 37.8 %collective-permute-start.5 = (bf16[512,1024]{1,0:T(8,128)(2,1)}, bf16[512,1024]{1,0:T(8,128)(2,1)}, u32[]{:S(2)}, u32[]{:S(2)}) collective-permute-start(bf16[512,1024]{1,0:T(8,128)(2,1)} %get-tuple-element.152.refs_0_.refs_6_), channel_id=1, source_target_pairs={{0,1},{1,0},{2,3},{3,2},{4,5},{5,4},{6,7},{7,6},{8,9},{9,8},{10,11... | collective-permute-start | bytes 3145736 | tf_op jit(solution)/shard_map/ppermute | solution.py:93
  90.1 37.5 %collective-permute-start.7 = (bf16[2048,512]{1,0:T(8,128)(2,1)}, bf16[2048,512]{1,0:T(8,128)(2,1)}, u32[]{:S(2)}, u32[]{:S(2)}) collective-permute-start(bf16[2048,512]{1,0:T(8,128)(2,1)} %get-tuple-element.163.refs_1_.refs_2_), channel_id=1, source_target_pairs={{0,8},{8,0},{16,24},{24,16},{1,9},{9,1},{17,25},{25,17},{2,10},{10... | collective-permute-start | bytes 6291464 | tf_op jit(solution)/shard_map/ppermute | solution.py:93
  140.5 125.1 %reduce-scatter.8.cloned.1.call-start = ((), (), s32[]{:S(2)}) async-start(), calls=%async_computation.10 | async-start | bytes 7077888 | tf_op jit(solution)/shard_map/reduce_scatter | solution.py:1001
  180.4 180.7 %reduce-scatter.10.cloned.1.call-start = ((), (), s32[]{:S(2)}) async-start(), calls=%async_computation.11 | async-start | bytes 7077888 | tf_op jit(solution)/shard_map/reduce_scatter | solution.py:1001
  180.5 67.9 %collective-permute-start.11 = (bf16[3,512,1536]{2,1,0:T(8,128)(2,1)}, bf16[3,512,1536]{2,1,0:T(8,128)(2,1)}, u32[]{:S(2)}, u32[]{:S(2)}) collective-permute-start(bf16[3,512,1536]{2,1,0:T(8,128)(2,1)} %get-tuple-element.169.refs_2_.refs_5_.refs_8_.refs_11_.refs_13_), channel_id=1, source_target_pairs={{0,8},{8,0},{16,24},{24,16},{1,9},{9,1},{17,25},{25,17},{2,10},{10... | collective-permute-start | bytes 14155784 | tf_op jit(solution)/shard_map/ppermute | solution.py:93
  265.0 145.8 %reduce-scatter.12.cloned.1.call-start = ((), (), s32[]{:S(2)}) async-start(), calls=%async_computation.12 | async-start | bytes 7077888 | tf_op jit(solution)/shard_map/reduce_scatter | solution.py:1001
  276.7 77.5 %all-to-all-start = ((bf16[4,128,2304]{2,1,0:T(8,128)(2,1)}), bf16[4,128,2304]{2,1,0:T(8,128)(2,1)S(1)}, u32[]{:S(2)}, u32[]{:S(2)}) async-start(bf16[4,128,2304]{2,1,0:T(8,128)(2,1)} %bitcast.71), calls=%async_computation.3 | async-start | bytes 4718592 | tf_op jit(solution)/shard_map/all_to_all | solution.py:1008
  289.8 64.3 %collective-permute-start.15 = (bf16[512,1024]{1,0:T(8,128)(2,1)}, bf16[512,1024]{1,0:T(8,128)(2,1)S(1)}, u32[]{:S(2)}, u32[]{:S(2)}) collective-permute-start(bf16[512,1024]{1,0:T(8,128)(2,1)} %get-tuple-element.196), channel_id=1, source_target_pairs={{0,16},{8,24},{16,0},{24,8},{1,17},{9,25},{17,1},{25,9},{2,18},{10... | collective-permute-start | bytes 3145736 | tf_op jit(solution)/shard_map/ppermute | solution.py:93
  294.1 35.8 %collective-permute-start.16 = (bf16[512,256]{1,0:T(8,128)(2,1)}, bf16[512,256]{1,0:T(8,128)(2,1)S(1)}, u32[]{:S(2)}, u32[]{:S(2)}) collective-permute-start(bf16[512,256]{1,0:T(8,128)(2,1)} %get-tuple-element.199), channel_id=1, source_target_pairs={{6,0},{7,1},{14,8},{15,9},{22,16},{23,17},{30,24},{31,25}} | collective-permute-start | bytes 786440 | tf_op jit(solution)/shard_map/ppermute | solution.py:1057
  299.2 53.5 %collective-permute-start.17 = (bf16[512,256]{1,0:T(8,128)(2,1)}, bf16[512,256]{1,0:T(8,128)(2,1)S(1)}, u32[]{:S(2)}, u32[]{:S(2)}) collective-permute-start(bf16[512,256]{1,0:T(8,128)(2,1)} %get-tuple-element.200), channel_id=1, source_target_pairs={{4,0},{6,2},{5,1},{7,3},{12,8},{14,10},{13,9},{15,11},{20,16},{22,... | collective-permute-start | bytes 786440 | tf_op jit(solution)/shard_map/ppermute | solution.py:1057
  304.4 48.3 %collective-permute-start.18 = (bf16[512,256]{1,0:T(8,128)(2,1)}, bf16[512,256]{1,0:T(8,128)(2,1)S(1)}, u32[]{:S(2)}, u32[]{:S(2)}) collective-permute-start(bf16[512,256]{1,0:T(8,128)(2,1)} %get-tuple-element.201), channel_id=1, source_target_pairs={{2,0},{4,2},{6,4},{3,1},{5,3},{7,5},{10,8},{12,10},{14,12},{11,9},... | collective-permute-start | bytes 786440 | tf_op jit(solution)/shard_map/ppermute | solution.py:1057
  361.1 82.7 %all-to-all-start.1 = ((bf16[4,128,2304]{2,1,0:T(8,128)(2,1)}), bf16[4,128,2304]{2,1,0:T(8,128)(2,1)S(1)}, u32[]{:S(2)}, u32[]{:S(2)}) async-start(bf16[4,128,2304]{2,1,0:T(8,128)(2,1)} %bitcast.70), calls=%async_computation.5 | async-start | bytes 4718592 | tf_op jit(solution)/shard_map/all_to_all | solution.py:1008
  366.9 133.2 %reduce-scatter.14.cloned.1.call-start = ((), (), s32[]{:S(2)}) async-start(), calls=%async_computation.13 | async-start | bytes 2949120 | tf_op jit(solution)/shard_map/reduce_scatter | solution.py:1076
  386.9 18.2 %collective-permute-start.19 = (bf16[512,1280]{1,0:T(8,128)(2,1)}, bf16[512,1280]{1,0:T(8,128)(2,1)}, u32[]{:S(2)}, u32[]{:S(2)}) collective-permute-start(bf16[512,1280]{1,0:T(8,128)(2,1)} %constant_dynamic-update-slice_fusion), channel_id=1, source_target_pairs={{0,8},{8,0},{16,24},{24,16},{1,9},{9,1},{17,25},{25,17},{2,10},{10... | collective-permute-start | bytes 3932168 | tf_op jit(solution)/shard_map/ppermute | solution.py:93
  391.8 25.9 %collective-permute-start.20 = (bf16[512,1024]{1,0:T(8,128)(2,1)}, bf16[512,1024]{1,0:T(8,128)(2,1)S(1)}, u32[]{:S(2)}, u32[]{:S(2)}) collective-permute-start(bf16[512,1024]{1,0:T(8,128)(2,1)} %dynamic-slice_bitcast_fusion.1), channel_id=1, source_target_pairs={{0,1},{1,0},{2,3},{3,2},{4,5},{5,4},{6,7},{7,6},{8,9},{9,8},{10,11... | collective-permute-start | bytes 3145736 | tf_op jit(solution)/shard_map/ppermute | solution.py:93
  410.8 33.0 %collective-permute-start.23 = (bf16[512,1280]{1,0:T(8,128)(2,1)}, bf16[512,1280]{1,0:T(8,128)(2,1)}, u32[]{:S(2)}, u32[]{:S(2)}) collective-permute-start(bf16[512,1280]{1,0:T(8,128)(2,1)} %get-tuple-element.226), channel_id=1, source_target_pairs={{0,16},{8,24},{16,0},{24,8},{1,17},{9,25},{17,1},{25,9},{2,18},{10... | collective-permute-start | bytes 3932168 | tf_op jit(solution)/shard_map/ppermute | solution.py:93
  456.4 68.5 %all-to-all-start.2 = ((bf16[4,128,2432]{2,1,0:T(8,128)(2,1)}), bf16[4,128,2432]{2,1,0:T(8,128)(2,1)S(1)}, u32[]{:S(2)}, u32[]{:S(2)}) async-start(bf16[4,128,2432]{2,1,0:T(8,128)(2,1)} %bitcast.40), calls=%async_computation.6 | async-start | bytes 4980736 | tf_op jit(solution)/shard_map/all_to_all | solution.py:1008
  461.9 31.4 %collective-permute-start.21 = (bf16[512,1024]{1,0:T(8,128)(2,1)}, bf16[512,1024]{1,0:T(8,128)(2,1)S(1)}, u32[]{:S(2)}, u32[]{:S(2)}) collective-permute-start(bf16[512,1024]{1,0:T(8,128)(2,1)} %dynamic-slice_bitcast_fusion), channel_id=1, source_target_pairs={{0,1},{1,0},{2,3},{3,2},{4,5},{5,4},{6,7},{7,6},{8,9},{9,8},{10,11... | collective-permute-start | bytes 3145736 | tf_op jit(solution)/shard_map/ppermute | solution.py:93
  463.7 28.5 %collective-permute-start.22 = (f32[512,128]{1,0:T(8,128)}, f32[512,128]{1,0:T(8,128)S(1)}, u32[]{:S(2)}, u32[]{:S(2)}) collective-permute-start(f32[512,128]{1,0:T(8,128)} %get-tuple-element.225), channel_id=1, source_target_pairs={{0,1},{1,0},{2,3},{3,2},{4,5},{5,4},{6,7},{7,6},{8,9},{9,8},{10,11... | collective-permute-start | bytes 786440 | tf_op jit(solution)/shard_map/ppermute | solution.py:93
  (45 other events, 421.2 us)
Sparse Core Ops, SparseCore 0:
  58.9 35.5 all-gather.1
  140.6 48.2 reduce-scatter.5
  191.4 59.9 reduce-scatter.7
  265.1 79.6 reduce-scatter.9
  347.0 59.9 reduce-scatter.11
  424.7 55.5 reduce-scatter.13

commit v4 on v3

--- a/solution.py
+++ b/solution.py
@@ -433,9 +433,33 @@
     )[0]
 
 
-def merge_kernel(o_own, o_oth, w_own, w_oth, full, gain, h1, a2, a2_t, r2, ssa, held, sums):
+def own_part_kernel(o_own, w_own, out):
+    out[0] = dot_nt(o_own[...], w_own[...])
+
+
+def own_part(o_own, w_own):
+    n, e = o_own.shape
+    d = w_own.shape[0]
+    dt = 512
+    return launch(
+        own_part_kernel,
+        (o_own, w_own),
+        grid=(d // dt,),
+        in_specs=[
+            pl.BlockSpec((n, e), lambda i: (0, 0), pipeline_mode=pl.Buffered(1)),
+            pl.BlockSpec((dt, e), lambda i: (i, 0)),
+        ],
+        out_specs=[pl.BlockSpec((1, n, dt), lambda i: (i, 0, 0))],
+        out_shape=[jax.ShapeDtypeStruct((d // dt, n, dt), F32)],
+        mib=40,
+        estimate=cost(n * d * e, 2 * d * e),
+        name="own_part",
+    )[0]
+
+
+def merge_kernel(part, o_oth, w_oth, full, gain, h1, a2, a2_t, r2, ssa, held, sums):
     i = pl.program_id(0)
-    attn = dot_nt(o_own[...], w_own[...]) + dot_nt(o_oth[...], w_oth[...])
+    attn = part[0] + dot_nt(o_oth[...], w_oth[...])
     x = full[...].astype(F32) + attn
     h1[0] = x
     held[i] = x
@@ -460,19 +484,18 @@
             a2_t[at, :] = act.T
 
 
-def merge(o_own, o_oth, w_own, w_oth, full, gain, deps=()):
+def merge(part, o_oth, w_oth, full, gain, deps=()):
     n, d = full.shape
     dt = 512
-    e = o_own.shape[1]
+    e = o_oth.shape[1]
     const = lambda a: pl.BlockSpec(a.shape, lambda i: (0, 0), pipeline_mode=pl.Buffered(1))
     return launch(
         merge_kernel,
-        (o_own, o_oth, w_own, w_oth, full, gain),
+        (part, o_oth, w_oth, full, gain),
         grid=(d // dt,),
         in_specs=[
-            const(o_own),
+            pl.BlockSpec((1, n, dt), lambda i: (i, 0, 0)),
             const(o_oth),
-            pl.BlockSpec((dt, e), lambda i: (i, 0)),
             pl.BlockSpec((dt, e), lambda i: (i, 0)),
             pl.BlockSpec((n, dt), lambda i: (0, i)),
             const(gain),
@@ -886,6 +909,39 @@
     )
 
 
+def finish_rows_kernel(shares, *outs):
+    at = 0
+    for out in outs[:-1]:
+        columns = slice(at, at + out.shape[1])
+        total = shares[0, :, columns].astype(F32)
+        for b in range(1, shares.shape[0]):
+            total = total + shares[b, :, columns].astype(F32)
+        out[...] = total
+        at += out.shape[1]
+    total = shares[0, :, at:].astype(F32)
+    for b in range(1, shares.shape[0]):
+        total = total + shares[b, :, at:].astype(F32)
+    outs[-1][...] = total.T
+
+
+def finish_rows(shares, widths):
+    _, rows, columns = shares.shape
+    left = columns - sum(widths)
+    whole = lambda shape: pl.BlockSpec(shape, lambda i: (0,) * len(shape))
+    shapes = [(rows, w) for w in widths] + [(left, rows)]
+    return launch(
+        finish_rows_kernel,
+        (shares,),
+        grid=(1,),
+        in_specs=[whole(shares.shape)],
+        out_specs=[whole(x) for x in shapes],
+        out_shape=[jax.ShapeDtypeStruct(x, F32) for x in shapes],
+        mib=32,
+        estimate=cost(0, 4 * shares.size),
+        name="finish_rows",
+    )
+
+
 def body(
     inputs,
     cotangent,
@@ -979,13 +1035,14 @@
     acc, ml = state
     o_own = flip(acc)
     o_oth = swap(o_own, "head", 1)
+    part_own = own_part(o_own, w_out)
     g_full = jnp.concatenate(
         [jnp.where(h == 0, g_own, g_oth), jnp.where(h == 0, g_oth, g_own)], axis=1
     )
     g_t = flip(g_full, "flip_g")
     o_mate, g_mate = mate(o_own), mate(g_t)
     h_one, a_two, a_two_t, inv_two, ssa = merge(
-        o_own, o_oth, w_out, w_out_oth, full, gain_two
+        part_own, o_oth, w_out_oth, full, gain_two
     )
     a_two_mate = mate(a_two_t)
 
@@ -1122,12 +1179,12 @@
     extra = jnp.concatenate(
         [coarse, fine, jnp.zeros((block_rows, PAIR - 12), BF16)], axis=1
     )
-    all_qkv = over_blk(jnp.concatenate([keep_qkv, extra, keep_out], axis=1))
+    all_qkv = over_blk(jnp.concatenate([keep_qkv, keep_out, extra], axis=1))
     grad_down, grad_gate, grad_up = finish([(all0.reshape(-1, all0.shape[2]), nblk), (all1, nblk), (all2, nblk), (sum3, 1)])
-    own_rows = lambda x: jnp.sum(x.reshape(nblk, -1, x.shape[1]).astype(F32), axis=0)
-    sum_qkv = own_rows(all_qkv)
-    sum_out = sum_qkv[:, sum_qkv.shape[1] - o_own.shape[1] :]
     qw, kvw = w_query.shape[1], w_key.shape[1]
+    sum_query, sum_key, sum_value, sum_out, small = finish_rows(
+        all_qkv.reshape(nblk, -1, all_qkv.shape[1]), (qw, kvw, kvw, o_own.shape[1])
+    )
 
     inv_one = lax.rsqrt(ssx[:, :1] * (1.0 / d) + EPS)
     d_one = lax.dynamic_index_in_dim(d_part, h, 0, keepdims=False).astype(F32) + d_other.astype(F32)
@@ -1136,18 +1193,17 @@
         d_one * by_head(gain_one) - norm_half * (row_total[:, :1] * (1.0 / d))
     )
 
-    width = qw + 2 * kvw
-    small = sum_qkv[:, width : width + 6] + sum_qkv[:, width + 6 : width + 12]
-    grad_attn_gain, grad_mlp_gain = small[:, 0], small[:, 1]
-    stats = jnp.sqrt(small[0, 3:6] / (small[0, 2] * d))
+    small = small[:6] + small[6:12]
+    grad_attn_gain, grad_mlp_gain = small[0], small[1]
+    stats = jnp.sqrt(small[3:6, 0] / (small[2, 0] * d))
 
     return (
         output,
         unflat(grad_input),
         grad_attn_gain,
-        sum_qkv[:, :qw],
-        sum_qkv[:, qw : qw + kvw],
-        sum_qkv[:, qw + kvw : width],
+        sum_query,
+        sum_key,
+        sum_value,
         sum_out,
         grad_mlp_gain,
         grad_gate,

time: 546 us -> 548 us (level)
  Pallas kernels: 246 us -> 254 us
  waiting for transfers between devices: 183 us -> 177 us
    pallas_call x28 -> x30, Pallas kernels: 246 us -> 254 us  [launch(): pl.pallas_call(wrapped, grid_spec=pltpu.PrefetchScalarGridSpec(num_scalar...]
    ppermute x21, waiting for transfers between devices: 108 us -> 101 us  [swap(): return lax.ppermute(x, axis, [(i, i ^ bit) for i in range(n)])]
    unnamed x68 -> x70, local copies, waits for them, and re-layouts: 15 us -> 16.4 us
  transfers between devices with their start and end apart: 36 -> 36, of which waited for: 14 -> 14; matrix products, arithmetic and copies ran while one was open for 7% -> 7% of each run, Pallas kernels for 44% -> 45%
where the time goes in v4:
time: 548 us; the launch traced here: 538 us
  Pallas kernels  254 us (46%)
  waiting for transfers between devices  177 us (32%)
  starting transfers between devices  38.8 us (7%)
  local copies, waits for them, and re-layouts  32.9 us (6%)
  other arithmetic  18.1 us (3%)
  between operations  17.6 us (3%)
    pallas_call x30, Pallas kernels, launch(): pl.pallas_call(wrapped, grid_spec=pltpu.PrefetchScalarGridSpec(num_scalar...  254 us
    ppermute x21, waiting for transfers between devices, swap(): return lax.ppermute(x, axis, [(i, i ^ bit) for i in range(n)])  101 us
    ppermute x3, waiting for transfers between devices, body(): lax.ppermute(part, 'blk', [(i, i - s) for i in range(s, nblk)])  47 us
    all_to_all x3, waiting for transfers between devices, over_blk(): return lax.all_to_all(x, 'blk', split_axis=0, concat_axis=0, tiled=True)  19.4 us
    unnamed x70, local copies, waits for them, and re-layouts  16.4 us
    all_to_all x3, starting transfers between devices, over_blk(): return lax.all_to_all(x, 'blk', split_axis=0, concat_axis=0, tiled=True)  15.4 us
    ppermute x21, starting transfers between devices, swap(): return lax.ppermute(x, axis, [(i, i ^ bit) for i in range(n)])  13.4 us
  transfers between devices with their start and end apart: 36, of which 14 were waited for; matrix products, arithmetic and copies ran while one was open for 7% of the time, Pallas kernels for 45%

profile of v4, /device:TPU:0, one launch (start us, length us, event | category | flops | bytes accessed | tf_op | source)
XLA Modules:
  0.0 538.0 jit_solution(1258243749414938185)
XLA Ops:
  15.7 18.0 %collective-permute-done.refs_2_ = bf16[512,1024]{1,0:T(8,128)(2,1)} collective-permute-done((bf16[512,1024]{1,0:T(8,128)(2,1)}, bf16[512,1024]{1,0:T(8,128)(2,1)}, u32[]{:S(2)}, u32[]{:S(2)}) %collective-permute-start) | collective-permute-done | bytes 1048608 | tf_op jit(solution)/shard_map/ppermute | solution.py:93
  37.7 6.9 %project.1 = (bf16[512,2048]{1,0:T(8,128)(2,1)}, bf16[512,2048]{1,0:T(8,128)(2,1)}, bf16[512,1024]{1,0:T(8,128)(2,1)}, bf16[512,256]{1,0:T(8,128)(2,1)}, f32[512,128]{1,0:T(8,128)}, /*index=5*/f32[8,128]{1,0:T(8,128)}) custom-call(s32[1]{0:T(128)} %bitcast.1.refs_0_, bf16[512,1024]{1,0:T(8,128)(2,1)S(1)} %bitcast.64, ...), custom_call_target="tpu_custom_call" | custom-call | flops 1073741824 | bytes 7130316 | tf_op jit(solution)/shard_map/project/pallas_call | solution.py:61
  48.8 7.6 %attend0.1 = (f32[1024,512]{1,0:T(8,128)S(1)}, f32[8,8,512]{2,1,0:T(8,128)S(1)}, f32[8,128]{1,0:T(8,128)}) custom-call(s32[1]{0:T(128)} %bitcast.refs_0_, bf16[512,1024]{1,0:T(8,128)(2,1)} %get-tuple-element.137.refs_1_, bf16[512,256]{1,0:T(8,128)(2,1)} %get-tuple-element.138.refs_2_.refs_5_, s32[1,1,512]{2,1,0:T(1,128)} %bitcast.87, ...), custom_call_target="tpu_custom_call" | custom-call | flops 2576980480 | bytes 4194304 | tf_op jit(solution)/shard_map/attend0/pallas_call | solution.py:61
  69.4 6.5 %own_part.1 = (f32[4,512,512]{2,1,0:T(8,128)}, f32[8,128]{1,0:T(8,128)}) custom-call(bf16[512,1024]{1,0:T(8,128)(2,1)} %get-tuple-element.160.refs_0_.refs_6_, bf16[2048,1024]{1,0:T(8,128)(2,1)} %refs_5_.3, f32[8,128]{1,0:T(8,128)} %get-tuple-element.161.refs_2_), custom_call_target="tpu_custom_call" | custom-call | flops 429496736 | bytes 1677721 | tf_op jit(solution)/shard_map/own_part/pallas_call | solution.py:61
  75.8 10.0 %collective-permute-done.6 = bf16[512,1024]{1,0:T(8,128)(2,1)} collective-permute-done((bf16[512,1024]{1,0:T(8,128)(2,1)S(1)}, bf16[512,1024]{1,0:T(8,128)(2,1)}, u32[]{:S(2)}, u32[]{:S(2)}) %collective-permute-start.6) | collective-permute-done | bytes 1048608 | tf_op jit(solution)/shard_map/ppermute | solution.py:93
  90.0 15.6 %collective-permute-done.5.refs_1_ = bf16[512,1024]{1,0:T(8,128)(2,1)} collective-permute-done((bf16[512,1024]{1,0:T(8,128)(2,1)}, bf16[512,1024]{1,0:T(8,128)(2,1)}, u32[]{:S(2)}, u32[]{:S(2)}) %collective-permute-start.5) | collective-permute-done | bytes 1048608 | tf_op jit(solution)/shard_map/ppermute | solution.py:93
  105.7 11.3 %merge.1 = (f32[4,512,512]{2,1,0:T(8,128)}, bf16[512,2048]{1,0:T(8,128)(2,1)}, bf16[2048,512]{1,0:T(8,128)(2,1)}, f32[512,128]{1,0:T(8,128)}, f32[512,128]{1,0:T(8,128)}, /*index=5*/f32[8,128]{1,0:T(8,128)}) custom-call(f32[4,512,512]{2,1,0:T(8,128)} %get-tuple-element.162.refs_0_, bf16[512,1024]{1,0:T(8,128)(2,1)} %collective-permute-done.5.refs_1_, ...), custom_call_target="tpu_custom_call" | custom-call | flops 2576980480 | bytes 8388608 | tf_op jit(solution)/shard_map/merge/pallas_call | solution.py:61
  117.0 8.2 %units0.1 = (bf16[3,512,512]{2,1,0:T(8,128)(2,1)}, f32[8,128]{1,0:T(8,128)}) custom-call(bf16[512,2048]{1,0:T(8,128)(2,1)} %get-tuple-element.170.refs_0_, bf16[512,2048]{1,0:T(8,128)(2,1)} %copy-done, bf16[2048,2816]{1,0:T(8,128)(2,1)} %refs_9_.1, bf16[2048,2816]{1,0:T(8,128)(2,1)} %refs_10_.1, bf16[2048,2816]{1,0:T(8,128)(2,1)} %refs_11_.1, ...), custom_call_target="tpu_custom_call" | custom-call | flops 2147483648 | bytes 2516582 | tf_op jit(solution)/shard_map/units0/pallas_call | solution.py:61
  130.4 8.6 %mlp0.1 = (bf16[1024,1536]{1,0:T(8,128)(2,1)}, f32[8,128]{1,0:T(8,128)}) custom-call(s32[2]{0:T(128)S(1)} %pad_add_fusion.refs_0_, bf16[2048,512]{1,0:T(8,128)(2,1)} %get-tuple-element.173.refs_1_.refs_2_, bf16[2048,512]{1,0:T(8,128)(2,1)} %get-tuple-element.173.refs_1_.refs_2_, bf16[2048,512]{1,0:T(8,128)(2,1)} %collective-permute-done.7.refs_3_.refs_4_, ...), custom_call_target="tpu_custom_call" | custom-call | flops 2576980480 | bytes 2516582 | tf_op jit(solution)/shard_map/mlp0/pallas_call | solution.py:61
  139.1 10.4 %units2.1 = (bf16[3,512,768]{2,1,0:T(8,128)(2,1)}, f32[8,128]{1,0:T(8,128)}) custom-call(bf16[512,2048]{1,0:T(8,128)(2,1)} %get-tuple-element.170.refs_0_, bf16[512,2048]{1,0:T(8,128)(2,1)} %copy-done, bf16[2048,2816]{1,0:T(8,128)(2,1)} %refs_9_.1, bf16[2048,2816]{1,0:T(8,128)(2,1)} %refs_10_.1, bf16[2048,2816]{1,0:T(8,128)(2,1)} %refs_11_.1, ...), custom_call_target="tpu_custom_call" | custom-call | flops 3221225472 | bytes 3774873 | tf_op jit(solution)/shard_map/units2/pallas_call | solution.py:61
  149.9 16.9 %units5.1 = (bf16[3,512,1536]{2,1,0:T(8,128)(2,1)}, f32[8,128]{1,0:T(8,128)}) custom-call(bf16[512,2048]{1,0:T(8,128)(2,1)} %get-tuple-element.170.refs_0_, bf16[512,2048]{1,0:T(8,128)(2,1)} %copy-done, bf16[2048,2816]{1,0:T(8,128)(2,1)} %refs_9_.1, bf16[2048,2816]{1,0:T(8,128)(2,1)} %refs_10_.1, bf16[2048,2816]{1,0:T(8,128)(2,1)} %refs_11_.1, ...), custom_call_target="tpu_custom_call" | custom-call | flops 6442450944 | bytes 7549747 | tf_op jit(solution)/shard_map/units5/pallas_call | solution.py:61
  168.4 10.3 %mlp1.1 = (bf16[1024,2304]{1,0:T(8,128)(2,1)}, f32[8,128]{1,0:T(8,128)}) custom-call(s32[2]{0:T(128)S(1)} %pad_add_fusion.refs_0_, bf16[2048,512]{1,0:T(8,128)(2,1)} %get-tuple-element.173.refs_1_.refs_2_, bf16[2048,512]{1,0:T(8,128)(2,1)} %get-tuple-element.173.refs_1_.refs_2_, bf16[2048,512]{1,0:T(8,128)(2,1)} %collective-permute-done.7.refs_3_.refs_4_, ...), custom_call_target="tpu_custom_call" | custom-call | flops 3865470464 | bytes 3774873 | tf_op jit(solution)/shard_map/mlp1/pallas_call | solution.py:61
  179.1 8.4 %reduce-scatter.6.cloned.1.call-done.refs_12_ = bf16[512,1536]{1,0:T(8,128)(2,1)} async-done(((bf16[1024,1536]{1,0:T(8,128)(2,1)}), bf16[512,1536]{1,0:T(8,128)(2,1)}) %reduce-scatter.6.cloned.1.call-update) | async-done | bytes 1572880 | tf_op jit(solution)/shard_map/reduce_scatter | solution.py:1058
  187.5 59.4 %exchange.1 = (f32[512,2048]{1,0:T(8,128)}, bf16[2,512,1024]{2,1,0:T(8,128)(2,1)}, bf16[4,128,1536]{2,1,0:T(8,128)(2,1)}, f32[8,128]{1,0:T(8,128)}) custom-call(bf16[3,512,512]{2,1,0:T(8,128)(2,1)} %get-tuple-element.172.refs_5_.refs_11_.refs_13_.refs_0_.refs_3_.refs_6_, ...), custom_call_target="tpu_custom_call" | custom-call | flops 7086695936 | bytes 13841203 | tf_op jit(solution)/shard_map/exchange/pallas_call | solution.py:61
  246.9 16.6 %mlp2.1 = (bf16[1024,2304]{1,0:T(8,128)(2,1)}, bf16[1024,2304]{1,0:T(8,128)(2,1)}, f32[8,128]{1,0:T(8,128)}) custom-call(s32[2]{0:T(128)S(1)} %pad_add_fusion.refs_0_, bf16[2048,512]{1,0:T(8,128)(2,1)} %get-tuple-element.173.refs_1_.refs_2_, bf16[2048,512]{1,0:T(8,128)(2,1)} %get-tuple-element.173.refs_1_.refs_2_, ...), custom_call_target="tpu_custom_call" | custom-call | flops 7730940928 | bytes 7549747 | tf_op jit(solution)/shard_map/mlp2/pallas_call | solution.py:61
  264.1 10.6 %stream.1 = (f32[512,2048]{1,0:T(8,128)}, bf16[2048,512]{1,0:T(8,128)(2,1)}, bf16[512,1024]{1,0:T(8,128)(2,1)}, f32[1,2048]{1,0:T(1,128)}, f32[8,128]{1,0:T(8,128)}) custom-call(f32[512,2048]{1,0:T(8,128)} %get-tuple-element.183.refs_0_, f32[4,512,512]{2,1,0:T(8,128)} %get-tuple-element.228.refs_1_, f32[512,128]{1,0:T(8,128)} %get-tuple-element.184.refs_2_, ...), custom_call_target="tpu_custom_call" | custom-call | flops 858993472 | bytes 10066329 | tf_op jit(solution)/shard_map/stream/pallas_call | solution.py:61
  304.3 24.2 %collective-permute-done.16.refs_8_.refs_0_ = bf16[512,256]{1,0:T(8,128)(2,1)S(1)} collective-permute-done((bf16[512,256]{1,0:T(8,128)(2,1)}, bf16[512,256]{1,0:T(8,128)(2,1)S(1)}, u32[]{:S(2)}, u32[]{:S(2)}) %collective-permute-start.16) | collective-permute-done | bytes 262176 | tf_op jit(solution)/shard_map/ppermute | solution.py:1114
  328.4 22.8 %collective-permute-done.17.refs_9_.refs_1_ = bf16[512,256]{1,0:T(8,128)(2,1)S(1)} collective-permute-done((bf16[512,256]{1,0:T(8,128)(2,1)}, bf16[512,256]{1,0:T(8,128)(2,1)S(1)}, u32[]{:S(2)}, u32[]{:S(2)}) %collective-permute-start.17) | collective-permute-done | bytes 262176 | tf_op jit(solution)/shard_map/ppermute | solution.py:1114
  365.4 15.8 %attend_back0.1 = (bf16[512,1024]{1,0:T(8,128)(2,1)}, bf16[512,256]{1,0:T(8,128)(2,1)}, f32[8,128]{1,0:T(8,128)}) custom-call(s32[1]{0:T(128)} %bitcast.refs_0_, bf16[512,1024]{1,0:T(8,128)(2,1)} %get-tuple-element.137.refs_1_, bf16[512,1024]{1,0:T(8,128)(2,1)} %get-tuple-element.189.refs_2_, f32[8,8,512]{2,1,0:T(8,128)} %copy-done.11, ...), custom_call_target="tpu_custom_call" | custom-call | flops 5798205952 | bytes 4194304 | tf_op jit(solution)/shard_map/attend_back0/pallas_call | solution.py:61
  390.8 10.5 %entry.1 = (bf16[2,512,1024]{2,1,0:T(8,128)(2,1)}, f32[1,2048]{1,0:T(1,128)}, f32[512,128]{1,0:T(8,128)}, f32[8,128]{1,0:T(8,128)}) custom-call(bf16[512,1024]{1,0:T(8,128)(2,1)} %get-tuple-element.214.refs_0_, bf16[512,256]{1,0:T(8,128)(2,1)} %get-tuple-element.217.refs_1_, bf16[2048,1024]{1,0:T(8,128)(2,1)} %refs_2_.7, bf16[2048,128]{1,0:T(8,128)(2,1)} %refs_3_.7, ...), custom_call_target="tpu_custom_call" | custom-call | flops 1073741824 | bytes 8388608 | tf_op jit(solution)/shard_map/entry/pallas_call | solution.py:61
  424.7 16.2 %collective-permute-done.26 = f32[33,128]{1,0:T(8,128)S(1)} collective-permute-done((f32[33,128]{1,0:T(8,128)S(1)}, f32[33,128]{1,0:T(8,128)S(1)}, u32[]{:S(2)}, u32[]{:S(2)}) %collective-permute-start.26) | collective-permute-done | bytes 16928 | tf_op jit(solution)/shard_map/ppermute | solution.py:93
  443.7 6.1 %qkv_keep.1 = (bf16[512,1280]{1,0:T(8,128)(2,1)}, f32[8,128]{1,0:T(8,128)}) custom-call(s32[1]{0:T(128)} %bitcast.15.refs_0_, bf16[2048,512]{1,0:T(8,128)(2,1)} %get-tuple-element.196.refs_1_, bf16[2048,512]{1,0:T(8,128)(2,1)} %collective-permute-done.14.refs_6_.refs_2_, bf16[1,512,1280]{2,1,0:T(8,128)(2,1)} %bitcast.19.refs_3_, ...), custom_call_target="tpu_custom_call" | custom-call | flops 1073741824 | bytes 1572864 | tf_op jit(solution)/shard_map/qkv_keep/pallas_call | solution.py:61
  462.4 28.2 %collective-permute-done.22 = f32[512,128]{1,0:T(8,128)S(1)} collective-permute-done((f32[512,128]{1,0:T(8,128)}, f32[512,128]{1,0:T(8,128)S(1)}, u32[]{:S(2)}, u32[]{:S(2)}) %collective-permute-start.22) | collective-permute-done | bytes 262176 | tf_op jit(solution)/shard_map/ppermute | solution.py:93
  503.9 19.4 %all-to-all-done.2.refs_0_ = bf16[4,128,2432]{2,1,0:T(8,128)(2,1)S(1)} async-done(((bf16[4,128,2432]{2,1,0:T(8,128)(2,1)}), bf16[4,128,2432]{2,1,0:T(8,128)(2,1)S(1)}, u32[]{:S(2)}, u32[]{:S(2)}) %all-to-all-start.2) | async-done | bytes 2490400 | tf_op jit(solution)/shard_map/all_to_all | solution.py:1065
  (198 shorter events, 151.8 us)
Async XLA Ops:
  7.2 98.5 %all-gather.2.cloned.1.call-start = ((), (), s32[]{:S(2)}) async-start(), calls=%async_computation.8 | async-start | bytes 5242880 | tf_op jit(solution)/shard_map/all_gather | solution.py:1032
  7.2 26.5 %collective-permute-start = (bf16[512,1024]{1,0:T(8,128)(2,1)}, bf16[512,1024]{1,0:T(8,128)(2,1)}, u32[]{:S(2)}, u32[]{:S(2)}) collective-permute-start(bf16[512,1024]{1,0:T(8,128)(2,1)} %bitcast.63), channel_id=1, source_target_pairs={{0,1},{1,0},{2,3},{3,2},{4,5},{5,4},{6,7},{7,6},{8,9},{9,8},{10,11... | collective-permute-start | bytes 3145736 | tf_op jit(solution)/shard_map/ppermute | solution.py:93
  33.7 25.1 %collective-permute-start.3 = (bf16[512,1024]{1,0:T(8,128)(2,1)}, bf16[512,1024]{1,0:T(8,128)(2,1)}, u32[]{:S(2)}, u32[]{:S(2)}) collective-permute-start(bf16[512,1024]{1,0:T(8,128)(2,1)} %constant_dynamic-slice_fusion), channel_id=1, source_target_pairs={{0,1},{1,0},{2,3},{3,2},{4,5},{5,4},{6,7},{7,6},{8,9},{9,8},{10,11... | collective-permute-start | bytes 3145736 | tf_op jit(solution)/shard_map/ppermute | solution.py:93
  58.8 128.7 %reduce-scatter.6.cloned.1.call-start = ((), (), s32[]{:S(2)}) async-start(), calls=%async_computation.9 | async-start | bytes 4718592 | tf_op jit(solution)/shard_map/reduce_scatter | solution.py:1058
  59.5 26.3 %collective-permute-start.6 = (bf16[512,1024]{1,0:T(8,128)(2,1)S(1)}, bf16[512,1024]{1,0:T(8,128)(2,1)}, u32[]{:S(2)}, u32[]{:S(2)}) collective-permute-start(bf16[512,1024]{1,0:T(8,128)(2,1)S(1)} %bitcast.74), channel_id=1, source_target_pairs={{0,1},{1,0},{2,3},{3,2},{4,5},{5,4},{6,7},{7,6},{8,9},{9,8},{10,11... | collective-permute-start | bytes 3145736 | tf_op jit(solution)/shard_map/ppermute | solution.py:93
  67.8 37.8 %collective-permute-start.5 = (bf16[512,1024]{1,0:T(8,128)(2,1)}, bf16[512,1024]{1,0:T(8,128)(2,1)}, u32[]{:S(2)}, u32[]{:S(2)}) collective-permute-start(bf16[512,1024]{1,0:T(8,128)(2,1)} %get-tuple-element.160.refs_0_.refs_6_), channel_id=1, source_target_pairs={{0,1},{1,0},{2,3},{3,2},{4,5},{5,4},{6,7},{7,6},{8,9},{9,8},{10,11... | collective-permute-start | bytes 3145736 | tf_op jit(solution)/shard_map/ppermute | solution.py:93
  90.0 35.7 %collective-permute-start.7 = (bf16[2048,512]{1,0:T(8,128)(2,1)}, bf16[2048,512]{1,0:T(8,128)(2,1)}, u32[]{:S(2)}, u32[]{:S(2)}) collective-permute-start(bf16[2048,512]{1,0:T(8,128)(2,1)} %get-tuple-element.173.refs_1_.refs_2_), channel_id=1, source_target_pairs={{0,8},{8,0},{16,24},{24,16},{1,9},{9,1},{17,25},{25,17},{2,10},{10... | collective-permute-start | bytes 6291464 | tf_op jit(solution)/shard_map/ppermute | solution.py:93
  139.1 125.0 %reduce-scatter.8.cloned.1.call-start = ((), (), s32[]{:S(2)}) async-start(), calls=%async_computation.10 | async-start | bytes 7077888 | tf_op jit(solution)/shard_map/reduce_scatter | solution.py:1058
  178.7 180.8 %reduce-scatter.10.cloned.1.call-start = ((), (), s32[]{:S(2)}) async-start(), calls=%async_computation.11 | async-start | bytes 7077888 | tf_op jit(solution)/shard_map/reduce_scatter | solution.py:1058
  178.8 68.1 %collective-permute-start.11 = (bf16[3,512,1536]{2,1,0:T(8,128)(2,1)}, bf16[3,512,1536]{2,1,0:T(8,128)(2,1)}, u32[]{:S(2)}, u32[]{:S(2)}) collective-permute-start(bf16[3,512,1536]{2,1,0:T(8,128)(2,1)} %get-tuple-element.179.refs_2_.refs_5_.refs_8_.refs_11_.refs_13_), channel_id=1, source_target_pairs={{0,8},{8,0},{16,24},{24,16},{1,9},{9,1},{17,25},{25,17},{2,10},{10... | collective-permute-start | bytes 14155784 | tf_op jit(solution)/shard_map/ppermute | solution.py:93
  263.5 145.7 %reduce-scatter.12.cloned.1.call-start = ((), (), s32[]{:S(2)}) async-start(), calls=%async_computation.12 | async-start | bytes 7077888 | tf_op jit(solution)/shard_map/reduce_scatter | solution.py:1058
  275.2 77.4 %all-to-all-start = ((bf16[4,128,2304]{2,1,0:T(8,128)(2,1)}), bf16[4,128,2304]{2,1,0:T(8,128)(2,1)S(1)}, u32[]{:S(2)}, u32[]{:S(2)}) async-start(bf16[4,128,2304]{2,1,0:T(8,128)(2,1)} %bitcast.73), calls=%async_computation.3 | async-start | bytes 4718592 | tf_op jit(solution)/shard_map/all_to_all | solution.py:1065
  288.4 64.3 %collective-permute-start.15 = (bf16[512,1024]{1,0:T(8,128)(2,1)}, bf16[512,1024]{1,0:T(8,128)(2,1)S(1)}, u32[]{:S(2)}, u32[]{:S(2)}) collective-permute-start(bf16[512,1024]{1,0:T(8,128)(2,1)} %get-tuple-element.206), channel_id=1, source_target_pairs={{0,16},{8,24},{16,0},{24,8},{1,17},{9,25},{17,1},{25,9},{2,18},{10... | collective-permute-start | bytes 3145736 | tf_op jit(solution)/shard_map/ppermute | solution.py:93
  292.7 35.7 %collective-permute-start.16 = (bf16[512,256]{1,0:T(8,128)(2,1)}, bf16[512,256]{1,0:T(8,128)(2,1)S(1)}, u32[]{:S(2)}, u32[]{:S(2)}) collective-permute-start(bf16[512,256]{1,0:T(8,128)(2,1)} %get-tuple-element.209), channel_id=1, source_target_pairs={{6,0},{7,1},{14,8},{15,9},{22,16},{23,17},{30,24},{31,25}} | collective-permute-start | bytes 786440 | tf_op jit(solution)/shard_map/ppermute | solution.py:1114
  297.7 53.6 %collective-permute-start.17 = (bf16[512,256]{1,0:T(8,128)(2,1)}, bf16[512,256]{1,0:T(8,128)(2,1)S(1)}, u32[]{:S(2)}, u32[]{:S(2)}) collective-permute-start(bf16[512,256]{1,0:T(8,128)(2,1)} %get-tuple-element.210), channel_id=1, source_target_pairs={{4,0},{6,2},{5,1},{7,3},{12,8},{14,10},{13,9},{15,11},{20,16},{22,... | collective-permute-start | bytes 786440 | tf_op jit(solution)/shard_map/ppermute | solution.py:1114
  303.0 48.3 %collective-permute-start.18 = (bf16[512,256]{1,0:T(8,128)(2,1)}, bf16[512,256]{1,0:T(8,128)(2,1)S(1)}, u32[]{:S(2)}, u32[]{:S(2)}) collective-permute-start(bf16[512,256]{1,0:T(8,128)(2,1)} %get-tuple-element.211), channel_id=1, source_target_pairs={{2,0},{4,2},{6,4},{3,1},{5,3},{7,5},{10,8},{12,10},{14,12},{11,9},... | collective-permute-start | bytes 786440 | tf_op jit(solution)/shard_map/ppermute | solution.py:1114
  359.5 82.7 %all-to-all-start.1 = ((bf16[4,128,2304]{2,1,0:T(8,128)(2,1)}), bf16[4,128,2304]{2,1,0:T(8,128)(2,1)S(1)}, u32[]{:S(2)}, u32[]{:S(2)}) async-start(bf16[4,128,2304]{2,1,0:T(8,128)(2,1)} %bitcast.72), calls=%async_computation.5 | async-start | bytes 4718592 | tf_op jit(solution)/shard_map/all_to_all | solution.py:1065
  365.4 133.2 %reduce-scatter.14.cloned.1.call-start = ((), (), s32[]{:S(2)}) async-start(), calls=%async_computation.13 | async-start | bytes 2949120 | tf_op jit(solution)/shard_map/reduce_scatter | solution.py:1133
  385.4 18.1 %collective-permute-start.19 = (bf16[512,1280]{1,0:T(8,128)(2,1)}, bf16[512,1280]{1,0:T(8,128)(2,1)}, u32[]{:S(2)}, u32[]{:S(2)}) collective-permute-start(bf16[512,1280]{1,0:T(8,128)(2,1)} %constant_dynamic-update-slice_fusion), channel_id=1, source_target_pairs={{0,8},{8,0},{16,24},{24,16},{1,9},{9,1},{17,25},{25,17},{2,10},{10... | collective-permute-start | bytes 3932168 | tf_op jit(solution)/shard_map/ppermute | solution.py:93
  390.2 25.9 %collective-permute-start.20 = (bf16[512,1024]{1,0:T(8,128)(2,1)}, bf16[512,1024]{1,0:T(8,128)(2,1)S(1)}, u32[]{:S(2)}, u32[]{:S(2)}) collective-permute-start(bf16[512,1024]{1,0:T(8,128)(2,1)} %dynamic-slice_bitcast_fusion.1), channel_id=1, source_target_pairs={{0,1},{1,0},{2,3},{3,2},{4,5},{5,4},{6,7},{7,6},{8,9},{9,8},{10,11... | collective-permute-start | bytes 3145736 | tf_op jit(solution)/shard_map/ppermute | solution.py:93
  409.2 33.0 %collective-permute-start.23 = (bf16[512,1280]{1,0:T(8,128)(2,1)}, bf16[512,1280]{1,0:T(8,128)(2,1)}, u32[]{:S(2)}, u32[]{:S(2)}) collective-permute-start(bf16[512,1280]{1,0:T(8,128)(2,1)} %get-tuple-element.236), channel_id=1, source_target_pairs={{0,16},{8,24},{16,0},{24,8},{1,17},{9,25},{17,1},{25,9},{2,18},{10... | collective-permute-start | bytes 3932168 | tf_op jit(solution)/shard_map/ppermute | solution.py:93
  454.8 68.5 %all-to-all-start.2 = ((bf16[4,128,2432]{2,1,0:T(8,128)(2,1)}), bf16[4,128,2432]{2,1,0:T(8,128)(2,1)S(1)}, u32[]{:S(2)}, u32[]{:S(2)}) async-start(bf16[4,128,2432]{2,1,0:T(8,128)(2,1)} %bitcast.40), calls=%async_computation.6 | async-start | bytes 4980736 | tf_op jit(solution)/shard_map/all_to_all | solution.py:1065
  460.3 31.5 %collective-permute-start.21 = (bf16[512,1024]{1,0:T(8,128)(2,1)}, bf16[512,1024]{1,0:T(8,128)(2,1)S(1)}, u32[]{:S(2)}, u32[]{:S(2)}) collective-permute-start(bf16[512,1024]{1,0:T(8,128)(2,1)} %dynamic-slice_bitcast_fusion), channel_id=1, source_target_pairs={{0,1},{1,0},{2,3},{3,2},{4,5},{5,4},{6,7},{7,6},{8,9},{9,8},{10,11... | collective-permute-start | bytes 3145736 | tf_op jit(solution)/shard_map/ppermute | solution.py:93
  462.1 28.5 %collective-permute-start.22 = (f32[512,128]{1,0:T(8,128)}, f32[512,128]{1,0:T(8,128)S(1)}, u32[]{:S(2)}, u32[]{:S(2)}) collective-permute-start(f32[512,128]{1,0:T(8,128)} %get-tuple-element.235), channel_id=1, source_target_pairs={{0,1},{1,0},{2,3},{3,2},{4,5},{5,4},{6,7},{7,6},{8,9},{9,8},{10,11... | collective-permute-start | bytes 786440 | tf_op jit(solution)/shard_map/ppermute | solution.py:93
  (46 other events, 420.9 us)
Sparse Core Ops, SparseCore 0:
  58.9 35.5 all-gather.1
  139.2 48.2 reduce-scatter.5
  189.9 59.9 reduce-scatter.7
  263.6 79.6 reduce-scatter.9
  345.5 59.9 reduce-scatter.11
  423.2 55.5 reduce-scatter.13

commit v5 on v4

--- a/solution.py
+++ b/solution.py
@@ -1095,10 +1095,6 @@
     d_attn_mate, a_one_mate = mate(d_attn_t), mate(gate(a_one_t))
     out_groups = [(d_attn_t, d_attn_mate, [(o_own[None], o_mate[None], 0)])]
     out_parts = (o_own.shape[1] // FT,)
-    (first_out,) = outer(
-        sc_send, out_groups, block_rows, 0, out_parts, "out_send", deps=(a_one_mate,)
-    )
-    got_out = swap(first_out, "dp", 2)
     to_other = gate(lax.dynamic_index_in_dim(branch, 1 - h, 0, keepdims=False))
     branch_oth = swap(to_other, "head", 1)
 
@@ -1114,9 +1110,8 @@
             lax.ppermute(part, "blk", [(i, i - s) for i in range(s, nblk)]) if s else part
         )
         if s == min(1, nblk - 1):
-            (keep_out,) = outer(
-                sc_keep, out_groups, block_rows, 0, out_parts, "out_keep", got_out,
-                deps=(all1,) + tuple(parts[: nblk - 1]),
+            (sum_out,) = both_halves(
+                out_groups, out_parts, "out", deps=(all1, a_one_mate) + tuple(parts[: nblk - 1])
             )
             all2 = over_blk(gate(sum2))
     d_q = state[0]
@@ -1179,7 +1174,7 @@
     extra = jnp.concatenate(
         [coarse, fine, jnp.zeros((block_rows, PAIR - 12), BF16)], axis=1
     )
-    all_qkv = over_blk(jnp.concatenate([keep_qkv, keep_out, extra], axis=1))
+    all_qkv = over_blk(jnp.concatenate([keep_qkv, sum_out, extra], axis=1))
     grad_down, grad_gate, grad_up = finish([(all0.reshape(-1, all0.shape[2]), nblk), (all1, nblk), (all2, nblk), (sum3, 1)])
     qw, kvw = w_query.shape[1], w_key.shape[1]
     sum_query, sum_key, sum_value, sum_out, small = finish_rows(

time: 548 us -> 560 us (1.022)
  waiting for transfers between devices: 177 us -> 196 us
    ppermute x21 -> x20, waiting for transfers between devices: 101 us -> 116 us  [swap(): return lax.ppermute(x, axis, [(i, i ^ bit) for i in range(n)])]
    all_to_all x3, waiting for transfers between devices: 19.4 us -> 27.3 us  [over_blk(): return lax.all_to_all(x, 'blk', split_axis=0, concat_axis=0, tiled=True)]
    pallas_call x30 -> x29, Pallas kernels: 254 us -> 251 us  [launch(): pl.pallas_call(wrapped, grid_spec=pltpu.PrefetchScalarGridSpec(num_scalar...]
    ppermute x21 -> x20, starting transfers between devices: 13.4 us -> 12.3 us  [swap(): return lax.ppermute(x, axis, [(i, i ^ bit) for i in range(n)])]
    unnamed x70 -> x72, local copies, waits for them, and re-layouts: 16.4 us -> 15.4 us
  transfers between devices with their start and end apart: 36 -> 36, of which waited for: 14 -> 14; matrix products, arithmetic and copies ran while one was open for 7% -> 6% of each run, Pallas kernels for 45% -> 44%
where the time goes in v5:
time: 560 us; the launch traced here: 550 us
  Pallas kernels  251 us (45%)
  waiting for transfers between devices  196 us (35%)
  starting transfers between devices  36.9 us (7%)
  local copies, waits for them, and re-layouts  30.7 us (5%)
  between operations  17.8 us (3%)
  other arithmetic  17.4 us (3%)
    pallas_call x29, Pallas kernels, launch(): pl.pallas_call(wrapped, grid_spec=pltpu.PrefetchScalarGridSpec(num_scalar...  251 us
    ppermute x20, waiting for transfers between devices, swap(): return lax.ppermute(x, axis, [(i, i ^ bit) for i in range(n)])  116 us
    ppermute x3, waiting for transfers between devices, body(): lax.ppermute(part, 'blk', [(i, i - s) for i in range(s, nblk)])  42.2 us
    all_to_all x3, waiting for transfers between devices, over_blk(): return lax.all_to_all(x, 'blk', split_axis=0, concat_axis=0, tiled=True)  27.3 us
    unnamed x72, local copies, waits for them, and re-layouts  15.4 us
    all_to_all x3, starting transfers between devices, over_blk(): return lax.all_to_all(x, 'blk', split_axis=0, concat_axis=0, tiled=True)  14.8 us
    ppermute x20, starting transfers between devices, swap(): return lax.ppermute(x, axis, [(i, i ^ bit) for i in range(n)])  12.3 us
  transfers between devices with their start and end apart: 36, of which 14 were waited for; matrix products, arithmetic and copies ran while one was open for 6% of the time, Pallas kernels for 44%

profile of v5, /device:TPU:0, one launch (start us, length us, event | category | flops | bytes accessed | tf_op | source)
XLA Modules:
  0.0 550.5 jit_solution(6279285645754918777)
XLA Ops:
  15.7 18.0 %collective-permute-done.refs_2_ = bf16[512,1024]{1,0:T(8,128)(2,1)} collective-permute-done((bf16[512,1024]{1,0:T(8,128)(2,1)}, bf16[512,1024]{1,0:T(8,128)(2,1)}, u32[]{:S(2)}, u32[]{:S(2)}) %collective-permute-start) | collective-permute-done | bytes 1048608 | tf_op jit(solution)/shard_map/ppermute | solution.py:93
  37.7 6.9 %project.1 = (bf16[512,2048]{1,0:T(8,128)(2,1)}, bf16[512,2048]{1,0:T(8,128)(2,1)}, bf16[512,1024]{1,0:T(8,128)(2,1)}, bf16[512,256]{1,0:T(8,128)(2,1)}, f32[512,128]{1,0:T(8,128)}, /*index=5*/f32[8,128]{1,0:T(8,128)}) custom-call(s32[1]{0:T(128)} %bitcast.1.refs_0_, bf16[512,1024]{1,0:T(8,128)(2,1)S(1)} %bitcast.64, ...), custom_call_target="tpu_custom_call" | custom-call | flops 1073741824 | bytes 7130316 | tf_op jit(solution)/shard_map/project/pallas_call | solution.py:61
  48.8 7.6 %attend0.1 = (f32[1024,512]{1,0:T(8,128)S(1)}, f32[8,8,512]{2,1,0:T(8,128)S(1)}, f32[8,128]{1,0:T(8,128)}) custom-call(s32[1]{0:T(128)} %bitcast.refs_0_, bf16[512,1024]{1,0:T(8,128)(2,1)} %get-tuple-element.135.refs_1_, bf16[512,256]{1,0:T(8,128)(2,1)} %get-tuple-element.136.refs_2_.refs_5_, s32[1,1,512]{2,1,0:T(1,128)} %bitcast.87, ...), custom_call_target="tpu_custom_call" | custom-call | flops 2576980480 | bytes 4194304 | tf_op jit(solution)/shard_map/attend0/pallas_call | solution.py:61
  69.4 6.5 %own_part.1 = (f32[4,512,512]{2,1,0:T(8,128)}, f32[8,128]{1,0:T(8,128)}) custom-call(bf16[512,1024]{1,0:T(8,128)(2,1)} %get-tuple-element.158.refs_0_.refs_6_, bf16[2048,1024]{1,0:T(8,128)(2,1)} %refs_5_.3, f32[8,128]{1,0:T(8,128)} %get-tuple-element.159.refs_2_), custom_call_target="tpu_custom_call" | custom-call | flops 429496736 | bytes 1677721 | tf_op jit(solution)/shard_map/own_part/pallas_call | solution.py:61
  75.8 10.0 %collective-permute-done.6 = bf16[512,1024]{1,0:T(8,128)(2,1)} collective-permute-done((bf16[512,1024]{1,0:T(8,128)(2,1)S(1)}, bf16[512,1024]{1,0:T(8,128)(2,1)}, u32[]{:S(2)}, u32[]{:S(2)}) %collective-permute-start.6) | collective-permute-done | bytes 1048608 | tf_op jit(solution)/shard_map/ppermute | solution.py:93
  90.1 15.6 %collective-permute-done.5.refs_1_ = bf16[512,1024]{1,0:T(8,128)(2,1)} collective-permute-done((bf16[512,1024]{1,0:T(8,128)(2,1)}, bf16[512,1024]{1,0:T(8,128)(2,1)}, u32[]{:S(2)}, u32[]{:S(2)}) %collective-permute-start.5) | collective-permute-done | bytes 1048608 | tf_op jit(solution)/shard_map/ppermute | solution.py:93
  105.7 11.3 %merge.1 = (f32[4,512,512]{2,1,0:T(8,128)}, bf16[512,2048]{1,0:T(8,128)(2,1)}, bf16[2048,512]{1,0:T(8,128)(2,1)}, f32[512,128]{1,0:T(8,128)}, f32[512,128]{1,0:T(8,128)}, /*index=5*/f32[8,128]{1,0:T(8,128)}) custom-call(f32[4,512,512]{2,1,0:T(8,128)} %get-tuple-element.160.refs_0_, bf16[512,1024]{1,0:T(8,128)(2,1)} %collective-permute-done.5.refs_1_, ...), custom_call_target="tpu_custom_call" | custom-call | flops 2576980480 | bytes 8388608 | tf_op jit(solution)/shard_map/merge/pallas_call | solution.py:61
  117.1 8.2 %units0.1 = (bf16[3,512,512]{2,1,0:T(8,128)(2,1)}, f32[8,128]{1,0:T(8,128)}) custom-call(bf16[512,2048]{1,0:T(8,128)(2,1)} %get-tuple-element.168.refs_0_, bf16[512,2048]{1,0:T(8,128)(2,1)} %copy-done, bf16[2048,2816]{1,0:T(8,128)(2,1)} %refs_9_.1, bf16[2048,2816]{1,0:T(8,128)(2,1)} %refs_10_.1, bf16[2048,2816]{1,0:T(8,128)(2,1)} %refs_11_.1, ...), custom_call_target="tpu_custom_call" | custom-call | flops 2147483648 | bytes 2516582 | tf_op jit(solution)/shard_map/units0/pallas_call | solution.py:61
  130.4 8.7 %mlp0.1 = (bf16[1024,1536]{1,0:T(8,128)(2,1)}, f32[8,128]{1,0:T(8,128)}) custom-call(s32[2]{0:T(128)S(1)} %pad_add_fusion.refs_0_, bf16[2048,512]{1,0:T(8,128)(2,1)} %get-tuple-element.171.refs_1_.refs_2_, bf16[2048,512]{1,0:T(8,128)(2,1)} %get-tuple-element.171.refs_1_.refs_2_, bf16[2048,512]{1,0:T(8,128)(2,1)} %collective-permute-done.7.refs_3_.refs_4_, ...), custom_call_target="tpu_custom_call" | custom-call | flops 2576980480 | bytes 2516582 | tf_op jit(solution)/shard_map/mlp0/pallas_call | solution.py:61
  139.1 10.4 %units2.1 = (bf16[3,512,768]{2,1,0:T(8,128)(2,1)}, f32[8,128]{1,0:T(8,128)}) custom-call(bf16[512,2048]{1,0:T(8,128)(2,1)} %get-tuple-element.168.refs_0_, bf16[512,2048]{1,0:T(8,128)(2,1)} %copy-done, bf16[2048,2816]{1,0:T(8,128)(2,1)} %refs_9_.1, bf16[2048,2816]{1,0:T(8,128)(2,1)} %refs_10_.1, bf16[2048,2816]{1,0:T(8,128)(2,1)} %refs_11_.1, ...), custom_call_target="tpu_custom_call" | custom-call | flops 3221225472 | bytes 3774873 | tf_op jit(solution)/shard_map/units2/pallas_call | solution.py:61
  149.9 17.0 %units5.1 = (bf16[3,512,1536]{2,1,0:T(8,128)(2,1)}, f32[8,128]{1,0:T(8,128)}) custom-call(bf16[512,2048]{1,0:T(8,128)(2,1)} %get-tuple-element.168.refs_0_, bf16[512,2048]{1,0:T(8,128)(2,1)} %copy-done, bf16[2048,2816]{1,0:T(8,128)(2,1)} %refs_9_.1, bf16[2048,2816]{1,0:T(8,128)(2,1)} %refs_10_.1, bf16[2048,2816]{1,0:T(8,128)(2,1)} %refs_11_.1, ...), custom_call_target="tpu_custom_call" | custom-call | flops 6442450944 | bytes 7549747 | tf_op jit(solution)/shard_map/units5/pallas_call | solution.py:61
  168.5 10.3 %mlp1.1 = (bf16[1024,2304]{1,0:T(8,128)(2,1)}, f32[8,128]{1,0:T(8,128)}) custom-call(s32[2]{0:T(128)S(1)} %pad_add_fusion.refs_0_, bf16[2048,512]{1,0:T(8,128)(2,1)} %get-tuple-element.171.refs_1_.refs_2_, bf16[2048,512]{1,0:T(8,128)(2,1)} %get-tuple-element.171.refs_1_.refs_2_, bf16[2048,512]{1,0:T(8,128)(2,1)} %collective-permute-done.7.refs_3_.refs_4_, ...), custom_call_target="tpu_custom_call" | custom-call | flops 3865470464 | bytes 3774873 | tf_op jit(solution)/shard_map/mlp1/pallas_call | solution.py:61
  179.2 8.3 %reduce-scatter.7.cloned.1.call-done.refs_12_ = bf16[512,1536]{1,0:T(8,128)(2,1)} async-done(((bf16[1024,1536]{1,0:T(8,128)(2,1)}), bf16[512,1536]{1,0:T(8,128)(2,1)}) %reduce-scatter.7.cloned.1.call-update) | async-done | bytes 1572880 | tf_op jit(solution)/shard_map/reduce_scatter | solution.py:1058
  187.5 59.4 %exchange.1 = (f32[512,2048]{1,0:T(8,128)}, bf16[2,512,1024]{2,1,0:T(8,128)(2,1)}, bf16[4,128,1536]{2,1,0:T(8,128)(2,1)}, f32[8,128]{1,0:T(8,128)}) custom-call(bf16[3,512,512]{2,1,0:T(8,128)(2,1)} %get-tuple-element.170.refs_5_.refs_11_.refs_13_.refs_0_.refs_3_.refs_6_, ...), custom_call_target="tpu_custom_call" | custom-call | flops 7086695936 | bytes 13841203 | tf_op jit(solution)/shard_map/exchange/pallas_call | solution.py:61
  246.9 16.7 %mlp2.1 = (bf16[1024,2304]{1,0:T(8,128)(2,1)}, bf16[1024,2304]{1,0:T(8,128)(2,1)}, f32[8,128]{1,0:T(8,128)}) custom-call(s32[2]{0:T(128)S(1)} %pad_add_fusion.refs_0_, bf16[2048,512]{1,0:T(8,128)(2,1)} %get-tuple-element.171.refs_1_.refs_2_, bf16[2048,512]{1,0:T(8,128)(2,1)} %get-tuple-element.171.refs_1_.refs_2_, ...), custom_call_target="tpu_custom_call" | custom-call | flops 7730940928 | bytes 7549747 | tf_op jit(solution)/shard_map/mlp2/pallas_call | solution.py:61
  268.1 10.5 %stream.1 = (f32[512,2048]{1,0:T(8,128)}, bf16[2048,512]{1,0:T(8,128)(2,1)}, bf16[512,1024]{1,0:T(8,128)(2,1)}, f32[1,2048]{1,0:T(1,128)}, f32[8,128]{1,0:T(8,128)}) custom-call(f32[512,2048]{1,0:T(8,128)} %get-tuple-element.181.refs_0_, f32[4,512,512]{2,1,0:T(8,128)} %get-tuple-element.224.refs_1_, f32[512,128]{1,0:T(8,128)} %get-tuple-element.182.refs_2_, ...), custom_call_target="tpu_custom_call" | custom-call | flops 858993472 | bytes 10066329 | tf_op jit(solution)/shard_map/stream/pallas_call | solution.py:61
  296.8 18.4 %collective-permute-done.15.refs_10_.refs_0_ = bf16[512,256]{1,0:T(8,128)(2,1)S(1)} collective-permute-done((bf16[512,256]{1,0:T(8,128)(2,1)}, bf16[512,256]{1,0:T(8,128)(2,1)S(1)}, u32[]{:S(2)}, u32[]{:S(2)}) %collective-permute-start.15) | collective-permute-done | bytes 262176 | tf_op jit(solution)/shard_map/ppermute | solution.py:1110
  315.2 23.8 %collective-permute-done.16.refs_11_.refs_1_ = bf16[512,256]{1,0:T(8,128)(2,1)S(1)} collective-permute-done((bf16[512,256]{1,0:T(8,128)(2,1)}, bf16[512,256]{1,0:T(8,128)(2,1)S(1)}, u32[]{:S(2)}, u32[]{:S(2)}) %collective-permute-start.16) | collective-permute-done | bytes 262176 | tf_op jit(solution)/shard_map/ppermute | solution.py:1110
  341.3 6.6 %out.1 = (bf16[1024,1024]{1,0:T(8,128)(2,1)}, f32[8,128]{1,0:T(8,128)}) custom-call(s32[2]{0:T(128)S(1)} %pad_add_fusion.refs_0_, bf16[2048,512]{1,0:T(8,128)(2,1)} %get-tuple-element.201.refs_1_.refs_2_, bf16[2048,512]{1,0:T(8,128)(2,1)} %get-tuple-element.201.refs_1_.refs_2_, bf16[2048,512]{1,0:T(8,128)(2,1)} %collective-permute-done.12.refs_3_.refs_4_, ...), custom_call_target="tpu_custom_call" | custom-call | flops 1717986944 | bytes 1677721 | tf_op jit(solution)/shard_map/out/pallas_call | solution.py:61
  353.9 16.0 %attend_back0.1 = (bf16[512,1024]{1,0:T(8,128)(2,1)}, bf16[512,256]{1,0:T(8,128)(2,1)}, f32[8,128]{1,0:T(8,128)}) custom-call(s32[1]{0:T(128)} %bitcast.refs_0_, bf16[512,1024]{1,0:T(8,128)(2,1)} %get-tuple-element.135.refs_1_, bf16[512,1024]{1,0:T(8,128)(2,1)} %get-tuple-element.187.refs_2_, f32[8,8,512]{2,1,0:T(8,128)} %copy-done.11, ...), custom_call_target="tpu_custom_call" | custom-call | flops 5798205952 | bytes 4194304 | tf_op jit(solution)/shard_map/attend_back0/pallas_call | solution.py:61
  377.5 10.4 %entry.1 = (bf16[2,512,1024]{2,1,0:T(8,128)(2,1)}, f32[1,2048]{1,0:T(1,128)}, f32[512,128]{1,0:T(8,128)}, f32[8,128]{1,0:T(8,128)}) custom-call(bf16[512,1024]{1,0:T(8,128)(2,1)} %get-tuple-element.210.refs_0_, bf16[512,256]{1,0:T(8,128)(2,1)} %get-tuple-element.213.refs_1_, bf16[2048,1024]{1,0:T(8,128)(2,1)} %refs_2_.7, bf16[2048,128]{1,0:T(8,128)(2,1)} %refs_3_.7, ...), custom_call_target="tpu_custom_call" | custom-call | flops 1073741824 | bytes 8388608 | tf_op jit(solution)/shard_map/entry/pallas_call | solution.py:61
  411.6 32.7 %collective-permute-done.25 = f32[33,128]{1,0:T(8,128)S(1)} collective-permute-done((f32[33,128]{1,0:T(8,128)S(1)}, f32[33,128]{1,0:T(8,128)S(1)}, u32[]{:S(2)}, u32[]{:S(2)}) %collective-permute-start.25) | collective-permute-done | bytes 16928 | tf_op jit(solution)/shard_map/ppermute | solution.py:93
  465.0 28.5 %collective-permute-done.21 = f32[512,128]{1,0:T(8,128)S(1)} collective-permute-done((f32[512,128]{1,0:T(8,128)}, f32[512,128]{1,0:T(8,128)S(1)}, u32[]{:S(2)}, u32[]{:S(2)}) %collective-permute-start.21) | collective-permute-done | bytes 262176 | tf_op jit(solution)/shard_map/ppermute | solution.py:93
  508.3 27.3 %all-to-all-done.2.refs_0_ = bf16[4,128,2432]{2,1,0:T(8,128)(2,1)S(1)} async-done(((bf16[4,128,2432]{2,1,0:T(8,128)(2,1)}), bf16[4,128,2432]{2,1,0:T(8,128)(2,1)S(1)}, u32[]{:S(2)}, u32[]{:S(2)}) %all-to-all-start.2) | async-done | bytes 2490400 | tf_op jit(solution)/shard_map/all_to_all | solution.py:1065
  (200 shorter events, 143.5 us)
Async XLA Ops:
  7.2 98.5 %all-gather.2.cloned.1.call-start = ((), (), s32[]{:S(2)}) async-start(), calls=%async_computation.9 | async-start | bytes 5242880 | tf_op jit(solution)/shard_map/all_gather | solution.py:1032
  7.2 26.5 %collective-permute-start = (bf16[512,1024]{1,0:T(8,128)(2,1)}, bf16[512,1024]{1,0:T(8,128)(2,1)}, u32[]{:S(2)}, u32[]{:S(2)}) collective-permute-start(bf16[512,1024]{1,0:T(8,128)(2,1)} %bitcast.63), channel_id=1, source_target_pairs={{0,1},{1,0},{2,3},{3,2},{4,5},{5,4},{6,7},{7,6},{8,9},{9,8},{10,11... | collective-permute-start | bytes 3145736 | tf_op jit(solution)/shard_map/ppermute | solution.py:93
  58.8 128.7 %reduce-scatter.7.cloned.1.call-start = ((), (), s32[]{:S(2)}) async-start(), calls=%async_computation.10 | async-start | bytes 4718592 | tf_op jit(solution)/shard_map/reduce_scatter | solution.py:1058
  59.5 26.3 %collective-permute-start.6 = (bf16[512,1024]{1,0:T(8,128)(2,1)S(1)}, bf16[512,1024]{1,0:T(8,128)(2,1)}, u32[]{:S(2)}, u32[]{:S(2)}) collective-permute-start(bf16[512,1024]{1,0:T(8,128)(2,1)S(1)} %bitcast.73), channel_id=1, source_target_pairs={{0,1},{1,0},{2,3},{3,2},{4,5},{5,4},{6,7},{7,6},{8,9},{9,8},{10,11... | collective-permute-start | bytes 3145736 | tf_op jit(solution)/shard_map/ppermute | solution.py:93
  67.8 37.8 %collective-permute-start.5 = (bf16[512,1024]{1,0:T(8,128)(2,1)}, bf16[512,1024]{1,0:T(8,128)(2,1)}, u32[]{:S(2)}, u32[]{:S(2)}) collective-permute-start(bf16[512,1024]{1,0:T(8,128)(2,1)} %get-tuple-element.158.refs_0_.refs_6_), channel_id=1, source_target_pairs={{0,1},{1,0},{2,3},{3,2},{4,5},{5,4},{6,7},{7,6},{8,9},{9,8},{10,11... | collective-permute-start | bytes 3145736 | tf_op jit(solution)/shard_map/ppermute | solution.py:93
  90.1 35.7 %collective-permute-start.7 = (bf16[2048,512]{1,0:T(8,128)(2,1)}, bf16[2048,512]{1,0:T(8,128)(2,1)}, u32[]{:S(2)}, u32[]{:S(2)}) collective-permute-start(bf16[2048,512]{1,0:T(8,128)(2,1)} %get-tuple-element.171.refs_1_.refs_2_), channel_id=1, source_target_pairs={{0,8},{8,0},{16,24},{24,16},{1,9},{9,1},{17,25},{25,17},{2,10},{10... | collective-permute-start | bytes 6291464 | tf_op jit(solution)/shard_map/ppermute | solution.py:93
  139.1 125.1 %reduce-scatter.9.cloned.1.call-start = ((), (), s32[]{:S(2)}) async-start(), calls=%async_computation.11 | async-start | bytes 7077888 | tf_op jit(solution)/shard_map/reduce_scatter | solution.py:1058
  178.8 169.2 %reduce-scatter.11.cloned.1.call-start = ((), (), s32[]{:S(2)}) async-start(), calls=%async_computation.12 | async-start | bytes 7077888 | tf_op jit(solution)/shard_map/reduce_scatter | solution.py:1058
  178.9 68.1 %collective-permute-start.11 = (bf16[3,512,1536]{2,1,0:T(8,128)(2,1)}, bf16[3,512,1536]{2,1,0:T(8,128)(2,1)}, u32[]{:S(2)}, u32[]{:S(2)}) collective-permute-start(bf16[3,512,1536]{2,1,0:T(8,128)(2,1)} %get-tuple-element.177.refs_2_.refs_5_.refs_8_.refs_11_.refs_13_), channel_id=1, source_target_pairs={{0,8},{8,0},{16,24},{24,16},{1,9},{9,1},{17,25},{25,17},{2,10},{10... | collective-permute-start | bytes 14155784 | tf_op jit(solution)/shard_map/ppermute | solution.py:93
  263.6 132.8 %reduce-scatter.13.cloned.1.call-start = ((), (), s32[]{:S(2)}) async-start(), calls=%async_computation.13 | async-start | bytes 7077888 | tf_op jit(solution)/shard_map/reduce_scatter | solution.py:1058
  264.2 75.5 %all-to-all-start = ((bf16[4,128,2304]{2,1,0:T(8,128)(2,1)}), bf16[4,128,2304]{2,1,0:T(8,128)(2,1)S(1)}, u32[]{:S(2)}, u32[]{:S(2)}) async-start(bf16[4,128,2304]{2,1,0:T(8,128)(2,1)} %bitcast.72), calls=%async_computation.3 | async-start | bytes 4718592 | tf_op jit(solution)/shard_map/all_to_all | solution.py:1065
  268.1 184.5 %reduce-scatter.15.cloned.1.call-start = ((), (), s32[]{:S(2)}) async-start(), calls=%async_computation.14 | async-start | bytes 3145728 | tf_op jit(solution)/shard_map/reduce_scatter | solution.py:1058
  278.6 60.5 %collective-permute-start.12 = (bf16[2048,512]{1,0:T(8,128)(2,1)}, bf16[2048,512]{1,0:T(8,128)(2,1)}, u32[]{:S(2)}, u32[]{:S(2)}) collective-permute-start(bf16[2048,512]{1,0:T(8,128)(2,1)} %get-tuple-element.201.refs_1_.refs_2_), channel_id=1, source_target_pairs={{0,8},{8,0},{16,24},{24,16},{1,9},{9,1},{17,25},{25,17},{2,10},{10... | collective-permute-start | bytes 6291464 | tf_op jit(solution)/shard_map/ppermute | solution.py:93
  278.6 61.2 %collective-permute-start.14 = (bf16[2048,512]{1,0:T(8,128)(2,1)}, bf16[2048,512]{1,0:T(8,128)(2,1)}, u32[]{:S(2)}, u32[]{:S(2)}) collective-permute-start(bf16[2048,512]{1,0:T(8,128)(2,1)} %get-tuple-element.204.refs_1_), channel_id=1, source_target_pairs={{0,8},{8,0},{16,24},{24,16},{1,9},{9,1},{17,25},{25,17},{2,10},{10... | collective-permute-start | bytes 6291464 | tf_op jit(solution)/shard_map/ppermute | solution.py:93
  285.2 30.0 %collective-permute-start.15 = (bf16[512,256]{1,0:T(8,128)(2,1)}, bf16[512,256]{1,0:T(8,128)(2,1)S(1)}, u32[]{:S(2)}, u32[]{:S(2)}) collective-permute-start(bf16[512,256]{1,0:T(8,128)(2,1)} %get-tuple-element.205), channel_id=1, source_target_pairs={{6,0},{7,1},{14,8},{15,9},{22,16},{23,17},{30,24},{31,25}} | collective-permute-start | bytes 786440 | tf_op jit(solution)/shard_map/ppermute | solution.py:1110
  290.4 48.6 %collective-permute-start.16 = (bf16[512,256]{1,0:T(8,128)(2,1)}, bf16[512,256]{1,0:T(8,128)(2,1)S(1)}, u32[]{:S(2)}, u32[]{:S(2)}) collective-permute-start(bf16[512,256]{1,0:T(8,128)(2,1)} %get-tuple-element.206), channel_id=1, source_target_pairs={{4,0},{6,2},{5,1},{7,3},{12,8},{14,10},{13,9},{15,11},{20,16},{22,... | collective-permute-start | bytes 786440 | tf_op jit(solution)/shard_map/ppermute | solution.py:1110
  295.5 43.6 %collective-permute-start.17 = (bf16[512,256]{1,0:T(8,128)(2,1)}, bf16[512,256]{1,0:T(8,128)(2,1)S(1)}, u32[]{:S(2)}, u32[]{:S(2)}) collective-permute-start(bf16[512,256]{1,0:T(8,128)(2,1)} %get-tuple-element.207), channel_id=1, source_target_pairs={{2,0},{4,2},{6,4},{3,1},{5,3},{7,5},{10,8},{12,10},{14,12},{11,9},... | collective-permute-start | bytes 786440 | tf_op jit(solution)/shard_map/ppermute | solution.py:1110
  348.0 97.0 %all-to-all-start.1 = ((bf16[4,128,2304]{2,1,0:T(8,128)(2,1)}), bf16[4,128,2304]{2,1,0:T(8,128)(2,1)S(1)}, u32[]{:S(2)}, u32[]{:S(2)}) async-start(bf16[4,128,2304]{2,1,0:T(8,128)(2,1)} %bitcast.71), calls=%async_computation.5 | async-start | bytes 4718592 | tf_op jit(solution)/shard_map/all_to_all | solution.py:1065
  353.9 149.2 %reduce-scatter.17.cloned.1.call-start = ((), (), s32[]{:S(2)}) async-start(), calls=%async_computation.15 | async-start | bytes 2949120 | tf_op jit(solution)/shard_map/reduce_scatter | solution.py:1128
  396.4 48.6 %collective-permute-start.22 = (bf16[512,1280]{1,0:T(8,128)(2,1)}, bf16[512,1280]{1,0:T(8,128)(2,1)}, u32[]{:S(2)}, u32[]{:S(2)}) collective-permute-start(bf16[512,1280]{1,0:T(8,128)(2,1)} %get-tuple-element.232), channel_id=1, source_target_pairs={{0,16},{8,24},{16,0},{24,8},{1,17},{9,25},{17,1},{25,9},{2,18},{10... | collective-permute-start | bytes 3932168 | tf_op jit(solution)/shard_map/ppermute | solution.py:93
  411.1 33.2 %collective-permute-start.25 = (f32[33,128]{1,0:T(8,128)S(1)}, f32[33,128]{1,0:T(8,128)S(1)}, u32[]{:S(2)}, u32[]{:S(2)}) collective-permute-start(f32[33,128]{1,0:T(8,128)S(1)} %fusion.19), channel_id=1, source_target_pairs={{0,16},{8,24},{16,0},{24,8},{1,17},{9,25},{17,1},{25,9},{2,18},{10... | collective-permute-start | bytes 50696 | tf_op jit(solution)/shard_map/ppermute | solution.py:93
  457.8 77.9 %all-to-all-start.2 = ((bf16[4,128,2432]{2,1,0:T(8,128)(2,1)}), bf16[4,128,2432]{2,1,0:T(8,128)(2,1)S(1)}, u32[]{:S(2)}, u32[]{:S(2)}) async-start(bf16[4,128,2432]{2,1,0:T(8,128)(2,1)} %bitcast.40), calls=%async_computation.7 | async-start | bytes 4980736 | tf_op jit(solution)/shard_map/all_to_all | solution.py:1065
  462.9 31.7 %collective-permute-start.20 = (bf16[512,1024]{1,0:T(8,128)(2,1)}, bf16[512,1024]{1,0:T(8,128)(2,1)S(1)}, u32[]{:S(2)}, u32[]{:S(2)}) collective-permute-start(bf16[512,1024]{1,0:T(8,128)(2,1)} %dynamic-slice_bitcast_fusion), channel_id=1, source_target_pairs={{0,1},{1,0},{2,3},{3,2},{4,5},{5,4},{6,7},{7,6},{8,9},{9,8},{10,11... | collective-permute-start | bytes 3145736 | tf_op jit(solution)/shard_map/ppermute | solution.py:93
  464.4 29.1 %collective-permute-start.21 = (f32[512,128]{1,0:T(8,128)}, f32[512,128]{1,0:T(8,128)S(1)}, u32[]{:S(2)}, u32[]{:S(2)}) collective-permute-start(f32[512,128]{1,0:T(8,128)} %get-tuple-element.231), channel_id=1, source_target_pairs={{0,1},{1,0},{2,3},{3,2},{4,5},{5,4},{6,7},{7,6},{8,9},{9,8},{10,11... | collective-permute-start | bytes 786440 | tf_op jit(solution)/shard_map/ppermute | solution.py:93
  (47 other events, 516.2 us)
Sparse Core Ops, SparseCore 0:
  58.9 35.5 all-gather.1
  139.2 48.2 reduce-scatter.6
  189.9 59.9 reduce-scatter.8
  263.7 57.1 reduce-scatter.10
  323.2 59.9 reduce-scatter.12
  385.3 48.1 reduce-scatter.14
  435.9 67.1 reduce-scatter.16

commit v6 on v5

--- a/solution.py
+++ b/solution.py
@@ -1110,8 +1110,9 @@
             lax.ppermute(part, "blk", [(i, i - s) for i in range(s, nblk)]) if s else part
         )
         if s == min(1, nblk - 1):
-            (sum_out,) = both_halves(
-                out_groups, out_parts, "out", deps=(all1, a_one_mate) + tuple(parts[: nblk - 1])
+            (both_out,) = outer(
+                sc_both, out_groups, block_rows, 0, out_parts, "out",
+                deps=(all1, a_one_mate) + tuple(parts[: nblk - 1]),
             )
             all2 = over_blk(gate(sum2))
     d_q = state[0]
@@ -1123,9 +1124,13 @@
     )
     qkv_groups = [(a_one_t, a_one_mate, [(d_qkv[None], d_qkv_mate[None], 0)])]
     qkv_parts = (d_qkv.shape[1] // FT,)
-    (first_qkv,) = outer(sc_send, qkv_groups, block_rows, 0, qkv_parts, "qkv_send")
+    sum3 = lax.psum_scatter(gate(sum3), "blk", scatter_dimension=0, tiled=True)
+    (first_qkv,) = outer(sc_send, qkv_groups, block_rows, 0, qkv_parts, "qkv_send", deps=(all2,))
     got_qkv = swap(first_qkv, "dp", 2)
-    sum3 = lax.psum_scatter(gate(sum3), "blk", scatter_dimension=0, tiled=True)
+    sum_out = lax.psum_scatter(
+        gate(both_out), "dp", scatter_dimension=0, axis_index_groups=y_groups, tiled=True
+    )
+    sum_out = lax.psum_scatter(sum_out, "blk", scatter_dimension=0, tiled=True)
     d_send = lax.dynamic_index_in_dim(d_part, 1 - h, 0, keepdims=False)
     d_send, row_sum, gain_one_sum, CHAIN[0] = lax.optimization_barrier(
         (d_send, row_sum, gain_one_sum, CHAIN[0])
@@ -1145,7 +1150,7 @@
     d_other = swap(d_send, "head", 1)
     row_total = row_sum + swap(row_sum, "head", 1)
     (keep_qkv,) = outer(
-        sc_keep, qkv_groups, block_rows, 0, qkv_parts, "qkv_keep", got_qkv, deps=(all2, branch_oth)
+        sc_keep, qkv_groups, block_rows, 0, qkv_parts, "qkv_keep", got_qkv, deps=(branch_oth,)
     )
     per_head = 1.0 / heads
     tail = jnp.stack(
@@ -1174,11 +1179,11 @@
     extra = jnp.concatenate(
         [coarse, fine, jnp.zeros((block_rows, PAIR - 12), BF16)], axis=1
     )
-    all_qkv = over_blk(jnp.concatenate([keep_qkv, sum_out, extra], axis=1))
+    all_qkv = over_blk(jnp.concatenate([keep_qkv, extra], axis=1))
     grad_down, grad_gate, grad_up = finish([(all0.reshape(-1, all0.shape[2]), nblk), (all1, nblk), (all2, nblk), (sum3, 1)])
     qw, kvw = w_query.shape[1], w_key.shape[1]
-    sum_query, sum_key, sum_value, sum_out, small = finish_rows(
-        all_qkv.reshape(nblk, -1, all_qkv.shape[1]), (qw, kvw, kvw, o_own.shape[1])
+    sum_query, sum_key, sum_value, small = finish_rows(
+        all_qkv.reshape(nblk, -1, all_qkv.shape[1]), (qw, kvw, kvw)
     )
 
     inv_one = lax.rsqrt(ssx[:, :1] * (1.0 / d) + EPS)
@@ -1199,7 +1204,7 @@
         sum_query,
         sum_key,
         sum_value,
-        sum_out,
+        sum_out.astype(F32),
         grad_mlp_gain,
         grad_gate,
         grad_up,

time: 560 us -> 591 us (1.055)
  waiting for transfers between devices: 196 us -> 230 us
    reduce_scatter x0 -> x2, waiting for transfers between devices: none -> 19.8 us  [the longest x1 19.8 us: body(): sum_out = lax.psum_scatter(sum_out, 'blk', scatter_dimension=0, tiled=True)]
    reduce_scatter x1, waiting for transfers between devices: 1.59 us -> 13.9 us  [body(): sum3 = lax.psum_scatter(gate(sum3), 'blk', scatter_dimension=0, tiled=True)]
    unnamed x72 -> x78, local copies, waits for them, and re-layouts: 15.4 us -> 16.2 us
  transfers between devices with their start and end apart: 36 -> 37, of which waited for: 14 -> 16; matrix products, arithmetic and copies ran while one was open for 6% -> 6% of each run, Pallas kernels for 44% -> 41%
where the time goes in v6:
time: 591 us; the launch traced here: 582 us
  Pallas kernels  250 us (42%)
  waiting for transfers between devices  230 us (39%)
  starting transfers between devices  36.3 us (6%)
  local copies, waits for them, and re-layouts  28.7 us (5%)
  other arithmetic  19.1 us (3%)
  between operations  17.8 us (3%)
    pallas_call x29, Pallas kernels, launch(): pl.pallas_call(wrapped, grid_spec=pltpu.PrefetchScalarGridSpec(num_scalar...  250 us
    ppermute x20, waiting for transfers between devices, swap(): return lax.ppermute(x, axis, [(i, i ^ bit) for i in range(n)])  119 us
    ppermute x3, waiting for transfers between devices, body(): lax.ppermute(part, 'blk', [(i, i - s) for i in range(s, nblk)])  42.5 us
    all_to_all x3, waiting for transfers between devices, over_blk(): return lax.all_to_all(x, 'blk', split_axis=0, concat_axis=0, tiled=True)  24.1 us
    reduce_scatter x1, waiting for transfers between devices, body(): sum_out = lax.psum_scatter(sum_out, 'blk', scatter_dimension=0, tiled=True)  19.8 us
    unnamed x78, local copies, waits for them, and re-layouts  16.2 us
    reduce_scatter x1, waiting for transfers between devices, body(): sum3 = lax.psum_scatter(gate(sum3), 'blk', scatter_dimension=0, tiled=True)  13.9 us
    all_to_all x3, starting transfers between devices, over_blk(): return lax.all_to_all(x, 'blk', split_axis=0, concat_axis=0, tiled=True)  13.7 us
  transfers between devices with their start and end apart: 37, of which 16 were waited for; matrix products, arithmetic and copies ran while one was open for 6% of the time, Pallas kernels for 41%

profile of v6, /device:TPU:0, one launch (start us, length us, event | category | flops | bytes accessed | tf_op | source)
XLA Modules:
  0.0 581.9 jit_solution(11951996334073306121)
XLA Ops:
  15.7 18.0 %collective-permute-done.refs_2_ = bf16[512,1024]{1,0:T(8,128)(2,1)} collective-permute-done((bf16[512,1024]{1,0:T(8,128)(2,1)}, bf16[512,1024]{1,0:T(8,128)(2,1)}, u32[]{:S(2)}, u32[]{:S(2)}) %collective-permute-start) | collective-permute-done | bytes 1048608 | tf_op jit(solution)/shard_map/ppermute | solution.py:93
  48.8 7.6 %attend0.1 = (f32[1024,512]{1,0:T(8,128)S(1)}, f32[8,8,512]{2,1,0:T(8,128)S(1)}, f32[8,128]{1,0:T(8,128)}) custom-call(s32[1]{0:T(128)} %bitcast.refs_0_, bf16[512,1024]{1,0:T(8,128)(2,1)} %get-tuple-element.136.refs_1_, bf16[512,256]{1,0:T(8,128)(2,1)} %get-tuple-element.137.refs_2_.refs_5_, s32[1,1,512]{2,1,0:T(1,128)} %bitcast.88, ...), custom_call_target="tpu_custom_call" | custom-call | flops 2576980480 | bytes 4194304 | tf_op jit(solution)/shard_map/attend0/pallas_call | solution.py:61
  75.9 9.9 %collective-permute-done.6 = bf16[512,1024]{1,0:T(8,128)(2,1)} collective-permute-done((bf16[512,1024]{1,0:T(8,128)(2,1)S(1)}, bf16[512,1024]{1,0:T(8,128)(2,1)}, u32[]{:S(2)}, u32[]{:S(2)}) %collective-permute-start.6) | collective-permute-done | bytes 1048608 | tf_op jit(solution)/shard_map/ppermute | solution.py:93
  90.1 15.6 %collective-permute-done.5.refs_1_ = bf16[512,1024]{1,0:T(8,128)(2,1)} collective-permute-done((bf16[512,1024]{1,0:T(8,128)(2,1)}, bf16[512,1024]{1,0:T(8,128)(2,1)}, u32[]{:S(2)}, u32[]{:S(2)}) %collective-permute-start.5) | collective-permute-done | bytes 1048608 | tf_op jit(solution)/shard_map/ppermute | solution.py:93
  105.7 11.3 %merge.1 = (f32[4,512,512]{2,1,0:T(8,128)}, bf16[512,2048]{1,0:T(8,128)(2,1)}, bf16[2048,512]{1,0:T(8,128)(2,1)}, f32[512,128]{1,0:T(8,128)}, f32[512,128]{1,0:T(8,128)}, /*index=5*/f32[8,128]{1,0:T(8,128)}) custom-call(f32[4,512,512]{2,1,0:T(8,128)} %get-tuple-element.161.refs_0_, bf16[512,1024]{1,0:T(8,128)(2,1)} %collective-permute-done.5.refs_1_, ...), custom_call_target="tpu_custom_call" | custom-call | flops 2576980480 | bytes 8388608 | tf_op jit(solution)/shard_map/merge/pallas_call | solution.py:61
  117.0 8.2 %units0.1 = (bf16[3,512,512]{2,1,0:T(8,128)(2,1)}, f32[8,128]{1,0:T(8,128)}) custom-call(bf16[512,2048]{1,0:T(8,128)(2,1)} %get-tuple-element.169.refs_0_, bf16[512,2048]{1,0:T(8,128)(2,1)} %copy-done, bf16[2048,2816]{1,0:T(8,128)(2,1)} %refs_9_.1, bf16[2048,2816]{1,0:T(8,128)(2,1)} %refs_10_.1, bf16[2048,2816]{1,0:T(8,128)(2,1)} %refs_11_.1, ...), custom_call_target="tpu_custom_call" | custom-call | flops 2147483648 | bytes 2516582 | tf_op jit(solution)/shard_map/units0/pallas_call | solution.py:61
  130.4 8.7 %mlp0.1 = (bf16[1024,1536]{1,0:T(8,128)(2,1)}, f32[8,128]{1,0:T(8,128)}) custom-call(s32[2]{0:T(128)S(1)} %pad_add_fusion.refs_0_, bf16[2048,512]{1,0:T(8,128)(2,1)} %get-tuple-element.172.refs_1_.refs_2_, bf16[2048,512]{1,0:T(8,128)(2,1)} %get-tuple-element.172.refs_1_.refs_2_, bf16[2048,512]{1,0:T(8,128)(2,1)} %collective-permute-done.7.refs_3_.refs_4_, ...), custom_call_target="tpu_custom_call" | custom-call | flops 2576980480 | bytes 2516582 | tf_op jit(solution)/shard_map/mlp0/pallas_call | solution.py:61
  139.2 10.4 %units2.1 = (bf16[3,512,768]{2,1,0:T(8,128)(2,1)}, f32[8,128]{1,0:T(8,128)}) custom-call(bf16[512,2048]{1,0:T(8,128)(2,1)} %get-tuple-element.169.refs_0_, bf16[512,2048]{1,0:T(8,128)(2,1)} %copy-done, bf16[2048,2816]{1,0:T(8,128)(2,1)} %refs_9_.1, bf16[2048,2816]{1,0:T(8,128)(2,1)} %refs_10_.1, bf16[2048,2816]{1,0:T(8,128)(2,1)} %refs_11_.1, ...), custom_call_target="tpu_custom_call" | custom-call | flops 3221225472 | bytes 3774873 | tf_op jit(solution)/shard_map/units2/pallas_call | solution.py:61
  149.9 17.0 %units5.1 = (bf16[3,512,1536]{2,1,0:T(8,128)(2,1)}, f32[8,128]{1,0:T(8,128)}) custom-call(bf16[512,2048]{1,0:T(8,128)(2,1)} %get-tuple-element.169.refs_0_, bf16[512,2048]{1,0:T(8,128)(2,1)} %copy-done, bf16[2048,2816]{1,0:T(8,128)(2,1)} %refs_9_.1, bf16[2048,2816]{1,0:T(8,128)(2,1)} %refs_10_.1, bf16[2048,2816]{1,0:T(8,128)(2,1)} %refs_11_.1, ...), custom_call_target="tpu_custom_call" | custom-call | flops 6442450944 | bytes 7549747 | tf_op jit(solution)/shard_map/units5/pallas_call | solution.py:61
  168.5 10.3 %mlp1.1 = (bf16[1024,2304]{1,0:T(8,128)(2,1)}, f32[8,128]{1,0:T(8,128)}) custom-call(s32[2]{0:T(128)S(1)} %pad_add_fusion.refs_0_, bf16[2048,512]{1,0:T(8,128)(2,1)} %get-tuple-element.172.refs_1_.refs_2_, bf16[2048,512]{1,0:T(8,128)(2,1)} %get-tuple-element.172.refs_1_.refs_2_, bf16[2048,512]{1,0:T(8,128)(2,1)} %collective-permute-done.7.refs_3_.refs_4_, ...), custom_call_target="tpu_custom_call" | custom-call | flops 3865470464 | bytes 3774873 | tf_op jit(solution)/shard_map/mlp1/pallas_call | solution.py:61
  179.2 8.4 %reduce-scatter.8.cloned.1.call-done.refs_12_ = bf16[512,1536]{1,0:T(8,128)(2,1)} async-done(((bf16[1024,1536]{1,0:T(8,128)(2,1)}), bf16[512,1536]{1,0:T(8,128)(2,1)}) %reduce-scatter.8.cloned.1.call-update) | async-done | bytes 1572880 | tf_op jit(solution)/shard_map/reduce_scatter | solution.py:1058
  187.5 59.4 %exchange.1 = (f32[512,2048]{1,0:T(8,128)}, bf16[2,512,1024]{2,1,0:T(8,128)(2,1)}, bf16[4,128,1536]{2,1,0:T(8,128)(2,1)}, f32[8,128]{1,0:T(8,128)}) custom-call(bf16[3,512,512]{2,1,0:T(8,128)(2,1)} %get-tuple-element.171.refs_5_.refs_11_.refs_13_.refs_0_.refs_3_.refs_6_, ...), custom_call_target="tpu_custom_call" | custom-call | flops 7086695936 | bytes 13841203 | tf_op jit(solution)/shard_map/exchange/pallas_call | solution.py:61
  246.9 16.6 %mlp2.1 = (bf16[1024,2304]{1,0:T(8,128)(2,1)}, bf16[1024,2304]{1,0:T(8,128)(2,1)}, f32[8,128]{1,0:T(8,128)}) custom-call(s32[2]{0:T(128)S(1)} %pad_add_fusion.refs_0_, bf16[2048,512]{1,0:T(8,128)(2,1)} %get-tuple-element.172.refs_1_.refs_2_, bf16[2048,512]{1,0:T(8,128)(2,1)} %get-tuple-element.172.refs_1_.refs_2_, ...), custom_call_target="tpu_custom_call" | custom-call | flops 7730940928 | bytes 7549747 | tf_op jit(solution)/shard_map/mlp2/pallas_call | solution.py:61
  268.2 10.3 %stream.1 = (f32[512,2048]{1,0:T(8,128)}, bf16[2048,512]{1,0:T(8,128)(2,1)}, bf16[512,1024]{1,0:T(8,128)(2,1)}, f32[1,2048]{1,0:T(1,128)}, f32[8,128]{1,0:T(8,128)}) custom-call(f32[512,2048]{1,0:T(8,128)} %get-tuple-element.182.refs_0_, f32[4,512,512]{2,1,0:T(8,128)} %get-tuple-element.228.refs_1_, f32[512,128]{1,0:T(8,128)} %get-tuple-element.183.refs_2_, ...), custom_call_target="tpu_custom_call" | custom-call | flops 858993472 | bytes 10066329 | tf_op jit(solution)/shard_map/stream/pallas_call | solution.py:61
  296.7 18.7 %collective-permute-done.15.refs_10_.refs_0_ = bf16[512,256]{1,0:T(8,128)(2,1)S(1)} collective-permute-done((bf16[512,256]{1,0:T(8,128)(2,1)}, bf16[512,256]{1,0:T(8,128)(2,1)S(1)}, u32[]{:S(2)}, u32[]{:S(2)}) %collective-permute-start.15) | collective-permute-done | bytes 262176 | tf_op jit(solution)/shard_map/ppermute | solution.py:1110
  315.4 23.8 %collective-permute-done.16.refs_11_.refs_1_ = bf16[512,256]{1,0:T(8,128)(2,1)S(1)} collective-permute-done((bf16[512,256]{1,0:T(8,128)(2,1)}, bf16[512,256]{1,0:T(8,128)(2,1)S(1)}, u32[]{:S(2)}, u32[]{:S(2)}) %collective-permute-start.16) | collective-permute-done | bytes 262176 | tf_op jit(solution)/shard_map/ppermute | solution.py:1110
  353.9 16.1 %attend_back0.1 = (bf16[512,1024]{1,0:T(8,128)(2,1)}, bf16[512,256]{1,0:T(8,128)(2,1)}, f32[8,128]{1,0:T(8,128)}) custom-call(s32[1]{0:T(128)} %bitcast.refs_0_, bf16[512,1024]{1,0:T(8,128)(2,1)} %get-tuple-element.136.refs_1_, bf16[512,1024]{1,0:T(8,128)(2,1)} %get-tuple-element.188.refs_2_, f32[8,8,512]{2,1,0:T(8,128)} %copy-done.11, ...), custom_call_target="tpu_custom_call" | custom-call | flops 5798205952 | bytes 4194304 | tf_op jit(solution)/shard_map/attend_back0/pallas_call | solution.py:61
  374.2 10.4 %entry.1 = (bf16[2,512,1024]{2,1,0:T(8,128)(2,1)}, f32[1,2048]{1,0:T(1,128)}, f32[512,128]{1,0:T(8,128)}, f32[8,128]{1,0:T(8,128)}) custom-call(bf16[512,1024]{1,0:T(8,128)(2,1)} %get-tuple-element.211.refs_0_, bf16[512,256]{1,0:T(8,128)(2,1)} %get-tuple-element.214.refs_1_, bf16[2048,1024]{1,0:T(8,128)(2,1)} %refs_2_.7, bf16[2048,128]{1,0:T(8,128)(2,1)} %refs_3_.7, ...), custom_call_target="tpu_custom_call" | custom-call | flops 1073741824 | bytes 8388608 | tf_op jit(solution)/shard_map/entry/pallas_call | solution.py:61
  384.6 22.5 %all-to-all-done.1.refs_2_ = bf16[4,128,2304]{2,1,0:T(8,128)(2,1)S(1)} async-done(((bf16[4,128,2304]{2,1,0:T(8,128)(2,1)}), bf16[4,128,2304]{2,1,0:T(8,128)(2,1)S(1)}, u32[]{:S(2)}, u32[]{:S(2)}) %all-to-all-start.1) | async-done | bytes 2359328 | tf_op jit(solution)/shard_map/all_to_all | solution.py:1065
  422.9 16.9 %collective-permute-done.19.refs_7_ = bf16[512,1024]{1,0:T(8,128)(2,1)S(1)} collective-permute-done((bf16[512,1024]{1,0:T(8,128)(2,1)}, bf16[512,1024]{1,0:T(8,128)(2,1)S(1)}, u32[]{:S(2)}, u32[]{:S(2)}) %collective-permute-start.19) | collective-permute-done | bytes 1048608 | tf_op jit(solution)/shard_map/ppermute | solution.py:93
  448.5 23.0 %collective-permute-done.25 = f32[33,128]{1,0:T(8,128)S(1)} collective-permute-done((f32[33,128]{1,0:T(8,128)S(1)}, f32[33,128]{1,0:T(8,128)S(1)}, u32[]{:S(2)}, u32[]{:S(2)}) %collective-permute-start.25) | collective-permute-done | bytes 16928 | tf_op jit(solution)/shard_map/ppermute | solution.py:93
  489.9 27.6 %collective-permute-done.21 = f32[512,128]{1,0:T(8,128)S(1)} collective-permute-done((f32[512,128]{1,0:T(8,128)}, f32[512,128]{1,0:T(8,128)S(1)}, u32[]{:S(2)}, u32[]{:S(2)}) %collective-permute-start.21) | collective-permute-done | bytes 262176 | tf_op jit(solution)/shard_map/ppermute | solution.py:93
  525.5 13.9 %reduce-scatter.16.cloned.1.call-done = bf16[128,2304]{1,0:T(8,128)(2,1)} async-done(((bf16[512,2304]{1,0:T(8,128)(2,1)}), bf16[128,2304]{1,0:T(8,128)(2,1)}) %reduce-scatter.16.cloned.1.call-update) | async-done | bytes 589840 | tf_op jit(solution)/shard_map/reduce_scatter | solution.py:1127
  553.0 19.8 %reduce-scatter.20.cloned.1.call-done = bf16[128,1024]{1,0:T(8,128)(2,1)} async-done(((bf16[512,1024]{1,0:T(8,128)(2,1)}), bf16[128,1024]{1,0:T(8,128)(2,1)}) %reduce-scatter.20.cloned.1.call-update) | async-done | bytes 262160 | tf_op jit(solution)/shard_map/reduce_scatter | solution.py:1133
  (210 shorter events, 159.7 us)
Async XLA Ops:
  7.2 98.5 %all-gather.2.cloned.1.call-start = ((), (), s32[]{:S(2)}) async-start(), calls=%async_computation.10 | async-start | bytes 5242880 | tf_op jit(solution)/shard_map/all_gather | solution.py:1032
  7.2 26.5 %collective-permute-start = (bf16[512,1024]{1,0:T(8,128)(2,1)}, bf16[512,1024]{1,0:T(8,128)(2,1)}, u32[]{:S(2)}, u32[]{:S(2)}) collective-permute-start(bf16[512,1024]{1,0:T(8,128)(2,1)} %bitcast.63), channel_id=1, source_target_pairs={{0,1},{1,0},{2,3},{3,2},{4,5},{5,4},{6,7},{7,6},{8,9},{9,8},{10,11... | collective-permute-start | bytes 3145736 | tf_op jit(solution)/shard_map/ppermute | solution.py:93
  58.8 128.7 %reduce-scatter.8.cloned.1.call-start = ((), (), s32[]{:S(2)}) async-start(), calls=%async_computation.11 | async-start | bytes 4718592 | tf_op jit(solution)/shard_map/reduce_scatter | solution.py:1058
  59.5 26.3 %collective-permute-start.6 = (bf16[512,1024]{1,0:T(8,128)(2,1)S(1)}, bf16[512,1024]{1,0:T(8,128)(2,1)}, u32[]{:S(2)}, u32[]{:S(2)}) collective-permute-start(bf16[512,1024]{1,0:T(8,128)(2,1)S(1)} %bitcast.74), channel_id=1, source_target_pairs={{0,1},{1,0},{2,3},{3,2},{4,5},{5,4},{6,7},{7,6},{8,9},{9,8},{10,11... | collective-permute-start | bytes 3145736 | tf_op jit(solution)/shard_map/ppermute | solution.py:93
  67.9 37.8 %collective-permute-start.5 = (bf16[512,1024]{1,0:T(8,128)(2,1)}, bf16[512,1024]{1,0:T(8,128)(2,1)}, u32[]{:S(2)}, u32[]{:S(2)}) collective-permute-start(bf16[512,1024]{1,0:T(8,128)(2,1)} %get-tuple-element.159.refs_0_.refs_6_), channel_id=1, source_target_pairs={{0,1},{1,0},{2,3},{3,2},{4,5},{5,4},{6,7},{7,6},{8,9},{9,8},{10,11... | collective-permute-start | bytes 3145736 | tf_op jit(solution)/shard_map/ppermute | solution.py:93
  90.1 35.7 %collective-permute-start.7 = (bf16[2048,512]{1,0:T(8,128)(2,1)}, bf16[2048,512]{1,0:T(8,128)(2,1)}, u32[]{:S(2)}, u32[]{:S(2)}) collective-permute-start(bf16[2048,512]{1,0:T(8,128)(2,1)} %get-tuple-element.172.refs_1_.refs_2_), channel_id=1, source_target_pairs={{0,8},{8,0},{16,24},{24,16},{1,9},{9,1},{17,25},{25,17},{2,10},{10... | collective-permute-start | bytes 6291464 | tf_op jit(solution)/shard_map/ppermute | solution.py:93
  139.1 125.1 %reduce-scatter.10.cloned.1.call-start = ((), (), s32[]{:S(2)}) async-start(), calls=%async_computation.12 | async-start | bytes 7077888 | tf_op jit(solution)/shard_map/reduce_scatter | solution.py:1058
  178.8 169.2 %reduce-scatter.12.cloned.1.call-start = ((), (), s32[]{:S(2)}) async-start(), calls=%async_computation.13 | async-start | bytes 7077888 | tf_op jit(solution)/shard_map/reduce_scatter | solution.py:1058
  178.9 68.1 %collective-permute-start.11 = (bf16[3,512,1536]{2,1,0:T(8,128)(2,1)}, bf16[3,512,1536]{2,1,0:T(8,128)(2,1)}, u32[]{:S(2)}, u32[]{:S(2)}) collective-permute-start(bf16[3,512,1536]{2,1,0:T(8,128)(2,1)} %get-tuple-element.178.refs_2_.refs_5_.refs_8_.refs_11_.refs_13_), channel_id=1, source_target_pairs={{0,8},{8,0},{16,24},{24,16},{1,9},{9,1},{17,25},{25,17},{2,10},{10... | collective-permute-start | bytes 14155784 | tf_op jit(solution)/shard_map/ppermute | solution.py:93
  263.6 121.0 %reduce-scatter.14.cloned.1.call-start = ((), (), s32[]{:S(2)}) async-start(), calls=%async_computation.14 | async-start | bytes 7077888 | tf_op jit(solution)/shard_map/reduce_scatter | solution.py:1058
  264.2 75.7 %all-to-all-start = ((bf16[4,128,2304]{2,1,0:T(8,128)(2,1)}), bf16[4,128,2304]{2,1,0:T(8,128)(2,1)S(1)}, u32[]{:S(2)}, u32[]{:S(2)}) async-start(bf16[4,128,2304]{2,1,0:T(8,128)(2,1)} %bitcast.73), calls=%async_computation.3 | async-start | bytes 4718592 | tf_op jit(solution)/shard_map/all_to_all | solution.py:1065
  278.5 60.7 %collective-permute-start.12 = (bf16[2048,512]{1,0:T(8,128)(2,1)}, bf16[2048,512]{1,0:T(8,128)(2,1)}, u32[]{:S(2)}, u32[]{:S(2)}) collective-permute-start(bf16[2048,512]{1,0:T(8,128)(2,1)} %get-tuple-element.202.refs_1_.refs_2_), channel_id=1, source_target_pairs={{0,8},{8,0},{16,24},{24,16},{1,9},{9,1},{17,25},{25,17},{2,10},{10... | collective-permute-start | bytes 6291464 | tf_op jit(solution)/shard_map/ppermute | solution.py:93
  278.5 61.4 %collective-permute-start.14 = (bf16[2048,512]{1,0:T(8,128)(2,1)}, bf16[2048,512]{1,0:T(8,128)(2,1)}, u32[]{:S(2)}, u32[]{:S(2)}) collective-permute-start(bf16[2048,512]{1,0:T(8,128)(2,1)} %get-tuple-element.205.refs_1_), channel_id=1, source_target_pairs={{0,8},{8,0},{16,24},{24,16},{1,9},{9,1},{17,25},{25,17},{2,10},{10... | collective-permute-start | bytes 6291464 | tf_op jit(solution)/shard_map/ppermute | solution.py:93
  285.1 30.3 %collective-permute-start.15 = (bf16[512,256]{1,0:T(8,128)(2,1)}, bf16[512,256]{1,0:T(8,128)(2,1)S(1)}, u32[]{:S(2)}, u32[]{:S(2)}) collective-permute-start(bf16[512,256]{1,0:T(8,128)(2,1)} %get-tuple-element.206), channel_id=1, source_target_pairs={{6,0},{7,1},{14,8},{15,9},{22,16},{23,17},{30,24},{31,25}} | collective-permute-start | bytes 786440 | tf_op jit(solution)/shard_map/ppermute | solution.py:1110
  290.3 48.9 %collective-permute-start.16 = (bf16[512,256]{1,0:T(8,128)(2,1)}, bf16[512,256]{1,0:T(8,128)(2,1)S(1)}, u32[]{:S(2)}, u32[]{:S(2)}) collective-permute-start(bf16[512,256]{1,0:T(8,128)(2,1)} %get-tuple-element.207), channel_id=1, source_target_pairs={{4,0},{6,2},{5,1},{7,3},{12,8},{14,10},{13,9},{15,11},{20,16},{22,... | collective-permute-start | bytes 786440 | tf_op jit(solution)/shard_map/ppermute | solution.py:1110
  295.4 43.8 %collective-permute-start.17 = (bf16[512,256]{1,0:T(8,128)(2,1)}, bf16[512,256]{1,0:T(8,128)(2,1)S(1)}, u32[]{:S(2)}, u32[]{:S(2)}) collective-permute-start(bf16[512,256]{1,0:T(8,128)(2,1)} %get-tuple-element.208), channel_id=1, source_target_pairs={{2,0},{4,2},{6,4},{3,1},{5,3},{7,5},{10,8},{12,10},{14,12},{11,9},... | collective-permute-start | bytes 786440 | tf_op jit(solution)/shard_map/ppermute | solution.py:1110
  348.0 59.1 %all-to-all-start.1 = ((bf16[4,128,2304]{2,1,0:T(8,128)(2,1)}), bf16[4,128,2304]{2,1,0:T(8,128)(2,1)S(1)}, u32[]{:S(2)}, u32[]{:S(2)}) async-start(bf16[4,128,2304]{2,1,0:T(8,128)(2,1)} %bitcast.72), calls=%async_computation.5 | async-start | bytes 4718592 | tf_op jit(solution)/shard_map/all_to_all | solution.py:1065
  353.9 133.5 %reduce-scatter.18.cloned.1.call-start = ((), (), s32[]{:S(2)}) async-start(), calls=%async_computation.16 | async-start | bytes 3145728 | tf_op jit(solution)/shard_map/reduce_scatter | solution.py:1130
  414.3 125.1 %reduce-scatter.16.cloned.1.call-start = ((), (), s32[]{:S(2)}) async-start(), calls=%async_computation.15 | async-start | bytes 2949120 | tf_op jit(solution)/shard_map/reduce_scatter | solution.py:1127
  419.6 52.6 %collective-permute-start.22 = (bf16[512,1280]{1,0:T(8,128)(2,1)}, bf16[512,1280]{1,0:T(8,128)(2,1)S(1)}, u32[]{:S(2)}, u32[]{:S(2)}) collective-permute-start(bf16[512,1280]{1,0:T(8,128)(2,1)} %get-tuple-element.236), channel_id=1, source_target_pairs={{0,16},{8,24},{16,0},{24,8},{1,17},{9,25},{17,1},{25,9},{2,18},{10... | collective-permute-start | bytes 3932168 | tf_op jit(solution)/shard_map/ppermute | solution.py:93
  483.2 63.1 %all-to-all-start.2 = ((bf16[4,128,1408]{2,1,0:T(8,128)(2,1)}), bf16[4,128,1408]{2,1,0:T(8,128)(2,1)S(1)}, u32[]{:S(2)}, u32[]{:S(2)}) async-start(bf16[4,128,1408]{2,1,0:T(8,128)(2,1)} %bitcast.70), calls=%async_computation.6 | async-start | bytes 2883584 | tf_op jit(solution)/shard_map/all_to_all | solution.py:1065
  487.1 85.7 %reduce-scatter.20.cloned.1.call-start = ((), (), s32[]{:S(2)}) async-start(), calls=%async_computation.17 | async-start | bytes 1310720 | tf_op jit(solution)/shard_map/reduce_scatter | solution.py:1133
  487.8 30.8 %collective-permute-start.20 = (bf16[512,1024]{1,0:T(8,128)(2,1)S(1)}, bf16[512,1024]{1,0:T(8,128)(2,1)S(1)}, u32[]{:S(2)}, u32[]{:S(2)}) collective-permute-start(bf16[512,1024]{1,0:T(8,128)(2,1)S(1)} %copy-done.24), channel_id=1, source_target_pairs={{0,1},{1,0},{2,3},{3,2},{4,5},{5,4},{6,7},{7,6},{8,9},{9,8},{10,11... | collective-permute-start | bytes 3145736 | tf_op jit(solution)/shard_map/ppermute | solution.py:93
  489.6 28.0 %collective-permute-start.21 = (f32[512,128]{1,0:T(8,128)}, f32[512,128]{1,0:T(8,128)S(1)}, u32[]{:S(2)}, u32[]{:S(2)}) collective-permute-start(f32[512,128]{1,0:T(8,128)} %get-tuple-element.235), channel_id=1, source_target_pairs={{0,1},{1,0},{2,3},{3,2},{4,5},{5,4},{6,7},{7,6},{8,9},{9,8},{10,11... | collective-permute-start | bytes 786440 | tf_op jit(solution)/shard_map/ppermute | solution.py:93
  (51 other events, 544.2 us)
Sparse Core Ops, SparseCore 0:
  58.9 35.5 all-gather.1
  139.2 48.2 reduce-scatter.7
  190.0 59.9 reduce-scatter.9
  263.7 57.1 reduce-scatter.11
  323.2 59.9 reduce-scatter.13
  414.4 51.4 reduce-scatter.17
  468.4 71.0 reduce-scatter.15
  541.8 30.8 reduce-scatter.19
